TPU v7x, 32 devices: a whole 2x2x4 slice. The times are simulated.
32 devices in a mesh: section: 2 (over x), dp: 4 (over y, core), tensor: 4 (over z).
Axes of the slice: x: 2, y: 2, z: 4, core: 2. Of those that a mesh axis runs over, the one named last changes fastest.
Arguments:
- incoming: bfloat16 [2, 3, 256, 8192], P('section', None, ('dp', 'tensor')), may hold values from -6 to 6
- hidden: bfloat16 [2, 3, 256, 8192], P('section', None, ('dp', 'tensor')), may hold values from -6 to 6
- expert_out: bfloat16 [2, 3, 256, 2, 8192], P('section', None, ('dp', 'tensor')), may hold values from -0.59765625 to 0.59765625
- routes: int32 [2, 3, 256, 2], P('section', None, ('dp', 'tensor')), may hold values from 0 to 3, all different within a row; in each aligned block of 16 rows (0 to 15, 16 to 31, ..., all dimensions but the last counted through in order) at most 16 rows name the same one
- expert_back: bfloat16 [2, 3, 1024, 8192], P('section', None, ('dp', 'tensor')), may hold values from -0.59765625 to 0.59765625
- scan_out: bfloat16 [2, 3, 256, 8192], P('section', None, 'dp', 'tensor'), may hold values from -6 to 6
- gate_in: bfloat16 [2, 3, 256, 8192], P('section', None, 'dp', 'tensor'), may hold values from -9 to 9
- w_out: bfloat16 [2, 8192, 8192], P('section', 'tensor'), may hold values from -0.0625 to 0.0625
- w_router: bfloat16 [2, 8192, 4], P('section', 'dp'), may hold values from -0.0625 to 0.0625
- norm_gain: bfloat16 [2, 8192], P('section', 'dp'), may hold values from 0.5 to 1.5
Outputs:
- passed: bfloat16 [2, 3, 256, 8192], P('section', None, ('dp', 'tensor'))
- scan_grad: bfloat16 [2, 3, 256, 8192], P('section', None, 'dp', 'tensor')
- gate_grad: bfloat16 [2, 3, 256, 8192], P('section', None, 'dp', 'tensor')
- expert_grad: bfloat16 [2, 3, 1024, 8192], P('section', None, ('dp', 'tensor'))
- w_out_grad: float32 [2, 8192, 8192], P('section', 'tensor', 'dp')
- router_grad: float32 [2, 8192, 4], P('section', 'dp')
- gain_grad: float32 [2, 8192], P('section', 'dp')
Inputs may be any that keep to these rules, and one draw needn't show every extreme that they name: `routes`: each row names 2 different experts. In each aligned block of 16 rows (the rows of one device) no expert is named by more than 16 rows, a bound that some block reaches.
All inputs are finite; a program needn't handle non-finite values.
Results may differ from a plain program's by a relative error of at most 0.025.
Values may be sent and summed in bfloat16 or wider, within the bound.
No kernel may reach another device: no remote copies, remote signals or barrier semaphores. Data moves between devices by JAX's collectives and lax.ppermute only.
A program may use at most 320 MiB of HBM per device.

v0:
```python
import jax
import jax.numpy as jnp
from jax import lax
from jax.sharding import PartitionSpec as P


def passed_along(shard, axis, by):
    length = lax.axis_size(axis)
    pairs = [(i, i + by) for i in range(length) if 0 <= i + by < length]
    return lax.ppermute(shard, axis, pairs)


def slot_rows(expert_ids, experts, capacity):
    flat_ids = expert_ids.reshape(-1)
    onehot = (flat_ids[:, None] == jnp.arange(experts, dtype=jnp.int32)[None, :]).astype(jnp.int32)
    before = jnp.cumsum(onehot, axis=0, dtype=jnp.int32) - onehot
    slot_index = jnp.sum(before * onehot, axis=1, dtype=jnp.int32)
    return flat_ids * capacity + slot_index


def on_device(
    incoming, hidden, expert_out, routes, expert_back, scan_out, gate_in, w_out, w_router, norm_gain
):
    micro_count = incoming.shape[1]
    tok_rows = incoming.shape[2]
    model_width = incoming.shape[3]
    top_count = routes.shape[3]
    experts = w_router.shape[2]
    tensor_size = lax.axis_size("tensor")
    capacity = expert_back.shape[2] // tensor_size
    inner_width = scan_out.shape[3]
    weight_rows = w_out[0]
    section_id = lax.axis_index("section")
    router_full, gain_full = (
        lax.all_gather(w_router[0], "dp", axis=0, tiled=True),
        lax.all_gather(norm_gain[0], "dp", axis=0, tiled=True),
    )
    gain_f = gain_full.astype(jnp.float32)
    expert_range = jnp.arange(experts, dtype=jnp.int32)
    router_acc = jnp.zeros((model_width, experts), jnp.float32)
    gain_acc = jnp.zeros((model_width,), jnp.float32)
    grad_acc = jnp.zeros((inner_width, model_width), jnp.float32)
    passed_list = []
    expert_list = []
    scan_list = []
    gate_list = []
    received = incoming[0, 0]
    for micro_step in range(micro_count):
        upstream = incoming[0, micro_step]
        if micro_step > 0:
            upstream = jnp.where(section_id == 1, upstream, received)
        returned = lax.all_to_all(
            expert_back[0, micro_step], "tensor", split_axis=0, concat_axis=0, tiled=True
        )
        hidden_f = hidden[0, micro_step].astype(jnp.float32)
        inv_rms = 1.0 / jnp.sqrt(jnp.mean(hidden_f * hidden_f, axis=1, keepdims=True) + 1e-05)
        normed = (hidden_f * inv_rms * gain_f).astype(jnp.bfloat16)
        logits = jnp.dot(normed, router_full, preferred_element_type=jnp.float32)
        weights = jnp.exp(logits)
        route_probs = weights / jnp.sum(weights, axis=1, keepdims=True)
        expert_ids = routes[0, micro_step]
        chosen = (expert_ids[:, :, None] == expert_range[None, None, :]).astype(jnp.float32)
        route_prob = jnp.sum(chosen * route_probs[:, None, :], axis=2)
        score_grad = jnp.einsum(
            "td,tkd->tk", upstream, expert_out[0, micro_step], preferred_element_type=jnp.float32
        )
        prob_grad = jnp.sum(chosen * score_grad[:, :, None], axis=1)
        logit_grad = (
            route_probs * (prob_grad - jnp.sum(route_probs * prob_grad, axis=1, keepdims=True))
        ).astype(jnp.bfloat16)
        row_index = slot_rows(expert_ids, experts, capacity)
        back_rows = (
            returned[row_index].astype(jnp.float32).reshape(tok_rows, top_count, model_width)
        )
        router_back = lax.dot_general(
            logit_grad, router_full, (((1,), (1,)), ((), ())), preferred_element_type=jnp.float32
        )
        norm_grad = router_back + jnp.sum(back_rows, axis=1)
        scaled = norm_grad * gain_f
        hidden_grad = inv_rms * scaled - hidden_f * inv_rms**3 * jnp.mean(
            scaled * hidden_f, axis=1, keepdims=True
        )
        upstream_f = upstream.astype(jnp.float32)
        passed = (upstream_f + hidden_grad).astype(jnp.bfloat16)
        if micro_step + 1 < micro_count:
            received = passed_along(passed, "section", -1)
        gain_acc = gain_acc + jnp.sum(norm_grad * hidden_f * inv_rms, axis=0)
        router_acc = router_acc + lax.dot_general(
            normed, logit_grad, (((0,), (0,)), ((), ())), preferred_element_type=jnp.float32
        )
        sent = (
            (route_prob[:, :, None] * upstream_f[:, None, :])
            .astype(jnp.bfloat16)
            .reshape(tok_rows * top_count, model_width)
        )
        send_buffer = (
            jnp.zeros((experts * capacity, model_width), jnp.bfloat16).at[row_index].set(sent)
        )
        dispatched = lax.all_to_all(send_buffer, "tensor", split_axis=0, concat_axis=0, tiled=True)
        scan_f = scan_out[0, micro_step].astype(jnp.float32)
        gate_f = gate_in[0, micro_step].astype(jnp.float32)
        sigmoid_gate = jax.nn.sigmoid(gate_f)
        gated = (scan_f * gate_f * sigmoid_gate).astype(jnp.bfloat16)
        shard_rows = lax.all_gather(passed, "tensor", axis=0, tiled=True)
        weight_sum = grad_acc
        inner_rows = lax.dot_general(
            shard_rows, weight_rows, (((1,), (1,)), ((), ())), preferred_element_type=jnp.float32
        )
        weight_sum = weight_sum + lax.dot_general(
            gated, shard_rows, (((0,), (0,)), ((), ())), preferred_element_type=jnp.float32
        )
        grad_acc = weight_sum
        scan_grad = (inner_rows * gate_f * sigmoid_gate).astype(jnp.bfloat16)
        gate_grad = (
            inner_rows * scan_f * sigmoid_gate * (1.0 + gate_f * (1.0 - sigmoid_gate))
        ).astype(jnp.bfloat16)
        passed_list.append(passed)
        expert_list.append(dispatched)
        scan_list.append(scan_grad)
        gate_list.append(gate_grad)
    weight_grad = lax.psum_scatter(
        grad_acc.astype(jnp.bfloat16), "dp", scatter_dimension=1, tiled=True
    ).astype(jnp.float32)
    summed = (
        lax.psum(router_acc.astype(jnp.bfloat16), "tensor").astype(jnp.float32),
        lax.psum(gain_acc.astype(jnp.bfloat16), "tensor").astype(jnp.float32),
    )
    router_part, gain_part = (
        lax.psum_scatter(
            summed[0].astype(jnp.bfloat16), "dp", scatter_dimension=0, tiled=True
        ).astype(jnp.float32),
        lax.psum_scatter(
            summed[1].astype(jnp.bfloat16), "dp", scatter_dimension=0, tiled=True
        ).astype(jnp.float32),
    )
    return (
        jnp.stack(passed_list)[None],
        jnp.stack(scan_list)[None],
        jnp.stack(gate_list)[None],
        jnp.stack(expert_list)[None],
        weight_grad[None],
        router_part[None],
        gain_part[None],
    )


def solution(mesh):
    placed = (
        P("section", None, ("dp", "tensor"), None),
        P("section", None, ("dp", "tensor"), None),
        P("section", None, ("dp", "tensor"), None, None),
        P("section", None, ("dp", "tensor"), None),
        P("section", None, ("dp", "tensor"), None),
        P("section", None, "dp", "tensor"),
        P("section", None, "dp", "tensor"),
        P("section", "tensor", None),
        P("section", "dp", None),
        P("section", "dp"),
    )
    return jax.shard_map(
        on_device,
        mesh=mesh,
        in_specs=placed,
        out_specs=(
            P("section", None, ("dp", "tensor"), None),
            P("section", None, "dp", "tensor"),
            P("section", None, "dp", "tensor"),
            P("section", None, ("dp", "tensor"), None),
            P("section", "tensor", "dp"),
            P("section", "dp", None),
            P("section", "dp"),
        ),
        check_vma=False,
    )
```

profile of v0, /device:TPU:0, one launch (start us, length us, event | category | flops | bytes accessed | tf_op | source)
XLA Modules:
  0.0 502.0 jit_solution(7957332952202406695)
XLA Ops:
  8.0 3.7 fusion.133
  11.7 6.3 %all-to-all-start = ((bf16[4,16,8192]{2,1,0:T(8,128)(2,1)}), bf16[4,16,8192]{2,1,0:T(8,128)(2,1)S(1)}, u32[]{:S(2)}, u32[]{:S(2)}) async-start(bf16[4,16,8192]{2,1,0:T(8,128)(2,1)} %bitcast.9), calls=%async_computation | async-start | bytes 2097152 | tf_op jit(solution)/shard_map/all_to_all | solution.py:52
  20.8 1.8 bitcast_convert_fusion.1
  22.6 2.5 fusion.79
  25.1 18.6 %all-to-all-done = bf16[4,16,8192]{2,1,0:T(8,128)(2,1)S(1)} async-done(((bf16[4,16,8192]{2,1,0:T(8,128)(2,1)}), bf16[4,16,8192]{2,1,0:T(8,128)(2,1)S(1)}, u32[]{:S(2)}, u32[]{:S(2)}) %all-to-all-start) | async-done | bytes 1048608 | tf_op jit(solution)/shard_map/all_to_all | solution.py:52
  43.7 3.5 all-to-all-start.1
  47.3 5.4 %all-gather = bf16[1,8192]{1,0:T(2,128)(2,1)S(1)} all-gather(bf16[1,2048]{1,0:T(2,128)(2,1)} %param.19), channel_id=2, replica_groups=mesh['section'=2,'dp'=4,'tensor'=4] {'dp'}, dimensions={1}, use_global_device_ids=true | all-gather | bytes 20480 | tf_op jit(solution)/shard_map/all_gather | solution.py:36
  52.8 5.4 %all-gather.1 = bf16[1,8192,4]{1,2,0:T(4,128)(2,1)S(1)} all-gather(bf16[1,2048,4]{1,2,0:T(4,128)(2,1)} %param.18), channel_id=3, replica_groups=mesh['section'=2,'dp'=4,'tensor'=4] {'dp'}, dimensions={1}, use_global_device_ids=true | all-gather | bytes 81920 | tf_op jit(solution)/shard_map/all_gather | solution.py:35
  60.7 1.7 gather_fusion
  62.4 1.7 reshape.242
  64.1 2.1 reduce_sum.255
  66.2 3.0 fusion.52
  69.3 3.2 all-to-all-done.1
  72.5 3.5 all-to-all-start.2
  80.8 1.7 gather_fusion.1
  82.4 1.7 reshape.244
  84.1 2.1 reduce_sum.263
  86.3 28.8 %all-to-all-done.2 = bf16[4,16,8192]{2,1,0:T(8,128)(2,1)S(1)} async-done(((bf16[4,16,8192]{2,1,0:T(8,128)(2,1)}), bf16[4,16,8192]{2,1,0:T(8,128)(2,1)S(1)}, u32[]{:S(2)}, u32[]{:S(2)}) %all-to-all-start.2) | async-done | bytes 1048608 | tf_op jit(solution)/shard_map/all_to_all | solution.py:52
  119.0 2.5 fusion.80
  122.2 2.1 fusion.62
  126.9 6.6 %collective-permute-done.1 = bf16[16,8192]{1,0:T(8,128)(2,1)S(1)} collective-permute-done((bf16[16,8192]{1,0:T(8,128)(2,1)S(1)}, bf16[16,8192]{1,0:T(8,128)(2,1)S(1)}, u32[]{:S(2)}, u32[]{:S(2)}) %collective-permute-start.1) | collective-permute-done | bytes 262176 | tf_op jit(solution)/shard_map/ppermute | solution.py:10
  134.5 2.6 fusion.81
  141.3 1.8 copy.68
  143.5 27.1 %fusion.88 = f32[2048,8192]{1,0:T(8,128)} fusion(bf16[64,8192]{1,0:T(8,128)(2,1)} %all-gather.6.cloned.1.call-done, bf16[1,3,64,2048]{3,2,1,0:T(8,128)(2,1)} %param.15, bf16[1,3,64,2048]{3,2,1,0:T(8,128)(2,1)} %param.16), kind=kOutput, calls=%fused_computation.142 | convolution fusion | flops 2148532224 | bytes 68681728 | tf_op jit(solution)/shard_map/dot_general | solution.py:109
  170.6 24.5 %fusion.86 = f32[2048,8192]{1,0:T(8,128)} fusion(bf16[64,8192]{1,0:T(8,128)(2,1)} %all-gather.8.cloned.1.call-done, bf16[1,3,64,2048]{3,2,1,0:T(8,128)(2,1)S(1)} %copy-done.7, bf16[1,3,64,2048]{3,2,1,0:T(8,128)(2,1)S(1)} %copy-done.8), kind=kOutput, calls=%fused_computation.141 | convolution fusion | flops 2148532224 | bytes 68681728 | tf_op jit(solution)/shard_map/dot_general | solution.py:109
  195.1 53.6 %add_convert_fusion = bf16[2048,8192]{1,0:T(8,128)(2,1)} fusion(f32[2048,8192]{1,0:T(8,128)} %fusion.88, f32[2048,8192]{1,0:T(8,128)} %fusion.86, bf16[64,8192]{1,0:T(8,128)(2,1)} %all-gather.10.cloned.1.call-done, bf16[1,3,64,2048]{3,2,1,0:T(8,128)(2,1)S(1)} %copy-done.7, bf16[1,3,64,2048]{3,2,1,0:T(8,128)(2,1)S(1)} %copy-done.8), kind=kOutput, calls=%fused_computation.6 | convolution fusion | flops 2198863872 | bytes 169345024 | tf_op jit(solution)/shard_map/dot_general | solution.py:109
  248.9 1.7 mul.490
  250.6 1.7 mul.491
  252.3 3.5 scatter_custom_fusion
  255.8 4.3 all-to-all-start.3
  261.7 1.7 mul.498
  263.6 3.6 scatter_custom_fusion.1
  268.6 1.7 mul.505
  270.5 10.5 %all-reduce = bf16[8192]{0:T(1024)(128)(2,1)S(1)} all-reduce(bf16[8192]{0:T(1024)(128)(2,1)S(1)} %add_convert_fusion.1), channel_id=6, replica_groups=mesh['section'=2,'dp'=4,'tensor'=4] {'dp'}, use_global_device_ids=true, to_apply=%region_37.38.clone | all-reduce | flops 8192 | bytes 32768
  281.1 3.4 scatter_custom_fusion.2
  284.5 2.2 maximum_bitcast_fusion.1
  288.1 19.1 %all-reduce.1 = (bf16[2048,4]{0,1:T(4,128)(2,1)S(1)}, bf16[2048]{0:T(1024)(128)(2,1)S(1)}) all-reduce(bf16[2048,4]{0,1:T(4,128)(2,1)S(1)} %copy.69, bf16[2048]{0:T(1024)(128)(2,1)S(1)} %dynamic-slice.1), channel_id=1, replica_groups=mesh['section'=2,'dp'=4,'tensor'=4] {'tensor'}, use_global_device_ids=true, to_apply=%region_31.32 | all-reduce | flops 10240 | bytes 40960 | tf_op jit(solution)/shard_map/psum | solution.py:125
  308.3 16.5 %fusion.4 = f32[64,2048]{1,0:T(8,128)} fusion(bf16[64,8192]{1,0:T(8,128)(2,1)S(1)} %copy-done, bf16[1,2048,8192]{2,1,0:T(8,128)(2,1)} %param.17), kind=kOutput, calls=%fused_computation.11 | convolution fusion | flops 2147483648 | bytes 35127296 | tf_op jit(solution)/shard_map/dot_general | solution.py:106
  324.9 3.5 all-to-all-start.4
  328.4 16.6 %fusion.2 = f32[64,2048]{1,0:T(8,128)} fusion(bf16[64,8192]{1,0:T(8,128)(2,1)S(1)} %copy-done.1, bf16[1,2048,8192]{2,1,0:T(8,128)(2,1)} %param.17), kind=kOutput, calls=%fused_computation.9 | convolution fusion | flops 2147483648 | bytes 35127296 | tf_op jit(solution)/shard_map/dot_general | solution.py:106
  345.0 5.4 %all-to-all-done.4 = bf16[4,16,8192]{2,1,0:T(8,128)(2,1)S(1)} async-done(((bf16[4,16,8192]{2,1,0:T(8,128)(2,1)}), bf16[4,16,8192]{2,1,0:T(8,128)(2,1)S(1)}, u32[]{:S(2)}, u32[]{:S(2)}) %all-to-all-start.4) | async-done | bytes 1048608 | tf_op jit(solution)/shard_map/all_to_all | solution.py:99
  350.5 3.5 all-to-all-start.5
  354.0 18.2 %fusion.104 = (bf16[1,64,2048]{2,1,0:T(8,128)(2,1)S(1)}, bf16[1,64,2048]{2,1,0:T(8,128)(2,1)}, bf16[1,64,2048]{2,1,0:T(8,128)(2,1)}, bf16[1,64,2048]{2,1,0:T(8,1...) fusion(f32[64,2048]{1,0:T(8,128)} %fusion.4, bf16[1,3,64,2048]{3,2,1,0:T(8,128)(2,1)} %param.15, ...), kind=kOutput, calls=%fused_computation.160 | convolution fusion | flops 2153381888 | bytes 38797312 | tf_op jit(solution)/shard_map/dot_general | solution.py:106
  372.2 2.6 maximum_bitcast_fusion.2
  374.8 3.1 all-to-all-done.5
  378.0 3.2 maximum_bitcast_fusion
  381.2 101.6 %reduce-scatter.5.cloned.1.call-done = bf16[2048,2048]{1,0:T(8,128)(2,1)} async-done(((bf16[2048,8192]{1,0:T(8,128)(2,1)}), bf16[2048,2048]{1,0:T(8,128)(2,1)}) %reduce-scatter.5.cloned.1.call-update) | async-done | bytes 8388624 | tf_op jit(solution)/shard_map/reduce_scatter | solution.py:121
  482.8 11.7 %bitcast_convert_fusion = f32[1,2048,2048]{2,1,0:T(8,128)} fusion(bf16[2048,2048]{1,0:T(8,128)(2,1)} %reduce-scatter.5.cloned.1.call-done), kind=kLoop, calls=%fused_computation.19 | loop fusion | flops 4194304 | bytes 25165824 | tf_op jit(solution)/shard_map/broadcast_in_dim | solution.py:141
  (139 shorter events, 28.2 us)
Async XLA Ops:
  8.0 114.2 %copy-start.6 = (bf16[1,3,16,8192]{3,2,1,0:T(8,128)(2,1)S(1)}, bf16[1,3,16,8192]{3,2,1,0:T(8,128)(2,1)}, u32[]{:S(2)}) copy-start(bf16[1,3,16,8192]{3,2,1,0:T(8,128)(2,1)} %param.11) | copy-start | bytes 2359300
  11.7 32.0 %all-to-all-start = ((bf16[4,16,8192]{2,1,0:T(8,128)(2,1)}), bf16[4,16,8192]{2,1,0:T(8,128)(2,1)S(1)}, u32[]{:S(2)}, u32[]{:S(2)}) async-start(bf16[4,16,8192]{2,1,0:T(8,128)(2,1)} %bitcast.9), calls=%async_computation | async-start | bytes 2097152 | tf_op jit(solution)/shard_map/all_to_all | solution.py:52
  19.4 40.0 %copy-start.19 = (s32[32]{0:T(128)}, s32[32]{0:T(128)S(1)}, u32[]{:S(2)}) copy-start(s32[32]{0:T(128)S(1)} %fusion.127) | copy-start | bytes 388
  20.1 39.3 %copy-start.18 = (s32[32]{0:T(128)}, s32[32]{0:T(128)S(1)}, u32[]{:S(2)}) copy-start(s32[32]{0:T(128)S(1)} %fusion.128) | copy-start | bytes 388
  20.8 31.9 %copy-start.17 = (s32[32]{0:T(128)}, s32[32]{0:T(128)S(1)}, u32[]{:S(2)}) copy-start(s32[32]{0:T(128)S(1)} %fusion.129) | copy-start | bytes 388
  43.7 28.7 %all-to-all-start.1 = ((bf16[4,16,8192]{2,1,0:T(8,128)(2,1)}), bf16[4,16,8192]{2,1,0:T(8,128)(2,1)S(1)}, u32[]{:S(2)}, u32[]{:S(2)}) async-start(bf16[4,16,8192]{2,1,0:T(8,128)(2,1)} %bitcast.21), calls=%async_computation.1 | async-start | bytes 2097152 | tf_op jit(solution)/shard_map/all_to_all | solution.py:52
  59.4 58.5 %copy-start.15 = (f32[16]{0:T(128)}, f32[16]{0:T(128)S(1)}, u32[]{:S(2)}) copy-start(f32[16]{0:T(128)S(1)} %get-tuple-element.48) | copy-start | bytes 196
  60.6 77.1 %copy-start.13 = (f32[16]{0:T(128)}, f32[16]{0:T(128)S(1)}, u32[]{:S(2)}) copy-start(f32[16]{0:T(128)S(1)} %get-tuple-element.49) | copy-start | bytes 196
  60.7 8.6 %copy-start.20 = (f32[16]{0:T(128)}, f32[16]{0:T(128)S(1)}, u32[]{:S(2)}) copy-start(f32[16]{0:T(128)S(1)} %multiply_reduce_fusion.2) | copy-start | bytes 196
  72.5 42.6 %all-to-all-start.2 = ((bf16[4,16,8192]{2,1,0:T(8,128)(2,1)}), bf16[4,16,8192]{2,1,0:T(8,128)(2,1)S(1)}, u32[]{:S(2)}, u32[]{:S(2)}) async-start(bf16[4,16,8192]{2,1,0:T(8,128)(2,1)} %bitcast.33), calls=%async_computation.2 | async-start | bytes 2097152 | tf_op jit(solution)/shard_map/all_to_all | solution.py:52
  76.0 67.5 %all-gather.6.cloned.1.call-start = ((), (), s32[]{:S(2)}) async-start(), calls=%async_computation.8 | async-start | bytes 1310720 | tf_op jit(solution)/shard_map/all_gather | solution.py:104
  77.4 1.3 copy-start.4
  77.4 40.5 %collective-permute-start = (bf16[16,8192]{1,0:T(8,128)(2,1)S(1)}, bf16[16,8192]{1,0:T(8,128)(2,1)}, u32[]{:S(2)}, u32[]{:S(2)}) collective-permute-start(bf16[16,8192]{1,0:T(8,128)(2,1)S(1)} %fusion.49), channel_id=1, source_target_pairs={{16,0},{17,1},{18,2},{19,3},{20,4},{21,5},{22,6},{23,7},{24,8},{25... | collective-permute-start | bytes 786440 | tf_op jit(solution)/shard_map/ppermute | solution.py:10
  78.8 91.8 %all-gather.8.cloned.1.call-start = ((), (), s32[]{:S(2)}) async-start(), calls=%async_computation.9 | async-start | bytes 1310720 | tf_op jit(solution)/shard_map/all_gather | solution.py:104
  79.5 38.4 %copy-start.16 = (f32[16]{0:T(128)}, f32[16]{0:T(128)S(1)}, u32[]{:S(2)}) copy-start(f32[16]{0:T(128)S(1)} %get-tuple-element.46) | copy-start | bytes 196
  80.7 57.0 %copy-start.14 = (f32[16]{0:T(128)}, f32[16]{0:T(128)S(1)}, u32[]{:S(2)}) copy-start(f32[16]{0:T(128)S(1)} %get-tuple-element.52) | copy-start | bytes 196
  125.2 1.3 copy-start.5
  125.2 8.3 %collective-permute-start.1 = (bf16[16,8192]{1,0:T(8,128)(2,1)S(1)}, bf16[16,8192]{1,0:T(8,128)(2,1)S(1)}, u32[]{:S(2)}, u32[]{:S(2)}) collective-permute-start(bf16[16,8192]{1,0:T(8,128)(2,1)S(1)} %fusion.59), channel_id=1, source_target_pairs={{16,0},{17,1},{18,2},{19,3},{20,4},{21,5},{22,6},{23,7},{24,8},{25... | collective-permute-start | bytes 786440 | tf_op jit(solution)/shard_map/ppermute | solution.py:10
  126.5 68.5 %all-gather.10.cloned.1.call-start = ((), (), s32[]{:S(2)}) async-start(), calls=%async_computation.10 | async-start | bytes 1310720 | tf_op jit(solution)/shard_map/all_gather | solution.py:104
  134.5 36.1 %copy-start.3 = (bf16[16,8192]{1,0:T(8,128)(2,1)}, bf16[16,8192]{1,0:T(8,128)(2,1)S(1)}, u32[]{:S(2)}) copy-start(bf16[16,8192]{1,0:T(8,128)(2,1)S(1)} %bitcast_select_fusion) | copy-start | bytes 786436
  139.2 147.5 %reduce-scatter.7.cloned.1.call-start = ((), (), s32[]{:S(2)}) async-start(), calls=%async_computation.12 | async-start | bytes 2621440
  143.2 27.4 %copy-start.7 = (bf16[1,3,64,2048]{3,2,1,0:T(8,128)(2,1)S(1)}, bf16[1,3,64,2048]{3,2,1,0:T(8,128)(2,1)}, u32[]{:S(2)}) copy-start(bf16[1,3,64,2048]{3,2,1,0:T(8,128)(2,1)} %param.15) | copy-start | bytes 2359300
  143.2 27.4 %copy-start.8 = (bf16[1,3,64,2048]{3,2,1,0:T(8,128)(2,1)S(1)}, bf16[1,3,64,2048]{3,2,1,0:T(8,128)(2,1)}, u32[]{:S(2)}) copy-start(bf16[1,3,64,2048]{3,2,1,0:T(8,128)(2,1)} %param.16) | copy-start | bytes 2359300
  143.2 339.5 %reduce-scatter.5.cloned.1.call-start = ((), (), s32[]{:S(2)}) async-start(), calls=%async_computation.11 | async-start | bytes 41943040 | tf_op jit(solution)/shard_map/reduce_scatter | solution.py:121
  248.6 11.4 %copy-start.21 = (u32[32]{0:T(128)S(1)}, u32[32]{0:T(128)}, u32[]{:S(2)}) copy-start(u32[32]{0:T(128)} %constant.58) | copy-start | bytes 388
  248.6 14.8 %copy-start.11 = (f32[16,2]{0,1:T(2,128)S(1)}, f32[16,2]{0,1:T(2,128)}, u32[]{:S(2)}) copy-start(f32[16,2]{0,1:T(2,128)} %get-tuple-element.17) | copy-start | bytes 388
  248.6 21.7 %copy-start.12 = (f32[16,2]{0,1:T(2,128)S(1)}, f32[16,2]{0,1:T(2,128)}, u32[]{:S(2)}) copy-start(f32[16,2]{0,1:T(2,128)} %get-tuple-element.19) | copy-start | bytes 388
  248.6 21.9 %copy-start.9 = (f32[8192]{0:T(1024)S(1)}, f32[8192]{0:T(1024)}, u32[]{:S(2)}) copy-start(f32[8192]{0:T(1024)} %get-tuple-element.9) | copy-start | bytes 98308
  248.7 21.9 %copy-start.10 = (f32[8192]{0:T(1024)S(1)}, f32[8192]{0:T(1024)}, u32[]{:S(2)}) copy-start(f32[8192]{0:T(1024)} %get-tuple-element.7) | copy-start | bytes 98308
  248.7 59.7 %copy-start = (bf16[64,8192]{1,0:T(8,128)(2,1)S(1)}, bf16[64,8192]{1,0:T(8,128)(2,1)}, u32[]{:S(2)}) copy-start(bf16[64,8192]{1,0:T(8,128)(2,1)} %all-gather.6.cloned.1.call-done) | copy-start | bytes 3145732
  248.7 79.7 %copy-start.1 = (bf16[64,8192]{1,0:T(8,128)(2,1)S(1)}, bf16[64,8192]{1,0:T(8,128)(2,1)}, u32[]{:S(2)}) copy-start(bf16[64,8192]{1,0:T(8,128)(2,1)} %all-gather.8.cloned.1.call-done) | copy-start | bytes 3145732
  255.8 69.1 %all-to-all-start.3 = ((bf16[4,16,8192]{2,1,0:T(8,128)(2,1)}), bf16[4,16,8192]{2,1,0:T(8,128)(2,1)}, u32[]{:S(2)}, u32[]{:S(2)}) async-start(bf16[4,16,8192]{2,1,0:T(8,128)(2,1)} %bitcast.57), calls=%async_computation.3 | async-start | bytes 2097152 | tf_op jit(solution)/shard_map/all_to_all | solution.py:99
  308.3 45.6 %copy-start.2 = (bf16[64,8192]{1,0:T(8,128)(2,1)S(1)}, bf16[64,8192]{1,0:T(8,128)(2,1)}, u32[]{:S(2)}) copy-start(bf16[64,8192]{1,0:T(8,128)(2,1)} %all-gather.10.cloned.1.call-done) | copy-start | bytes 3145732
  324.9 25.6 %all-to-all-start.4 = ((bf16[4,16,8192]{2,1,0:T(8,128)(2,1)}), bf16[4,16,8192]{2,1,0:T(8,128)(2,1)S(1)}, u32[]{:S(2)}, u32[]{:S(2)}) async-start(bf16[4,16,8192]{2,1,0:T(8,128)(2,1)} %bitcast.256), calls=%async_computation.4 | async-start | bytes 2097152 | tf_op jit(solution)/shard_map/all_to_all | solution.py:99
  350.5 27.5 %all-to-all-start.5 = ((bf16[4,16,8192]{2,1,0:T(8,128)(2,1)}), bf16[4,16,8192]{2,1,0:T(8,128)(2,1)S(1)}, u32[]{:S(2)}, u32[]{:S(2)}) async-start(bf16[4,16,8192]{2,1,0:T(8,128)(2,1)} %bitcast.61), calls=%async_computation.5 | async-start | bytes 2097152 | tf_op jit(solution)/shard_map/all_to_all | solution.py:99
Sparse Core Ops, SparseCore 0:
  78.9 39.4 all-gather.5
  126.7 28.9 all-gather.7
  157.8 27.4 all-gather.9
Sparse Core Ops, SparseCore 1:
  143.3 30.2 reduce-scatter.6
  248.8 233.9 reduce-scatter.4
where the time goes:
time: 508 us; the launch traced here: 502 us
  matrix products  175 us (34%)
  waiting for transfers between devices  167 us (33%)
  other arithmetic  48.6 us (10%)
  blocking collectives  40.4 us (8%)
  starting transfers between devices  27.9 us (5%)
  local copies, waits for them, and re-layouts  26.2 us (5%)
  between operations  16.9 us (3%)
    dot_general x3, matrix products, on_device(): lax.dot_general(gated, shard_rows, (((0,), (0,)), ((), ())), preferred_el...  105 us
    reduce_scatter x1, waiting for transfers between devices, on_device(): lax.psum_scatter(grad_acc.astype(jnp.bfloat16), 'dp', scatter_dimension=1...  102 us
    dot_general x3, matrix products, on_device(): lax.dot_general(shard_rows, weight_rows, (((1,), (1,)), ((), ())), prefer...  51.4 us
    all_to_all x3, waiting for transfers between devices, on_device(): lax.all_to_all(expert_back[0, micro_step], 'tensor', split_axis=0, concat...  50.6 us
    psum x1, blocking collectives, on_device(): lax.psum(router_acc.astype(jnp.bfloat16), 'tensor').astype(jnp.float32)  19.1 us
    all_to_all x3, starting transfers between devices, on_device(): lax.all_to_all(expert_back[0, micro_step], 'tensor', split_axis=0, concat...  13.4 us
    broadcast_in_dim x1, other arithmetic, on_device(): weight_grad[None]  11.7 us
    all_to_all x3, starting transfers between devices, on_device(): lax.all_to_all(send_buffer, 'tensor', split_axis=0, concat_axis=0, tiled=...  11.3 us
  transfers between devices with their start and end apart: 13, of which 7 were waited for; matrix products, arithmetic and copies ran while one was open for 47% of the time, Pallas kernels for 0%

commit v1 on v0

v1 whole, which is shorter than its diff:
```python
import jax
import jax.numpy as jnp
from jax import lax
from jax.sharding import PartitionSpec as P

F32 = jnp.float32
BF16 = jnp.bfloat16


def partner(shard, axis, mask):
    length = lax.axis_size(axis)
    return lax.ppermute(shard, axis, [(i, i ^ mask) for i in range(length)])


def around(shard, axis, by):
    length = lax.axis_size(axis)
    return lax.ppermute(shard, axis, [(i, (i + by) % length) for i in range(length)])


def exchange_rows(block, axis):
    length = lax.axis_size(axis)
    got = [around(block, axis, length - r) for r in range(1, length)]
    return [block] + got


def line_gather(block, only_section=None):
    length = lax.axis_size("tensor")
    if length > 4:
        return exchange_rows(block, "tensor")
    me = lax.axis_index("tensor")
    if only_section is None:
        axes, base = "tensor", 0
    else:
        axes, base = ("section", "tensor"), only_section * length
    up, down = block, block
    ups, downs = [], []
    for s in range(1, length):
        up = lax.ppermute(up, axes, [(base + i, base + i + 1) for i in range(s - 1, length - 1)])
        down = lax.ppermute(down, axes, [(base + i, base + i - 1) for i in range(1, length - s + 1)])
        ups.append(up)
        downs.append(down)
    got = [block]
    for r in range(1, length):
        got.append(jnp.where(me + r < length, downs[r - 1], ups[length - r - 1]))
    return got


def turned(blocks, start):
    length = blocks.shape[0]
    twice = jnp.concatenate([blocks, blocks], axis=0)
    return lax.dynamic_slice_in_dim(twice, start, length, axis=0)


def earlier(named):
    count = named.shape[-1]
    order = jnp.arange(count, dtype=jnp.int32)
    before = (order[:, None] < order[None, :]).astype(F32)
    return jnp.sum(named[..., :, None] * before, axis=-2)


def on_device(
    incoming, hidden, expert_out, routes, expert_back, scan_out, gate_in, w_out, w_router, norm_gain
):
    micro = incoming.shape[1]
    rows = incoming.shape[2]
    width = incoming.shape[3]
    experts = w_router.shape[2]
    n = lax.axis_size("tensor")
    n_dp = lax.axis_size("dp")
    cap = expert_back.shape[2] // n
    inner = scan_out.shape[3]
    group = scan_out.shape[2]
    columns = width // n_dp
    me = lax.axis_index("tensor")
    me_dp = lax.axis_index("dp")
    upper = lax.axis_index("section") == 1
    weight = w_out[0]

    def tied(value, *others):
        return lax.optimization_barrier((value,) + others)[0]

    back = expert_back[0].reshape(micro, n, cap, width)
    returned = [lax.dynamic_index_in_dim(back, me, 1, False)]
    for r in range(1, n):
        s = n - r
        block = lax.dynamic_index_in_dim(back, (me + s) % n, 1, False)
        returned.append(around(block, "tensor", s))

    small = jnp.concatenate([w_router[0].T, norm_gain[0][None]], axis=0)
    smalls = jnp.stack([small] + [partner(small, "dp", m) for m in range(1, n_dp)])
    smalls = jnp.stack([lax.dynamic_index_in_dim(smalls, me_dp ^ g, 0, False) for g in range(n_dp)])
    smalls = jnp.swapaxes(smalls, 0, 1).reshape(experts + 1, width)
    router = smalls[:experts]
    gain = smalls[experts:].astype(F32)

    scan_f = scan_out[0].astype(F32)
    gate_f = gate_in[0].astype(F32)
    sig = jax.nn.sigmoid(gate_f)
    gated = (scan_f * gate_f * sig).astype(BF16)
    gated = turned(jnp.swapaxes(gated.reshape(micro, n, rows, inner), 0, 1), me)
    gated = jnp.swapaxes(gated, 0, 1).reshape(micro * group, inner)
    if n_dp == 4:
        across = partner(gated, "dp", 2)
        pair = partner(jnp.stack([gated, across]), "dp", 1)
        gated_all = [gated, pair[0], across, pair[1]]
    else:
        gated_all = [gated] + [partner(gated, "dp", m) for m in range(1, n_dp)]

    hidden_f = hidden[0].astype(F32)
    inv_rms = 1.0 / jnp.sqrt(jnp.mean(hidden_f * hidden_f, axis=2, keepdims=True) + 1e-05)
    normed = (hidden_f * inv_rms * gain).astype(BF16)
    logits = lax.dot_general(
        normed, router, (((2,), (1,)), ((), ())), preferred_element_type=F32
    )
    weights = jnp.exp(logits)
    probs = weights / jnp.sum(weights, axis=2, keepdims=True)
    chosen = (routes[0][..., None] == jnp.arange(experts, dtype=jnp.int32)).astype(F32)
    named = jnp.sum(chosen, axis=2)
    marked = jnp.where(named > 0, probs, -1.0)
    marks = jnp.stack(exchange_rows(marked, "tensor"))

    named_t = jnp.swapaxes(named, 1, 2)
    place = earlier(named_t)
    slots = jnp.arange(cap, dtype=F32)
    pick = named_t[..., None] * (place[..., None] == slots)
    pick = turned(jnp.swapaxes(pick, 0, 1), me)
    pick = jnp.transpose(pick, (1, 2, 0, 3)).reshape(micro, rows, n * cap).astype(BF16)

    mine = lax.dynamic_index_in_dim(marks, me, 3, False)
    mine = jnp.swapaxes(mine, 0, 1)
    mine_named = (mine >= 0).astype(F32)
    mine_place = earlier(mine_named)
    put = mine_named[..., None] * (mine_place[..., None] == slots)
    slot_prob = jnp.sum(put * mine[..., None], axis=2)
    owner = (me + jnp.arange(n, dtype=jnp.int32)) % n
    at = (jnp.arange(n, dtype=jnp.int32)[:, None] == owner[None, :]).astype(F32)
    put = jnp.einsum("jr,mric->mjcri", at, put).reshape(micro, n * cap, n * rows).astype(BF16)
    slot_prob = jnp.einsum("jr,mrc->mjc", at, slot_prob).reshape(micro, n * cap, 1)

    back_sum = jnp.stack(
        [
            jnp.dot(
                pick[t],
                jnp.concatenate([x[t] for x in returned], axis=0),
                preferred_element_type=F32,
            )
            for t in range(micro)
        ]
    )

    def step_back(t0, t1, upstream):
        upstream_f = upstream.astype(F32)
        score = jnp.sum(upstream_f[:, :, None, :] * expert_out[0, t0:t1].astype(F32), axis=3)
        prob_grad = jnp.sum(chosen[t0:t1] * score[..., None], axis=2)
        p = probs[t0:t1]
        logit_grad = (p * (prob_grad - jnp.sum(p * prob_grad, axis=2, keepdims=True))).astype(BF16)
        norm_grad = back_sum[t0:t1] + lax.dot_general(
            logit_grad, router, (((2,), (0,)), ((), ())), preferred_element_type=F32
        )
        h = hidden_f[t0:t1]
        inv = inv_rms[t0:t1]
        scaled = norm_grad * gain
        hidden_grad = inv * scaled - h * inv**3 * jnp.mean(scaled * h, axis=2, keepdims=True)
        passed = (upstream_f + hidden_grad).astype(BF16)
        return passed, logit_grad, norm_grad

    first, logit_first, norm_first = step_back(0, micro, incoming[0])
    received = lax.ppermute(first[: micro - 1], "section", [(1, 0)])
    gathered = [jnp.concatenate(line_gather(first[0]), axis=0)]
    later_up = jnp.where(upper, incoming[0, 1:], received)
    later, logit_later, norm_later = step_back(1, micro, later_up)
    passed_all = jnp.concatenate([first[:1], later], axis=0)
    for t in range(1, micro):
        gathered.append(jnp.concatenate(line_gather(later[t - 1]), axis=0))
    sources = []
    for t in range(micro):
        rows_in = tied(incoming[0, t], gathered[micro - 1])
        sources.append(jnp.concatenate(line_gather(rows_in), axis=0))
    for t in range(1, micro):
        above = lax.ppermute(gathered[t - 1], "section", [(1, 0)])
        sources[t] = jnp.where(upper, sources[t], above)

    logit_grads = jnp.concatenate([logit_first[:1], logit_later], axis=0)
    norm_grads = jnp.concatenate([norm_first[:1], norm_later], axis=0)
    router_term = lax.dot_general(
        logit_grads.reshape(micro * rows, experts),
        normed.reshape(micro * rows, width),
        (((0,), (0,)), ((), ())),
        preferred_element_type=F32,
    )
    gain_term = jnp.sum(norm_grads * hidden_f * inv_rms, axis=(0, 1))[None]
    term = jnp.concatenate([router_term, gain_term], axis=0)
    total = lax.dynamic_slice_in_dim(term, me_dp * columns, columns, axis=1)
    for m in range(1, n_dp):
        sent = lax.dynamic_slice_in_dim(term, (me_dp ^ m) * columns, columns, axis=1)
        total = total + partner(sent, "dp", m)
    total = sum(exchange_rows(total, "tensor"))

    scan_grads, gate_grads = [None] * micro, [None] * micro
    column_parts = [[] for _ in range(n_dp)]
    for ts in ([0], list(range(1, micro))):
        held = jnp.concatenate([gathered[t] for t in ts], axis=0)
        for m in range(n_dp):
            block = lax.dynamic_slice_in_dim(held, (me_dp ^ m) * columns, columns, axis=1)
            column_parts[m].append(partner(block, "dp", m) if m else block)
        inner_rows = lax.dot_general(
            held, weight, (((1,), (1,)), ((), ())), preferred_element_type=F32
        )
        for i, t in enumerate(ts):
            mine_rows = inner_rows[i * group : (i + 1) * group].reshape(n, rows, inner)
            mine_rows = turned(mine_rows, (n - me) % n).reshape(group, inner)
            scan_grads[t] = (mine_rows * gate_f[t] * sig[t]).astype(BF16)
            gate_grads[t] = (
                mine_rows * scan_f[t] * sig[t] * (1.0 + gate_f[t] * (1.0 - sig[t]))
            ).astype(BF16)
    expert_grads = [
        (slot_prob[t] * jnp.dot(put[t], sources[t], preferred_element_type=F32)).astype(BF16)
        for t in range(micro)
    ]
    left = jnp.concatenate(gated_all, axis=0)
    right = jnp.concatenate([x for parts_m in column_parts for x in parts_m], axis=0)
    weight_grad = lax.dot_general(
        left, right, (((0,), (0,)), ((), ())), preferred_element_type=F32
    )
    return (
        passed_all[None],
        jnp.stack(scan_grads)[None],
        jnp.stack(gate_grads)[None],
        jnp.stack(expert_grads)[None],
        weight_grad[None],
        total[:experts].T[None],
        total[experts][None],
    )


def solution(mesh):
    placed = (
        P("section", None, ("dp", "tensor"), None),
        P("section", None, ("dp", "tensor"), None),
        P("section", None, ("dp", "tensor"), None, None),
        P("section", None, ("dp", "tensor"), None),
        P("section", None, ("dp", "tensor"), None),
        P("section", None, "dp", "tensor"),
        P("section", None, "dp", "tensor"),
        P("section", "tensor", None),
        P("section", "dp", None),
        P("section", "dp"),
    )
    return jax.shard_map(
        on_device,
        mesh=mesh,
        in_specs=placed,
        out_specs=(
            P("section", None, ("dp", "tensor"), None),
            P("section", None, "dp", "tensor"),
            P("section", None, "dp", "tensor"),
            P("section", None, ("dp", "tensor"), None),
            P("section", "tensor", "dp"),
            P("section", "dp", None),
            P("section", "dp"),
        ),
        check_vma=False,
    )
```

time: 508 us -> 315 us (0.62)
  matrix products: 175 us -> 51.4 us
  waiting for transfers between devices: 167 us -> 111 us
  starting transfers between devices: 27.9 us -> 82.8 us
  blocking collectives: 40.4 us -> 0 us
  between operations: 16.9 us -> 1.98 us
  other arithmetic: 48.6 us -> 34.4 us
    dot_general x18 -> x13, matrix products: 175 us -> 50.4 us  [the longest x2 31.4 us: on_device(): lax.dot_general(held, weight, (((1,), (1,)), ((), ())), preferred_element...]
    ppermute x2 -> x62, waiting for transfers between devices: 6.57 us -> 111 us  [the longest x18 62.3 us: line_gather(): lax.ppermute(down, axes, [(base + i, base + i - 1) for i in range(1, leng...]
    reduce_scatter x1 -> x0, waiting for transfers between devices: 102 us -> none  [on_device(): lax.psum_scatter(grad_acc.astype(jnp.bfloat16), 'dp', scatter_dimension=1...]
    ppermute x2 -> x62, starting transfers between devices: 2.58 us -> 82.8 us  [the longest x18 30 us: line_gather(): lax.ppermute(up, axes, [(base + i, base + i + 1) for i in range(s - 1, le...]
    all_to_all x6 -> x0, waiting for transfers between devices: 59.2 us -> none  [the longest x3 50.6 us: on_device(): lax.all_to_all(expert_back[0, micro_step], 'tensor', split_axis=0, concat...]
    all_to_all x6 -> x0, starting transfers between devices: 24.7 us -> none  [the longest x3 13.4 us: on_device(): lax.all_to_all(expert_back[0, micro_step], 'tensor', split_axis=0, concat...]
    psum x1 -> x0, blocking collectives: 19.1 us -> none  [on_device(): lax.psum(router_acc.astype(jnp.bfloat16), 'tensor').astype(jnp.float32)]
    squeeze x0 -> x15, local copies, waits for them, and re-layouts: none -> 16.1 us  [the longest x4 4.51 us: on_device(): x[t]]
  transfers between devices with their start and end apart: 13 -> 62, of which waited for: 7 -> 21; matrix products, arithmetic and copies ran while one was open for 47% -> 34% of each run, Pallas kernels for 0% -> 0%
where the time goes in v1:
time: 315 us; the launch traced here: 311 us
  waiting for transfers between devices  111 us (35%)
  starting transfers between devices  82.8 us (26%)
  matrix products  51.4 us (16%)
  other arithmetic  34.4 us (11%)
  local copies, waits for them, and re-layouts  29.5 us (9%)
    ppermute x18, waiting for transfers between devices, line_gather(): lax.ppermute(down, axes, [(base + i, base + i - 1) for i in range(1, leng...  62.3 us
    ppermute x9, waiting for transfers between devices, around(): lax.ppermute(shard, axis, [(i, (i + by) % length) for i in range(length)])  33.7 us
    dot_general x2, matrix products, on_device(): lax.dot_general(held, weight, (((1,), (1,)), ((), ())), preferred_element...  31.4 us
    ppermute x18, starting transfers between devices, line_gather(): lax.ppermute(up, axes, [(base + i, base + i + 1) for i in range(s - 1, le...  30 us
    ppermute x18, starting transfers between devices, line_gather(): lax.ppermute(down, axes, [(base + i, base + i - 1) for i in range(1, leng...  23.3 us
    ppermute x9, starting transfers between devices, around(): lax.ppermute(shard, axis, [(i, (i + by) % length) for i in range(length)])  16.2 us
    ppermute x14, waiting for transfers between devices, partner(): return lax.ppermute(shard, axis, [(i, i ^ mask) for i in range(length)])  14.9 us
    dot_general x1, matrix products, on_device(): lax.dot_general(left, right, (((0,), (0,)), ((), ())), preferred_element_...  11.6 us
  transfers between devices with their start and end apart: 62, of which 21 were waited for; matrix products, arithmetic and copies ran while one was open for 34% of the time, Pallas kernels for 0%

profile of v1, /device:TPU:0, one launch (start us, length us, event | category | flops | bytes accessed | tf_op | source)
XLA Modules:
  0.0 311.5 jit_solution(9275730283231935156)
XLA Ops:
  1.4 3.0 collective-permute-start.4
  4.6 3.1 %dynamic-slice_bitcast_fusion.2 = (bf16[3,16,8192]{2,1,0:T(8,128)(2,1)}, bf16[3,16,8192]{2,1,0:T(8,128)(2,1)}, bf16[3,16,8192]{2,1,0:T(8,128)(2,1)}) fusion(bf16[3,4,16,8192]{3,2,1,0:T(8,128)(2,1)} %bitcast.300, s32[]{:T(128)S(6)} %select_n.197, s32[]{:T(128)S(6)} %select_n.201, s32[]{:T(128)S(6)} %select_n.199), kind=kLoop, calls=%fused_computation.126 | loop fusion | bytes 4718604 | tf_op jit(solution)/shard_map/jit(dynamic_index_in_dim)/squeeze | solution.py:86
  7.8 4.0 %collective-permute-start = (bf16[3,16,8192]{2,1,0:T(8,128)(2,1)}, bf16[3,16,8192]{2,1,0:T(8,128)(2,1)}, u32[]{:S(2)}, u32[]{:S(2)}) collective-permute-start(bf16[3,16,8192]{2,1,0:T(8,128)(2,1)} %get-tuple-element.38), channel_id=1, source_target_pairs={{0,3},{1,0},{2,1},{3,2},{4,7},{5,4},{6,5},{7,6},{8,11},{9,8},{10,9... | collective-permute-start | bytes 2359304 | tf_op jit(solution)/shard_map/ppermute | solution.py:17
  14.9 3.1 %fusion.17 = f32[3,16,2]{2,1,0:T(8,128)S(1)} fusion(bf16[1,3,16,2,8192]{4,3,2,1,0:T(2,128)(2,1)} %param.12, f32[3,16,8192]{2,1,0:T(8,128)S(1)} %bitcast_convert_fusion), kind=kLoop, calls=%fused_computation.29 | loop fusion | flops 2359200 | bytes 3146112 | tf_op jit(solution)/shard_map/reduce_sum | solution.py:153
  18.1 3.0 multiply_convert_fusion
  21.4 2.1 dynamic-slice_bitcast_fusion.5
  29.9 4.4 %collective-permute-start.26 = (f32[3,16,4]{1,2,0:T(4,128)S(1)}, f32[3,16,4]{1,2,0:T(4,128)S(1)}, u32[]{:S(2)}, u32[]{:S(2)}) collective-permute-start(f32[3,16,4]{1,2,0:T(4,128)S(1)} %get-tuple-element.91), channel_id=1, source_target_pairs={{0,2},{1,3},{2,0},{3,1},{4,6},{5,7},{6,4},{7,5},{8,10},{9,11},{10,... | collective-permute-start | bytes 2312 | tf_op jit(solution)/shard_map/ppermute | solution.py:17
  34.9 12.2 %collective-permute-done.27 = f32[3,16,4]{1,2,0:T(4,128)S(1)} collective-permute-done((f32[3,16,4]{1,2,0:T(4,128)S(1)}, f32[3,16,4]{1,2,0:T(4,128)S(1)}, u32[]{:S(2)}, u32[]{:S(2)}) %collective-permute-start.27) | collective-permute-done | bytes 800 | tf_op jit(solution)/shard_map/ppermute | solution.py:17
  47.7 1.5 collective-permute-start.48
  56.5 1.5 squeeze.159
  62.1 21.5 %collective-permute-done.1 = bf16[3,16,8192]{2,1,0:T(8,128)(2,1)S(1)} collective-permute-done((bf16[3,16,8192]{2,1,0:T(8,128)(2,1)}, bf16[3,16,8192]{2,1,0:T(8,128)(2,1)S(1)}, u32[]{:S(2)}, u32[]{:S(2)}) %collective-permute-start.1) | collective-permute-done | bytes 786464 | tf_op jit(solution)/shard_map/ppermute | solution.py:17
  89.5 2.0 collective-permute-start.8
  92.8 2.6 pad_maximum_fusion
  95.8 1.4 collective-permute-start.9
  97.1 3.5 %collective-permute-done.7 = bf16[16,8192]{1,0:T(8,128)(2,1)} collective-permute-done((bf16[16,8192]{1,0:T(8,128)(2,1)S(1)}, bf16[16,8192]{1,0:T(8,128)(2,1)}, u32[]{:S(2)}, u32[]{:S(2)}) %collective-permute-start.7) | collective-permute-done | bytes 262176 | tf_op jit(solution)/shard_map/ppermute | solution.py:39
  102.1 1.3 fusion.18
  103.6 2.1 multiply_reduce_fusion
  106.6 1.6 collective-permute-start.57
  111.1 1.7 collective-permute-done.58
  112.9 2.7 collective-permute-start.61
  115.5 1.7 collective-permute-start.60
  117.2 2.8 collective-permute-start.59
  123.6 4.6 %collective-permute-start.14 = (bf16[16,8192]{1,0:T(8,128)(2,1)S(1)}, bf16[16,8192]{1,0:T(8,128)(2,1)S(1)}, u32[]{:S(2)}, u32[]{:S(2)}) collective-permute-start(bf16[16,8192]{1,0:T(8,128)(2,1)S(1)} %get-tuple-element.70), channel_id=1, source_target_pairs={{0,1},{1,2},{2,3},{4,5},{5,6},{6,7},{8,9},{9,10},{10,11},{12,13},{... | collective-permute-start | bytes 786440 | tf_op jit(solution)/shard_map/ppermute | solution.py:38
  132.5 6.8 %collective-permute-done.12 = bf16[16,8192]{1,0:T(8,128)(2,1)S(1)} collective-permute-done((bf16[16,8192]{1,0:T(8,128)(2,1)}, bf16[16,8192]{1,0:T(8,128)(2,1)S(1)}, u32[]{:S(2)}, u32[]{:S(2)}) %collective-permute-start.12) | collective-permute-done | bytes 262176 | tf_op jit(solution)/shard_map/ppermute | solution.py:39
  141.4 15.4 %fusion = f32[4,16,2048]{2,1,0:T(8,128)S(1)} fusion(bf16[4,16,8192]{2,1,0:T(8,128)(2,1)S(1)} %bitcast.296, bf16[1,2048,8192]{2,1,0:T(8,128)(2,1)} %param.17), kind=kOutput, calls=%fused_computation | convolution fusion | flops 2147483648 | bytes 35127296 | tf_op jit(solution)/shard_map/dot_general | solution.py:206
  162.6 8.7 %collective-permute-done.17 = bf16[16,8192]{1,0:T(8,128)(2,1)S(1)} collective-permute-done((bf16[16,8192]{1,0:T(8,128)(2,1)S(1)}, bf16[16,8192]{1,0:T(8,128)(2,1)S(1)}, u32[]{:S(2)}, u32[]{:S(2)}) %collective-permute-start.17) | collective-permute-done | bytes 262176 | tf_op jit(solution)/shard_map/ppermute | solution.py:39
  175.5 8.1 %collective-permute-done.23 = bf16[16,8192]{1,0:T(8,128)(2,1)S(1)} collective-permute-done((bf16[16,8192]{1,0:T(8,128)(2,1)S(1)}, bf16[16,8192]{1,0:T(8,128)(2,1)S(1)}, u32[]{:S(2)}, u32[]{:S(2)}) %collective-permute-start.23) | collective-permute-done | bytes 262176 | tf_op jit(solution)/shard_map/ppermute | solution.py:39
  184.3 2.5 collective-permute-done.18
  189.0 6.0 %collective-permute-done.24 = bf16[16,8192]{1,0:T(8,128)(2,1)S(1)} collective-permute-done((bf16[16,8192]{1,0:T(8,128)(2,1)S(1)}, bf16[16,8192]{1,0:T(8,128)(2,1)S(1)}, u32[]{:S(2)}, u32[]{:S(2)}) %collective-permute-start.24) | collective-permute-done | bytes 262176 | tf_op jit(solution)/shard_map/ppermute | solution.py:39
  195.1 2.2 collective-permute-start.29
  198.5 16.0 %fusion.2 = f32[128,2048]{1,0:T(8,128)S(1)} fusion(bf16[128,8192]{1,0:T(8,128)(2,1)S(1)} %constant_dynamic-update-slice_fusion, bf16[1,2048,8192]{2,1,0:T(8,128)(2,1)} %param.17), kind=kOutput, calls=%fused_computation.2 | convolution fusion | flops 4294967296 | bytes 36700160 | tf_op jit(solution)/shard_map/dot_general | solution.py:206
  220.5 4.5 %collective-permute-start.35 = (bf16[16,8192]{1,0:T(8,128)(2,1)S(1)}, bf16[16,8192]{1,0:T(8,128)(2,1)S(1)}, u32[]{:S(2)}, u32[]{:S(2)}) collective-permute-start(bf16[16,8192]{1,0:T(8,128)(2,1)S(1)} %copy-done.27), channel_id=1, source_target_pairs={{0,1},{1,2},{2,3},{4,5},{5,6},{6,7},{8,9},{9,10},{10,11},{12,13},{... | collective-permute-start | bytes 786440 | tf_op jit(solution)/shard_map/ppermute | solution.py:38
  227.0 1.4 collective-permute-start.34
  230.4 1.5 slice_bitcast_fusion.2
  231.9 6.4 %collective-permute-start.42 = (bf16[16,8192]{1,0:T(8,128)(2,1)S(1)}, bf16[16,8192]{1,0:T(8,128)(2,1)S(1)}, u32[]{:S(2)}, u32[]{:S(2)}) collective-permute-start(bf16[16,8192]{1,0:T(8,128)(2,1)S(1)} %copy-done.26), channel_id=1, source_target_pairs={{0,1},{1,2},{2,3},{4,5},{5,6},{6,7},{8,9},{9,10},{10,11},{12,13},{... | collective-permute-start | bytes 786440 | tf_op jit(solution)/shard_map/ppermute | solution.py:38
  240.4 1.6 collective-permute-done.32
  243.4 6.0 %collective-permute-done.41 = bf16[16,8192]{1,0:T(8,128)(2,1)S(1)} collective-permute-done((bf16[16,8192]{1,0:T(8,128)(2,1)S(1)}, bf16[16,8192]{1,0:T(8,128)(2,1)S(1)}, u32[]{:S(2)}, u32[]{:S(2)}) %collective-permute-start.41) | collective-permute-done | bytes 262176 | tf_op jit(solution)/shard_map/ppermute | solution.py:39
  250.9 1.6 collective-permute-done.38
  254.9 7.4 %collective-permute-done.45 = bf16[16,8192]{1,0:T(8,128)(2,1)S(1)} collective-permute-done((bf16[16,8192]{1,0:T(8,128)(2,1)S(1)}, bf16[16,8192]{1,0:T(8,128)(2,1)S(1)}, u32[]{:S(2)}, u32[]{:S(2)}) %collective-permute-start.45) | collective-permute-done | bytes 262176 | tf_op jit(solution)/shard_map/ppermute | solution.py:39
  262.3 1.9 collective-permute-done.51
  266.3 2.0 collective-permute-done.53
  270.3 9.1 %collective-permute-done.55 = bf16[128,2048]{1,0:T(8,128)(2,1)S(1)} collective-permute-done((bf16[128,2048]{1,0:T(8,128)(2,1)S(1)}, bf16[128,2048]{1,0:T(8,128)(2,1)S(1)}, u32[]{:S(2)}, u32[]{:S(2)}) %collective-permute-start.55) | collective-permute-done | bytes 524320 | tf_op jit(solution)/shard_map/ppermute | solution.py:12
  280.4 11.6 %convolution_bitcast_fusion.4 = f32[1,2048,2048]{2,1,0:T(8,128)} fusion(bf16[768,2048]{1,0:T(8,128)(2,1)S(1)} %constant_dynamic-update-slice_fusion.8, bf16[192,2048]{1,0:T(8,128)(2,1)S(1)} %get-tuple-element.46, bf16[192,2048]{1,0:T(8,128)(2,1)} %collective-permute-done.48, bf16[192,2048]{1,0:T(8,128)(2,1)S(1)} %get-tuple-element.45, ...), kind=kOutput, calls=%fused_computation.19 | convolution fusion | flops 6455033856 | bytes 23068672 | tf_op jit(solution)/shard_map/dot_general | solution.py:222
  296.4 6.9 %collective-permute-done.39 = bf16[16,8192]{1,0:T(8,128)(2,1)S(1)} collective-permute-done((bf16[16,8192]{1,0:T(8,128)(2,1)S(1)}, bf16[16,8192]{1,0:T(8,128)(2,1)S(1)}, u32[]{:S(2)}, u32[]{:S(2)}) %collective-permute-start.39) | collective-permute-done | bytes 262176 | tf_op jit(solution)/shard_map/ppermute | solution.py:39
  303.4 1.4 fusion.9
  304.9 1.7 fusion.8
  306.5 2.4 collective-permute-done.46
  309.4 2.0 maximum_bitcast_fusion
  (293 shorter events, 87.0 us)
Async XLA Ops:
  1.4 26.5 %collective-permute-start.4 = (bf16[5,2048]{1,0:T(8,128)(2,1)S(1)}, bf16[5,2048]{1,0:T(8,128)(2,1)S(1)}, u32[]{:S(2)}, u32[]{:S(2)}) collective-permute-start(bf16[5,2048]{1,0:T(8,128)(2,1)S(1)} %get-tuple-element.85), channel_id=1, source_target_pairs={{0,8},{4,12},{8,0},{12,4},{1,9},{5,13},{9,1},{13,5},{2,10},{6,14},... | collective-permute-start | bytes 61448 | tf_op jit(solution)/shard_map/ppermute | solution.py:12
  4.4 23.5 %collective-permute-start.3 = (bf16[5,2048]{1,0:T(8,128)(2,1)S(1)}, bf16[5,2048]{1,0:T(8,128)(2,1)S(1)}, u32[]{:S(2)}, u32[]{:S(2)}) collective-permute-start(bf16[5,2048]{1,0:T(8,128)(2,1)S(1)} %get-tuple-element.85), channel_id=1, source_target_pairs={{0,4},{4,0},{8,12},{12,8},{1,5},{5,1},{9,13},{13,9},{2,6},{6,2},{1... | collective-permute-start | bytes 61448 | tf_op jit(solution)/shard_map/ppermute | solution.py:12
  4.4 23.5 %collective-permute-start.5 = (bf16[5,2048]{1,0:T(8,128)(2,1)S(1)}, bf16[5,2048]{1,0:T(8,128)(2,1)}, u32[]{:S(2)}, u32[]{:S(2)}) collective-permute-start(bf16[5,2048]{1,0:T(8,128)(2,1)S(1)} %get-tuple-element.85), channel_id=1, source_target_pairs={{0,12},{4,8},{8,4},{12,0},{1,13},{5,9},{9,5},{13,1},{2,14},{6,10},... | collective-permute-start | bytes 61448 | tf_op jit(solution)/shard_map/ppermute | solution.py:12
  7.8 51.9 %collective-permute-start = (bf16[3,16,8192]{2,1,0:T(8,128)(2,1)}, bf16[3,16,8192]{2,1,0:T(8,128)(2,1)}, u32[]{:S(2)}, u32[]{:S(2)}) collective-permute-start(bf16[3,16,8192]{2,1,0:T(8,128)(2,1)} %get-tuple-element.38), channel_id=1, source_target_pairs={{0,3},{1,0},{2,1},{3,2},{4,7},{5,4},{6,5},{7,6},{8,11},{9,8},{10,9... | collective-permute-start | bytes 2359304 | tf_op jit(solution)/shard_map/ppermute | solution.py:17
  11.8 49.1 %collective-permute-start.2 = (bf16[3,16,8192]{2,1,0:T(8,128)(2,1)}, bf16[3,16,8192]{2,1,0:T(8,128)(2,1)}, u32[]{:S(2)}, u32[]{:S(2)}) collective-permute-start(bf16[3,16,8192]{2,1,0:T(8,128)(2,1)} %get-tuple-element.39), channel_id=1, source_target_pairs={{0,1},{1,2},{2,3},{3,0},{4,5},{5,6},{6,7},{7,4},{8,9},{9,10},{10,1... | collective-permute-start | bytes 2359304 | tf_op jit(solution)/shard_map/ppermute | solution.py:17
  29.9 17.3 %collective-permute-start.27 = (f32[3,16,4]{1,2,0:T(4,128)S(1)}, f32[3,16,4]{1,2,0:T(4,128)S(1)}, u32[]{:S(2)}, u32[]{:S(2)}) collective-permute-start(f32[3,16,4]{1,2,0:T(4,128)S(1)} %get-tuple-element.91), channel_id=1, source_target_pairs={{0,1},{1,2},{2,3},{3,0},{4,5},{5,6},{6,7},{7,4},{8,9},{9,10},{10,1... | collective-permute-start | bytes 2312 | tf_op jit(solution)/shard_map/ppermute | solution.py:17
  29.9 17.8 %collective-permute-start.26 = (f32[3,16,4]{1,2,0:T(4,128)S(1)}, f32[3,16,4]{1,2,0:T(4,128)S(1)}, u32[]{:S(2)}, u32[]{:S(2)}) collective-permute-start(f32[3,16,4]{1,2,0:T(4,128)S(1)} %get-tuple-element.91), channel_id=1, source_target_pairs={{0,2},{1,3},{2,0},{3,1},{4,6},{5,7},{6,4},{7,5},{8,10},{9,11},{10,... | collective-permute-start | bytes 2312 | tf_op jit(solution)/shard_map/ppermute | solution.py:17
  34.3 14.9 %collective-permute-start.25 = (f32[3,16,4]{1,2,0:T(4,128)S(1)}, f32[3,16,4]{1,2,0:T(4,128)S(1)}, u32[]{:S(2)}, u32[]{:S(2)}) collective-permute-start(f32[3,16,4]{1,2,0:T(4,128)S(1)} %get-tuple-element.91), channel_id=1, source_target_pairs={{0,3},{1,0},{2,1},{3,2},{4,7},{5,4},{6,5},{7,6},{8,11},{9,8},{10,9... | collective-permute-start | bytes 2312 | tf_op jit(solution)/shard_map/ppermute | solution.py:17
  47.1 36.5 %collective-permute-start.1 = (bf16[3,16,8192]{2,1,0:T(8,128)(2,1)}, bf16[3,16,8192]{2,1,0:T(8,128)(2,1)S(1)}, u32[]{:S(2)}, u32[]{:S(2)}) collective-permute-start(bf16[3,16,8192]{2,1,0:T(8,128)(2,1)} %get-tuple-element.40), channel_id=1, source_target_pairs={{0,2},{1,3},{2,0},{3,1},{4,6},{5,7},{6,4},{7,5},{8,10},{9,11},{10,... | collective-permute-start | bytes 2359304 | tf_op jit(solution)/shard_map/ppermute | solution.py:17
  47.7 45.1 %collective-permute-start.48 = (bf16[192,2048]{1,0:T(8,128)(2,1)S(1)}, bf16[192,2048]{1,0:T(8,128)(2,1)}, u32[]{:S(2)}, u32[]{:S(2)}) collective-permute-start(bf16[192,2048]{1,0:T(8,128)(2,1)S(1)} %bitcast.297), channel_id=1, source_target_pairs={{0,8},{4,12},{8,0},{12,4},{1,9},{5,13},{9,1},{13,5},{2,10},{6,14},... | collective-permute-start | bytes 2359304 | tf_op jit(solution)/shard_map/ppermute | solution.py:12
  86.6 15.4 %collective-permute-start.6 = (bf16[2,16,8192]{2,1,0:T(8,128)(2,1)S(1)}, bf16[2,16,8192]{2,1,0:T(8,128)(2,1)S(1)}, u32[]{:S(2)}, u32[]{:S(2)}) collective-permute-start(bf16[2,16,8192]{2,1,0:T(8,128)(2,1)S(1)} %slice.291), channel_id=1, source_target_pairs={{16,0},{17,1},{18,2},{19,3},{20,4},{21,5},{22,6},{23,7},{24,8},{25... | collective-permute-start | bytes 1572872 | tf_op jit(solution)/shard_map/ppermute | solution.py:168
  95.4 133.7 %collective-permute-start.49 = (bf16[2,192,2048]{2,1,0:T(8,128)(2,1)}, bf16[2,192,2048]{2,1,0:T(8,128)(2,1)}, u32[]{:S(2)}, u32[]{:S(2)}) collective-permute-start(bf16[2,192,2048]{2,1,0:T(8,128)(2,1)} %pad_maximum_fusion), channel_id=1, source_target_pairs={{0,4},{4,0},{8,12},{12,8},{1,5},{5,1},{9,13},{13,9},{2,6},{6,2},{1... | collective-permute-start | bytes 4718600 | tf_op jit(solution)/shard_map/ppermute | solution.py:12
  95.8 12.9 %collective-permute-start.9 = (bf16[16,8192]{1,0:T(8,128)(2,1)}, bf16[16,8192]{1,0:T(8,128)(2,1)}, u32[]{:S(2)}, u32[]{:S(2)}) collective-permute-start(bf16[16,8192]{1,0:T(8,128)(2,1)} %collective-permute-done.8), channel_id=1, source_target_pairs={{1,2},{2,3},{5,6},{6,7},{9,10},{10,11},{13,14},{14,15},{17,18},{18... | collective-permute-start | bytes 786440 | tf_op jit(solution)/shard_map/ppermute | solution.py:38
  117.2 11.0 %collective-permute-start.59 = (f32[5,2048]{1,0:T(8,128)S(1)}, f32[5,2048]{1,0:T(8,128)S(1)}, u32[]{:S(2)}, u32[]{:S(2)}) collective-permute-start(f32[5,2048]{1,0:T(8,128)S(1)} %fusion.112), channel_id=1, source_target_pairs={{0,3},{1,0},{2,1},{3,2},{4,7},{5,4},{6,5},{7,6},{8,11},{9,8},{10,9... | collective-permute-start | bytes 122888 | tf_op jit(solution)/shard_map/ppermute | solution.py:17
  121.0 39.6 %collective-permute-start.20 = (bf16[16,8192]{1,0:T(8,128)(2,1)S(1)}, bf16[16,8192]{1,0:T(8,128)(2,1)S(1)}, u32[]{:S(2)}, u32[]{:S(2)}) collective-permute-start(bf16[16,8192]{1,0:T(8,128)(2,1)S(1)} %get-tuple-element.69), channel_id=1, source_target_pairs={{0,1},{1,2},{2,3},{4,5},{5,6},{6,7},{8,9},{9,10},{10,11},{12,13},{... | collective-permute-start | bytes 786440 | tf_op jit(solution)/shard_map/ppermute | solution.py:38
  122.3 39.6 %collective-permute-start.19 = (bf16[16,8192]{1,0:T(8,128)(2,1)S(1)}, bf16[16,8192]{1,0:T(8,128)(2,1)S(1)}, u32[]{:S(2)}, u32[]{:S(2)}) collective-permute-start(bf16[16,8192]{1,0:T(8,128)(2,1)S(1)} %get-tuple-element.69), channel_id=1, source_target_pairs={{1,0},{2,1},{3,2},{5,4},{6,5},{7,6},{9,8},{10,9},{11,10},{13,12},{... | collective-permute-start | bytes 786440 | tf_op jit(solution)/shard_map/ppermute | solution.py:39
  123.6 17.0 %collective-permute-start.14 = (bf16[16,8192]{1,0:T(8,128)(2,1)S(1)}, bf16[16,8192]{1,0:T(8,128)(2,1)S(1)}, u32[]{:S(2)}, u32[]{:S(2)}) collective-permute-start(bf16[16,8192]{1,0:T(8,128)(2,1)S(1)} %get-tuple-element.70), channel_id=1, source_target_pairs={{0,1},{1,2},{2,3},{4,5},{5,6},{6,7},{8,9},{9,10},{10,11},{12,13},{... | collective-permute-start | bytes 786440 | tf_op jit(solution)/shard_map/ppermute | solution.py:38
  139.2 17.5 %collective-permute-start.13 = (bf16[16,8192]{1,0:T(8,128)(2,1)S(1)}, bf16[16,8192]{1,0:T(8,128)(2,1)S(1)}, u32[]{:S(2)}, u32[]{:S(2)}) collective-permute-start(bf16[16,8192]{1,0:T(8,128)(2,1)S(1)} %get-tuple-element.70), channel_id=1, source_target_pairs={{1,0},{2,1},{3,2},{5,4},{6,5},{7,6},{9,8},{10,9},{11,10},{13,12},{... | collective-permute-start | bytes 786440 | tf_op jit(solution)/shard_map/ppermute | solution.py:39
  140.7 17.4 %collective-permute-start.15 = (bf16[16,8192]{1,0:T(8,128)(2,1)S(1)}, bf16[16,8192]{1,0:T(8,128)(2,1)S(1)}, u32[]{:S(2)}, u32[]{:S(2)}) collective-permute-start(bf16[16,8192]{1,0:T(8,128)(2,1)S(1)} %collective-permute-done.14), channel_id=1, source_target_pairs={{1,2},{2,3},{5,6},{6,7},{9,10},{10,11},{13,14},{14,15},{17,18},{18... | collective-permute-start | bytes 786440 | tf_op jit(solution)/shard_map/ppermute | solution.py:38
  156.8 14.5 %collective-permute-start.17 = (bf16[16,8192]{1,0:T(8,128)(2,1)S(1)}, bf16[16,8192]{1,0:T(8,128)(2,1)S(1)}, u32[]{:S(2)}, u32[]{:S(2)}) collective-permute-start(bf16[16,8192]{1,0:T(8,128)(2,1)S(1)} %collective-permute-done.13), channel_id=1, source_target_pairs={{1,0},{2,1},{5,4},{6,5},{9,8},{10,9},{13,12},{14,13},{17,16},{18,1... | collective-permute-start | bytes 786440 | tf_op jit(solution)/shard_map/ppermute | solution.py:39
  158.1 14.5 %collective-permute-start.16 = (bf16[16,8192]{1,0:T(8,128)(2,1)S(1)}, bf16[16,8192]{1,0:T(8,128)(2,1)S(1)}, u32[]{:S(2)}, u32[]{:S(2)}) collective-permute-start(bf16[16,8192]{1,0:T(8,128)(2,1)S(1)} %collective-permute-done.15), channel_id=1, source_target_pairs={{2,3},{6,7},{10,11},{14,15},{18,19},{22,23},{26,27},{30,31}} | collective-permute-start | bytes 786440 | tf_op jit(solution)/shard_map/ppermute | solution.py:38
  160.6 144.2 %collective-permute-start.40 = (bf16[64,8192]{1,0:T(8,128)(2,1)S(1)}, bf16[64,8192]{1,0:T(8,128)(2,1)}, u32[]{:S(2)}, u32[]{:S(2)}) collective-permute-start(bf16[64,8192]{1,0:T(8,128)(2,1)S(1)} %pad_maximum_fusion.1), channel_id=1, source_target_pairs={{16,0},{17,1},{18,2},{19,3},{20,4},{21,5},{22,6},{23,7},{24,8},{25... | collective-permute-start | bytes 3145736 | tf_op jit(solution)/shard_map/ppermute | solution.py:180
  161.9 13.5 %collective-permute-start.21 = (bf16[16,8192]{1,0:T(8,128)(2,1)S(1)}, bf16[16,8192]{1,0:T(8,128)(2,1)S(1)}, u32[]{:S(2)}, u32[]{:S(2)}) collective-permute-start(bf16[16,8192]{1,0:T(8,128)(2,1)S(1)} %collective-permute-done.20), channel_id=1, source_target_pairs={{1,2},{2,3},{5,6},{6,7},{9,10},{10,11},{13,14},{14,15},{17,18},{18... | collective-permute-start | bytes 786440 | tf_op jit(solution)/shard_map/ppermute | solution.py:38
  171.3 12.3 %collective-permute-start.23 = (bf16[16,8192]{1,0:T(8,128)(2,1)S(1)}, bf16[16,8192]{1,0:T(8,128)(2,1)S(1)}, u32[]{:S(2)}, u32[]{:S(2)}) collective-permute-start(bf16[16,8192]{1,0:T(8,128)(2,1)S(1)} %collective-permute-done.19), channel_id=1, source_target_pairs={{1,0},{2,1},{5,4},{6,5},{9,8},{10,9},{13,12},{14,13},{17,16},{18,1... | collective-permute-start | bytes 786440 | tf_op jit(solution)/shard_map/ppermute | solution.py:39
  172.6 14.1 %collective-permute-start.18 = (bf16[16,8192]{1,0:T(8,128)(2,1)S(1)}, bf16[16,8192]{1,0:T(8,128)(2,1)S(1)}, u32[]{:S(2)}, u32[]{:S(2)}) collective-permute-start(bf16[16,8192]{1,0:T(8,128)(2,1)S(1)} %collective-permute-done.17), channel_id=1, source_target_pairs={{1,0},{5,4},{9,8},{13,12},{17,16},{21,20},{25,24},{29,28}} | collective-permute-start | bytes 786440 | tf_op jit(solution)/shard_map/ppermute | solution.py:39
  175.5 44.3 %collective-permute-start.50 = (bf16[64,2048]{1,0:T(8,128)(2,1)}, bf16[64,2048]{1,0:T(8,128)(2,1)}, u32[]{:S(2)}, u32[]{:S(2)}) collective-permute-start(bf16[64,2048]{1,0:T(8,128)(2,1)} %get-tuple-element.49), channel_id=1, source_target_pairs={{0,4},{4,0},{8,12},{12,8},{1,5},{5,1},{9,13},{13,9},{2,6},{6,2},{1... | collective-permute-start | bytes 786440 | tf_op jit(solution)/shard_map/ppermute | solution.py:12
  195.1 31.9 %collective-permute-start.29 = (bf16[16,8192]{1,0:T(8,128)(2,1)}, bf16[16,8192]{1,0:T(8,128)(2,1)}, u32[]{:S(2)}, u32[]{:S(2)}) collective-permute-start(bf16[16,8192]{1,0:T(8,128)(2,1)} %get-tuple-element.10), channel_id=1, source_target_pairs={{0,1},{1,2},{2,3},{4,5},{5,6},{6,7},{8,9},{9,10},{10,11},{12,13},{... | collective-permute-start | bytes 786440 | tf_op jit(solution)/shard_map/ppermute | solution.py:38
  197.2 31.2 %collective-permute-start.28 = (bf16[16,8192]{1,0:T(8,128)(2,1)}, bf16[16,8192]{1,0:T(8,128)(2,1)}, u32[]{:S(2)}, u32[]{:S(2)}) collective-permute-start(bf16[16,8192]{1,0:T(8,128)(2,1)} %get-tuple-element.10), channel_id=1, source_target_pairs={{1,0},{2,1},{3,2},{5,4},{6,5},{7,6},{9,8},{10,9},{11,10},{13,12},{... | collective-permute-start | bytes 786440 | tf_op jit(solution)/shard_map/ppermute | solution.py:39
  220.5 11.4 %collective-permute-start.35 = (bf16[16,8192]{1,0:T(8,128)(2,1)S(1)}, bf16[16,8192]{1,0:T(8,128)(2,1)S(1)}, u32[]{:S(2)}, u32[]{:S(2)}) collective-permute-start(bf16[16,8192]{1,0:T(8,128)(2,1)S(1)} %copy-done.27), channel_id=1, source_target_pairs={{0,1},{1,2},{2,3},{4,5},{5,6},{6,7},{8,9},{9,10},{10,11},{12,13},{... | collective-permute-start | bytes 786440 | tf_op jit(solution)/shard_map/ppermute | solution.py:38
  227.0 11.4 %collective-permute-start.34 = (bf16[16,8192]{1,0:T(8,128)(2,1)S(1)}, bf16[16,8192]{1,0:T(8,128)(2,1)S(1)}, u32[]{:S(2)}, u32[]{:S(2)}) collective-permute-start(bf16[16,8192]{1,0:T(8,128)(2,1)S(1)} %copy-done.27), channel_id=1, source_target_pairs={{1,0},{2,1},{3,2},{5,4},{6,5},{7,6},{9,8},{10,9},{11,10},{13,12},{... | collective-permute-start | bytes 786440 | tf_op jit(solution)/shard_map/ppermute | solution.py:39
  228.4 11.2 %collective-permute-start.30 = (bf16[16,8192]{1,0:T(8,128)(2,1)}, bf16[16,8192]{1,0:T(8,128)(2,1)S(1)}, u32[]{:S(2)}, u32[]{:S(2)}) collective-permute-start(bf16[16,8192]{1,0:T(8,128)(2,1)} %collective-permute-done.29), channel_id=1, source_target_pairs={{1,2},{2,3},{5,6},{6,7},{9,10},{10,11},{13,14},{14,15},{17,18},{18... | collective-permute-start | bytes 786440 | tf_op jit(solution)/shard_map/ppermute | solution.py:38
  229.1 12.8 %collective-permute-start.32 = (bf16[16,8192]{1,0:T(8,128)(2,1)}, bf16[16,8192]{1,0:T(8,128)(2,1)S(1)}, u32[]{:S(2)}, u32[]{:S(2)}) collective-permute-start(bf16[16,8192]{1,0:T(8,128)(2,1)} %collective-permute-done.28), channel_id=1, source_target_pairs={{1,0},{2,1},{5,4},{6,5},{9,8},{10,9},{13,12},{14,13},{17,16},{18,1... | collective-permute-start | bytes 786440 | tf_op jit(solution)/shard_map/ppermute | solution.py:39
  231.9 11.3 %collective-permute-start.42 = (bf16[16,8192]{1,0:T(8,128)(2,1)S(1)}, bf16[16,8192]{1,0:T(8,128)(2,1)S(1)}, u32[]{:S(2)}, u32[]{:S(2)}) collective-permute-start(bf16[16,8192]{1,0:T(8,128)(2,1)S(1)} %copy-done.26), channel_id=1, source_target_pairs={{0,1},{1,2},{2,3},{4,5},{5,6},{6,7},{8,9},{9,10},{10,11},{12,13},{... | collective-permute-start | bytes 786440 | tf_op jit(solution)/shard_map/ppermute | solution.py:38
  238.4 10.9 %collective-permute-start.41 = (bf16[16,8192]{1,0:T(8,128)(2,1)S(1)}, bf16[16,8192]{1,0:T(8,128)(2,1)S(1)}, u32[]{:S(2)}, u32[]{:S(2)}) collective-permute-start(bf16[16,8192]{1,0:T(8,128)(2,1)S(1)} %copy-done.26), channel_id=1, source_target_pairs={{1,0},{2,1},{3,2},{5,4},{6,5},{7,6},{9,8},{10,9},{11,10},{13,12},{... | collective-permute-start | bytes 786440 | tf_op jit(solution)/shard_map/ppermute | solution.py:39
  239.7 10.6 %collective-permute-start.36 = (bf16[16,8192]{1,0:T(8,128)(2,1)S(1)}, bf16[16,8192]{1,0:T(8,128)(2,1)S(1)}, u32[]{:S(2)}, u32[]{:S(2)}) collective-permute-start(bf16[16,8192]{1,0:T(8,128)(2,1)S(1)} %collective-permute-done.35), channel_id=1, source_target_pairs={{1,2},{2,3},{5,6},{6,7},{9,10},{10,11},{13,14},{14,15},{17,18},{18... | collective-permute-start | bytes 786440 | tf_op jit(solution)/shard_map/ppermute | solution.py:38
  241.9 10.6 %collective-permute-start.38 = (bf16[16,8192]{1,0:T(8,128)(2,1)S(1)}, bf16[16,8192]{1,0:T(8,128)(2,1)S(1)}, u32[]{:S(2)}, u32[]{:S(2)}) collective-permute-start(bf16[16,8192]{1,0:T(8,128)(2,1)S(1)} %collective-permute-done.34), channel_id=1, source_target_pairs={{1,0},{2,1},{5,4},{6,5},{9,8},{10,9},{13,12},{14,13},{17,16},{18,1... | collective-permute-start | bytes 786440 | tf_op jit(solution)/shard_map/ppermute | solution.py:39
  243.3 25.7 %collective-permute-start.54 = (bf16[64,2048]{1,0:T(8,128)(2,1)S(1)}, bf16[64,2048]{1,0:T(8,128)(2,1)S(1)}, u32[]{:S(2)}, u32[]{:S(2)}) collective-permute-start(bf16[64,2048]{1,0:T(8,128)(2,1)S(1)} %copy-done.24), channel_id=1, source_target_pairs={{0,12},{4,8},{8,4},{12,0},{1,13},{5,9},{9,5},{13,1},{2,14},{6,10},... | collective-permute-start | bytes 786440 | tf_op jit(solution)/shard_map/ppermute | solution.py:12
  249.3 16.2 %collective-permute-start.52 = (bf16[64,2048]{1,0:T(8,128)(2,1)S(1)}, bf16[64,2048]{1,0:T(8,128)(2,1)S(1)}, u32[]{:S(2)}, u32[]{:S(2)}) collective-permute-start(bf16[64,2048]{1,0:T(8,128)(2,1)S(1)} %copy-done.25), channel_id=1, source_target_pairs={{0,8},{4,12},{8,0},{12,4},{1,9},{5,13},{9,1},{13,5},{2,10},{6,14},... | collective-permute-start | bytes 786440 | tf_op jit(solution)/shard_map/ppermute | solution.py:12
  252.5 9.7 %collective-permute-start.45 = (bf16[16,8192]{1,0:T(8,128)(2,1)S(1)}, bf16[16,8192]{1,0:T(8,128)(2,1)S(1)}, u32[]{:S(2)}, u32[]{:S(2)}) collective-permute-start(bf16[16,8192]{1,0:T(8,128)(2,1)S(1)} %collective-permute-done.41), channel_id=1, source_target_pairs={{1,0},{2,1},{5,4},{6,5},{9,8},{10,9},{13,12},{14,13},{17,16},{18,1... | collective-permute-start | bytes 786440 | tf_op jit(solution)/shard_map/ppermute | solution.py:39
  253.9 14.4 %collective-permute-start.53 = (bf16[128,2048]{1,0:T(8,128)(2,1)S(1)}, bf16[128,2048]{1,0:T(8,128)(2,1)S(1)}, u32[]{:S(2)}, u32[]{:S(2)}) collective-permute-start(bf16[128,2048]{1,0:T(8,128)(2,1)S(1)} %get-tuple-element.42), channel_id=1, source_target_pairs={{0,8},{4,12},{8,0},{12,4},{1,9},{5,13},{9,1},{13,5},{2,10},{6,14},... | collective-permute-start | bytes 1572872 | tf_op jit(solution)/shard_map/ppermute | solution.py:12
  264.2 44.8 %collective-permute-start.47 = (bf16[64,8192]{1,0:T(8,128)(2,1)S(1)}, bf16[64,8192]{1,0:T(8,128)(2,1)S(1)}, u32[]{:S(2)}, u32[]{:S(2)}) collective-permute-start(bf16[64,8192]{1,0:T(8,128)(2,1)S(1)} %pad_maximum_fusion.3), channel_id=1, source_target_pairs={{16,0},{17,1},{18,2},{19,3},{20,4},{21,5},{22,6},{23,7},{24,8},{25... | collective-permute-start | bytes 3145736 | tf_op jit(solution)/shard_map/ppermute | solution.py:180
  265.5 14.0 %collective-permute-start.55 = (bf16[128,2048]{1,0:T(8,128)(2,1)S(1)}, bf16[128,2048]{1,0:T(8,128)(2,1)S(1)}, u32[]{:S(2)}, u32[]{:S(2)}) collective-permute-start(bf16[128,2048]{1,0:T(8,128)(2,1)S(1)} %get-tuple-element.41), channel_id=1, source_target_pairs={{0,12},{4,8},{8,4},{12,0},{1,13},{5,9},{9,5},{13,1},{2,14},{6,10},... | collective-permute-start | bytes 1572872 | tf_op jit(solution)/shard_map/ppermute | solution.py:12
  268.3 23.7 %collective-permute-start.31 = (bf16[16,8192]{1,0:T(8,128)(2,1)S(1)}, bf16[16,8192]{1,0:T(8,128)(2,1)S(1)}, u32[]{:S(2)}, u32[]{:S(2)}) collective-permute-start(bf16[16,8192]{1,0:T(8,128)(2,1)S(1)} %collective-permute-done.30), channel_id=1, source_target_pairs={{2,3},{6,7},{10,11},{14,15},{18,19},{22,23},{26,27},{30,31}} | collective-permute-start | bytes 786440 | tf_op jit(solution)/shard_map/ppermute | solution.py:38
  269.0 25.3 %collective-permute-start.33 = (bf16[16,8192]{1,0:T(8,128)(2,1)S(1)}, bf16[16,8192]{1,0:T(8,128)(2,1)S(1)}, u32[]{:S(2)}, u32[]{:S(2)}) collective-permute-start(bf16[16,8192]{1,0:T(8,128)(2,1)S(1)} %collective-permute-done.32), channel_id=1, source_target_pairs={{1,0},{5,4},{9,8},{13,12},{17,16},{21,20},{25,24},{29,28}} | collective-permute-start | bytes 786440 | tf_op jit(solution)/shard_map/ppermute | solution.py:39
  279.5 15.6 %collective-permute-start.37 = (bf16[16,8192]{1,0:T(8,128)(2,1)S(1)}, bf16[16,8192]{1,0:T(8,128)(2,1)S(1)}, u32[]{:S(2)}, u32[]{:S(2)}) collective-permute-start(bf16[16,8192]{1,0:T(8,128)(2,1)S(1)} %collective-permute-done.36), channel_id=1, source_target_pairs={{2,3},{6,7},{10,11},{14,15},{18,19},{22,23},{26,27},{30,31}} | collective-permute-start | bytes 786440 | tf_op jit(solution)/shard_map/ppermute | solution.py:38
  292.0 11.3 %collective-permute-start.39 = (bf16[16,8192]{1,0:T(8,128)(2,1)S(1)}, bf16[16,8192]{1,0:T(8,128)(2,1)S(1)}, u32[]{:S(2)}, u32[]{:S(2)}) collective-permute-start(bf16[16,8192]{1,0:T(8,128)(2,1)S(1)} %collective-permute-done.38), channel_id=1, source_target_pairs={{1,0},{5,4},{9,8},{13,12},{17,16},{21,20},{25,24},{29,28}} | collective-permute-start | bytes 786440 | tf_op jit(solution)/shard_map/ppermute | solution.py:39
  294.3 10.5 %collective-permute-start.44 = (bf16[16,8192]{1,0:T(8,128)(2,1)S(1)}, bf16[16,8192]{1,0:T(8,128)(2,1)S(1)}, u32[]{:S(2)}, u32[]{:S(2)}) collective-permute-start(bf16[16,8192]{1,0:T(8,128)(2,1)S(1)} %collective-permute-done.43), channel_id=1, source_target_pairs={{2,3},{6,7},{10,11},{14,15},{18,19},{22,23},{26,27},{30,31}} | collective-permute-start | bytes 786440 | tf_op jit(solution)/shard_map/ppermute | solution.py:38
  295.1 13.9 %collective-permute-start.46 = (bf16[16,8192]{1,0:T(8,128)(2,1)S(1)}, bf16[16,8192]{1,0:T(8,128)(2,1)S(1)}, u32[]{:S(2)}, u32[]{:S(2)}) collective-permute-start(bf16[16,8192]{1,0:T(8,128)(2,1)S(1)} %collective-permute-done.45), channel_id=1, source_target_pairs={{1,0},{5,4},{9,8},{13,12},{17,16},{21,20},{25,24},{29,28}} | collective-permute-start | bytes 786440 | tf_op jit(solution)/shard_map/ppermute | solution.py:39
  (59 other events, 419.5 us)

commit v2 on v0

v2 whole, which is shorter than its diff:
```python
import functools

import jax
import jax.numpy as jnp
from jax import lax
from jax.experimental import pallas as pl
from jax.experimental.pallas import tpu as pltpu
from jax.sharding import PartitionSpec as P

F32 = jnp.float32
BF16 = jnp.bfloat16
SMALL = pl.CostEstimate(flops=0, bytes_accessed=0, transcendentals=0)
PARAMS = pltpu.CompilerParams(vmem_limit_bytes=56 * 1024 * 1024)


def partner(shard, axis, mask):
    length = lax.axis_size(axis)
    return lax.ppermute(shard, axis, [(i, i ^ mask) for i in range(length)])


def around(shard, axis, by):
    length = lax.axis_size(axis)
    return lax.ppermute(shard, axis, [(i, (i + by) % length) for i in range(length)])


def exchange_rows(block):
    length = lax.axis_size("tensor")
    if length == 4:
        return [block] + [partner(block, "tensor", r) for r in range(1, length)]
    return [block] + [around(block, "tensor", length - r) for r in range(1, length)]


def first_stage(block):
    if lax.axis_size("tensor") != 4:
        return exchange_rows(block)
    return [block, partner(block, "tensor", 1), partner(block, "tensor", 2)]


def second_stage(held, *before):
    if lax.axis_size("tensor") != 4:
        return held
    block, one, two = lax.optimization_barrier(tuple(held) + before)[:3]
    middle = lax.ppermute(block, "tensor", [(1, 2), (2, 1)])
    ends = lax.ppermute(two, "tensor", [(2, 3), (1, 0)])
    return [block, one, two, middle, ends]


def joined(held, *before):
    if len(held) == lax.axis_size("tensor"):
        return held
    block, one, two, middle, ends = held
    middle, ends = lax.optimization_barrier((middle, ends) + before)[:2]
    me = lax.axis_index("tensor")
    inside = (me == 1) | (me == 2)
    return [block, one, two, jnp.where(inside, middle, ends)]


def position(r):
    n = lax.axis_size("tensor")
    me = lax.axis_index("tensor")
    return me ^ r if n == 4 else (me + r) % n


def tied(value, *others):
    return lax.optimization_barrier((value,) + others)[0]


def chunks(width):
    step = min(width, 1024)
    return [slice(i, i + step) for i in range(0, width, step)]


def selected(routes_ref, count):
    ids = routes_ref[...]
    column = lax.broadcasted_iota(jnp.int32, (ids.shape[0], count), 1)
    return [(ids[:, k : k + 1] == column).astype(F32) for k in range(ids.shape[1])]


def probs_kernel(experts, hidden_ref, small_ref, routes_ref, probs_ref, inv_ref, marked_ref):
    width = hidden_ref.shape[1]
    square = jnp.zeros((hidden_ref.shape[0], 1), F32)
    for c in chunks(width):
        h = hidden_ref[:, c].astype(F32)
        square += jnp.sum(h * h, axis=1, keepdims=True)
    inv = 1.0 / jnp.sqrt(square / width + 1e-05)
    logits = jnp.zeros((hidden_ref.shape[0], small_ref.shape[0]), F32)
    for c in chunks(width):
        gain = small_ref[experts : experts + 1, c].astype(F32)
        normed = (hidden_ref[:, c].astype(F32) * inv * gain).astype(BF16)
        logits += lax.dot_general(
            normed, small_ref[:, c], (((1,), (1,)), ((), ())), preferred_element_type=F32
        )
    column = lax.broadcasted_iota(jnp.int32, logits.shape, 1)
    weights = jnp.where(column < experts, jnp.exp(jnp.where(column < experts, logits, 0.0)), 0.0)
    probs = weights / jnp.sum(weights, axis=1, keepdims=True)
    probs_ref[...] = probs
    inv_ref[...] = inv
    named = sum(selected(routes_ref, logits.shape[1]))
    marked_ref[...] = jnp.where(named > 0, probs, -1.0)


def step_kernel(experts, parts, kept, choose, flag_ref, *refs):
    refs = list(refs)
    up_ref = refs.pop(0)
    other_ref = refs.pop(0) if choose else None
    hidden_ref, out_ref, routes_ref, probs_ref, inv_ref, small_ref = refs[:6]
    back_refs, refs = refs[6 : 6 + parts], refs[6 + parts :]
    passed_ref, term_ref, norm_ref, upstream_ref = refs
    width = up_ref.shape[2]
    rows = up_ref.shape[1]
    cap = back_refs[0].shape[1]
    t = pl.program_id(0)

    @pl.when(t == 0)
    def _():
        term_ref[...] = jnp.zeros_like(term_ref)

    choice = selected(routes_ref.at[0], probs_ref.shape[2])
    named = sum(choice)
    row = lax.broadcasted_iota(jnp.int32, (rows, rows), 0)
    column = lax.broadcasted_iota(jnp.int32, (rows, rows), 1)
    place = jnp.dot(
        (column < row).astype(BF16), named.astype(BF16), preferred_element_type=F32
    )
    expert = lax.broadcasted_iota(jnp.int32, named.shape, 1)
    slot = lax.broadcasted_iota(jnp.int32, (rows, cap), 1).astype(F32)
    picks = []
    for i in range(parts):
        mine = expert == flag_ref[1 + i]
        is_named = jnp.sum(jnp.where(mine, named, 0.0), axis=1, keepdims=True)
        at = jnp.sum(jnp.where(mine, place, 0.0), axis=1, keepdims=True)
        picks.append(jnp.where((at == slot) & (is_named > 0), 1.0, 0.0))
    pick = jnp.concatenate(picks, axis=1).astype(BF16)

    score = [jnp.zeros((rows, 1), F32) for _ in choice]
    for c in chunks(width):
        up = up_ref[0, :, c].astype(F32)
        if choose:
            up = jnp.where(flag_ref[0] == 1, up, other_ref[0, :, c].astype(F32))
        upstream_ref[:, c] = up
        for k in range(len(choice)):
            out = out_ref[0, :, k * width + c.start : k * width + c.stop].astype(F32)
            score[k] += jnp.sum(up * out, axis=1, keepdims=True)
    prob_grad = sum(a * b for a, b in zip(score, choice))
    p = probs_ref[0]
    logit_grad = (p * (prob_grad - jnp.sum(p * prob_grad, axis=1, keepdims=True))).astype(BF16)
    inv = inv_ref[0]
    mean = jnp.zeros((rows, 1), F32)
    for c in chunks(width):
        norm = jnp.dot(logit_grad, small_ref[:, c], preferred_element_type=F32)
        back = jnp.concatenate([ref[0, :, c] for ref in back_refs], axis=0)
        norm += jnp.dot(pick, back, preferred_element_type=F32)
        norm_ref[:, c] = norm
        gain = small_ref[experts : experts + 1, c].astype(F32)
        mean += jnp.sum(norm * gain * hidden_ref[0, :, c].astype(F32), axis=1, keepdims=True)
    mean = mean / width
    for c in chunks(width):
        gain = small_ref[experts : experts + 1, c].astype(F32)
        h = hidden_ref[0, :, c].astype(F32)
        grad = inv * (norm_ref[:, c] * gain) - h * inv**3 * mean
        passed_ref[0, :, c] = (upstream_ref[:, c] + grad).astype(BF16)

    @pl.when(t < kept)
    def _():
        for c in chunks(width):
            gain = small_ref[experts : experts + 1, c].astype(F32)
            scaled = hidden_ref[0, :, c].astype(F32) * inv
            normed = (scaled * gain).astype(BF16)
            router = lax.dot_general(
                logit_grad, normed, (((0,), (0,)), ((), ())), preferred_element_type=F32
            )
            gains = jnp.sum(norm_ref[:, c] * scaled, axis=0, keepdims=True)
            line = lax.broadcasted_iota(jnp.int32, router.shape, 0)
            term_ref[:, c] += jnp.where(line == experts, gains, router)


def gate_kernel(order_ref, scan_ref, gate_ref, out_ref):
    for r in range(out_ref.shape[1]):
        gate = gate_ref[0, order_ref[r]].astype(F32)
        scan = scan_ref[0, order_ref[r]].astype(F32)
        out_ref[0, r] = (scan * gate * (1.0 / (1.0 + jnp.exp(-gate)))).astype(BF16)


def inner_kernel(n, order_ref, *refs):
    blocks = refs[: 2 * n]
    weight_ref, scan_ref, gate_ref, scan_out, gate_out, held = refs[2 * n :]
    rows = blocks[0].shape[1]
    group = n * rows

    @pl.when(pl.program_id(0) == 0)
    def _():
        for i, ref in enumerate(blocks):
            for t in range(ref.shape[0]):
                step = t if i < n else t + 1
                start = pl.multiple_of(step * group + order_ref[i % n] * rows, 16)
                held[pl.ds(start, rows), :] = ref[t]

    inner = lax.dot_general(
        held[...], weight_ref[...], (((1,), (1,)), ((), ())), preferred_element_type=F32
    )
    for t in range(scan_ref.shape[0]):
        part = inner[t * group : (t + 1) * group]
        gate = gate_ref[t].astype(F32)
        scan = scan_ref[t].astype(F32)
        sig = 1.0 / (1.0 + jnp.exp(-gate))
        scan_out[t] = (part * gate * sig).astype(BF16)
        gate_out[t] = (part * scan * sig * (1.0 + gate * (1.0 - sig))).astype(BF16)


def columns_kernel(n, *refs):
    blocks, out_ref = refs[:n], refs[-1]
    rows = blocks[0].shape[1]
    for t in range(blocks[0].shape[0]):
        for r, ref in enumerate(blocks):
            start = (t * n + r) * rows
            out_ref[0, start : start + rows, :] = ref[t]
    if len(refs) > n + 1:
        start = blocks[0].shape[0] * n * rows
        out_ref[0, start:, :] = (refs[n][...] + refs[n + 1][...]).astype(BF16)


def weight_kernel(order_ref, *refs):
    lefts, (first_ref, later_ref, out_ref, held) = refs[:-4], refs[-4:]
    groups, rows, _ = first_ref.shape
    depth = lefts[0].shape[0]

    @pl.when(pl.program_id(0) == 0)
    def _():
        for g in range(groups):
            start = pl.multiple_of(order_ref[g] * depth, 16)
            held[pl.ds(start, rows), :] = first_ref[g]
            start = pl.multiple_of(order_ref[g] * depth + rows, 16)
            held[pl.ds(start, depth - rows), :] = later_ref[g, : depth - rows, :]

    left = jnp.concatenate([ref[...] for ref in lefts], axis=0)
    out_ref[...] = lax.dot_general(
        left, held[...], (((0,), (0,)), ((), ())), preferred_element_type=F32
    )


def dispatch_kernel(n, order_ref, marks_ref, *refs):
    out_ref = refs[2 * n]
    _, rows, width = refs[0].shape
    cap = out_ref.shape[1] // n
    row = lax.broadcasted_iota(jnp.int32, (rows, rows), 0)
    column = lax.broadcasted_iota(jnp.int32, (rows, rows), 1)
    before = (row < column).astype(BF16)
    slot = lax.broadcasted_iota(jnp.int32, (cap, rows), 0).astype(F32)
    owner = lax.broadcasted_iota(jnp.int32, (n * cap, rows), 0) // cap
    puts, prob = [], 0.0
    for r in range(n):
        mark = marks_ref[0, r : r + 1, :]
        named = (mark >= 0).astype(F32)
        place = jnp.dot(named.astype(BF16), before, preferred_element_type=F32)
        put = jnp.where((slot == place) & (named > 0), 1.0, 0.0)
        put = jnp.where(owner == order_ref[r], jnp.concatenate([put] * n, axis=0), 0.0)
        prob += jnp.sum(put * mark, axis=1, keepdims=True)
        puts.append(put)
    put = jnp.concatenate(puts, axis=1).astype(BF16)

    def fill(sources):
        for c in chunks(width):
            source = jnp.concatenate([ref[0, :, c] for ref in sources], axis=0)
            moved = jnp.dot(put, source, preferred_element_type=F32)
            out_ref[0, :, c] = (prob * moved).astype(BF16)

    @pl.when(pl.program_id(0) == 0)
    def _():
        fill(refs[:n])

    @pl.when(pl.program_id(0) > 0)
    def _():
        fill(refs[n : 2 * n])


def whole_spec(array, extra=0):
    zeros = (0,) * array.ndim
    return pl.BlockSpec(array.shape, lambda *_: zeros, pipeline_mode=pl.Buffered(1))


def on_device(
    incoming, hidden, expert_out, routes, expert_back, scan_out, gate_in, w_out, w_router, norm_gain
):
    micro = incoming.shape[1]
    rows = incoming.shape[2]
    width = incoming.shape[3]
    experts = w_router.shape[2]
    n = lax.axis_size("tensor")
    n_dp = lax.axis_size("dp")
    cap = expert_back.shape[2] // n
    inner = scan_out.shape[3]
    group = scan_out.shape[2]
    columns = width // n_dp
    padded = -(-(experts + 1) // 16) * 16
    me = lax.axis_index("tensor")
    me_dp = lax.axis_index("dp")
    section = lax.axis_index("section")
    upper = section == 1
    order = jnp.stack([position(r) for r in range(n)]).astype(jnp.int32)
    weight = w_out[0]
    call = functools.partial(pl.pallas_call, compiler_params=PARAMS, cost_estimate=SMALL)

    back = expert_back[0].reshape(micro, n, cap, width)
    returned = [lax.dynamic_index_in_dim(back, me, 1, False)]
    for r in range(1, n):
        if n == 4:
            block = lax.dynamic_index_in_dim(back, me ^ r, 1, False)
            returned.append(partner(block, "tensor", r))
        else:
            block = lax.dynamic_index_in_dim(back, (me + n - r) % n, 1, False)
            returned.append(around(block, "tensor", n - r))

    small = jnp.concatenate([w_router[0].T, norm_gain[0][None]], axis=0)
    smalls = lax.all_gather(small, "dp", axis=1, tiled=True)
    smalls = jnp.pad(smalls, ((0, padded - experts - 1), (0, 0)))

    probs, inv_rms, marked = call(
        functools.partial(probs_kernel, experts),
        out_shape=(
            jax.ShapeDtypeStruct((micro * rows, padded), F32),
            jax.ShapeDtypeStruct((micro * rows, 1), F32),
            jax.ShapeDtypeStruct((micro * rows, padded), F32),
        ),
        name="probs",
    )(hidden[0].reshape(micro * rows, width), smalls, routes[0].reshape(micro * rows, -1))
    probs = probs.reshape(micro, rows, padded)
    inv_rms = inv_rms.reshape(micro, rows, 1)
    out_rows = expert_out[0].reshape(micro, rows, -1)
    flag = jnp.concatenate([section.astype(jnp.int32)[None], order])

    def step_back(t0, t1, kept, upstream, other=None):
        count = t1 - t0
        shifted = [hidden[0], out_rows, routes[0], probs, inv_rms]
        arrays, shift = [upstream], [t0]
        if other is not None:
            arrays, shift = arrays + [other], shift + [0]
        arrays, shift = arrays + shifted, shift + [t0] * len(shifted)
        specs = []
        for a, s in zip(arrays, shift):
            rest = (0,) * (a.ndim - 1)
            specs.append(
                pl.BlockSpec((1,) + a.shape[1:], lambda t, s=s, rest=rest: (t + s,) + rest)
            )
        arrays.append(smalls)
        specs.append(whole_spec(smalls))
        for a in returned:
            specs.append(pl.BlockSpec((1,) + a.shape[1:], lambda t: (t + t0, 0, 0)))
            arrays.append(a)
        return call(
            functools.partial(step_kernel, experts, len(returned), kept, other is not None),
            grid=(count,),
            out_shape=(
                jax.ShapeDtypeStruct((count, rows, width), BF16),
                jax.ShapeDtypeStruct((padded, width), F32),
            ),
            in_specs=[pl.BlockSpec(memory_space=pltpu.SMEM)] + specs,
            out_specs=(
                pl.BlockSpec((1, rows, width), lambda t: (t, 0, 0)),
                pl.BlockSpec((padded, width), lambda t: (0, 0)),
            ),
            scratch_shapes=[pltpu.VMEM((rows, width), F32)] * 2,
            name="step",
        )(flag, *arrays)

    def columns_over(blocks, terms=()):
        count = blocks[0].shape[0]
        high = count * group + (padded if terms else 0)
        split = call(
            functools.partial(columns_kernel, n),
            grid=(n_dp,),
            out_shape=jax.ShapeDtypeStruct((n_dp, high, columns), BF16),
            in_specs=[pl.BlockSpec((count, rows, columns), lambda g: (0, 0, g))] * n
            + [pl.BlockSpec((padded, columns), lambda g: (0, g))] * len(terms),
            out_specs=pl.BlockSpec((1, high, columns), lambda g: (g, 0, 0)),
            name="columns",
        )(*blocks, *terms)
        return lax.all_to_all(split, "dp", split_axis=0, concat_axis=0, tiled=True)

    first, term_first = step_back(0, micro - 1, 1, incoming[0])
    received = lax.ppermute(first, "section", [(1, 0)])
    near_rows = exchange_rows(first[:1])

    four = (micro, n, rows, inner)
    spec = pl.BlockSpec((1, n, rows, inner), lambda t, o: (t, 0, 0, 0))
    gated = call(
        gate_kernel,
        out_shape=jax.ShapeDtypeStruct(four, BF16),
        grid_spec=pltpu.PrefetchScalarGridSpec(
            num_scalar_prefetch=1, grid=(micro,), in_specs=[spec] * 2, out_specs=spec
        ),
        name="gate",
    )(order, tied(scan_out[0].reshape(four), first), gate_in[0].reshape(four))
    gated = gated.reshape(micro * group, inner)
    if n_dp == 4:
        across = partner(gated, "dp", 2)
        lefts = [gated, partner(gated, "dp", 1), across, partner(across, "dp", 1)]
    else:
        lefts = [gated] + [partner(gated, "dp", m) for m in range(1, n_dp)]


    later, term_later = step_back(
        1, micro, micro, incoming[0], received
    )
    passed_all = jnp.concatenate([first[:1], later], axis=0)
    far_half = first_stage(tied(later, *near_rows[1:]))
    far_rows = joined(second_stage(far_half, *lefts))
    across_first = columns_over([tied(near_rows[0], *far_half[1:])] + near_rows[1:])
    upstream = jnp.where(upper, incoming[0, 1:], received)
    source_first = joined(second_stage(first_stage(tied(incoming[0, :1], *far_half[1:]))))
    source_half = first_stage(tied(upstream, *source_first[1:]))
    rights = [across_first, columns_over(
        [tied(far_rows[0], across_first)] + far_rows[1:], (term_first, term_later)
    )]

    tile = min(inner, 256)
    blocks = near_rows + far_rows
    rows_spec = pl.BlockSpec((micro, group, tile), lambda i, o: (0, 0, i))
    scan_grad, gate_grad = call(
        functools.partial(inner_kernel, n),
        out_shape=[jax.ShapeDtypeStruct((micro, group, inner), BF16)] * 2,
        grid_spec=pltpu.PrefetchScalarGridSpec(
            num_scalar_prefetch=1,
            grid=(inner // tile,),
            in_specs=[whole_spec(b) for b in blocks]
            + [pl.BlockSpec((tile, width), lambda i, o: (i, 0))]
            + [rows_spec] * 2,
            out_specs=[rows_spec] * 2,
            scratch_shapes=[pltpu.VMEM((micro * group, width), BF16)],
        ),
        name="project",
    )(order, *blocks, weight, scan_out[0], gate_in[0])

    source_later = second_stage(source_half, scan_grad)
    depth = lefts[0].shape[0]
    order_dp = me_dp ^ jnp.arange(n_dp, dtype=jnp.int32)
    weight_grad = call(
        weight_kernel,
        out_shape=jax.ShapeDtypeStruct((inner, columns), F32),
        grid_spec=pltpu.PrefetchScalarGridSpec(
            num_scalar_prefetch=1,
            grid=(inner // tile,),
            in_specs=[pl.BlockSpec((depth, tile), lambda i, o: (0, i))] * n_dp
            + [whole_spec(x) for x in rights],
            out_specs=pl.BlockSpec((tile, columns), lambda i, o: (i, 0)),
            scratch_shapes=[pltpu.VMEM((n_dp * depth, columns), BF16)],
        ),
        name="weight_grad",
    )(order_dp, *lefts, *rights)

    source_later = joined(source_later, weight_grad)
    total = jnp.sum(tied(rights[1], scan_grad)[:, -padded:].astype(F32), axis=0)[: experts + 1]
    marks = marked[:, :experts].T.reshape(1, -1)
    marks = jnp.pad(marks, ((0, 0), (0, -marks.shape[1] % columns))).reshape(-1, columns)
    if n == 4:
        both = partner(jnp.concatenate([total, marks], axis=0), "tensor", 1)
        total = total + both[: experts + 1]
        marks = jnp.concatenate([marks, both[experts + 1 :]], axis=0)
        both = partner(jnp.concatenate([total, marks], axis=0), "tensor", 2)
        total = total + both[: experts + 1]
        marks = jnp.concatenate([marks, both[experts + 1 :]], axis=0)
    else:
        shared = exchange_rows(jnp.concatenate([total, marks], axis=0))
        total = sum(x[: experts + 1] for x in shared)
        marks = jnp.concatenate([x[experts + 1 :] for x in shared], axis=0)
    marks = marks.reshape(n, -1)[:, : experts * micro * rows].reshape(n, experts, micro, rows)
    mine = jnp.swapaxes(lax.dynamic_index_in_dim(marks, me, 1, False), 0, 1)

    expert_grad = call(
        functools.partial(dispatch_kernel, n),
        out_shape=jax.ShapeDtypeStruct((micro, n * cap, width), BF16),
        grid_spec=pltpu.PrefetchScalarGridSpec(
            num_scalar_prefetch=1,
            grid=(micro,),
            in_specs=[pl.BlockSpec((1, n, rows), lambda t, o: (t, 0, 0))]
            + [whole_spec(x) for x in source_first]
            + [pl.BlockSpec((1, rows, width), lambda t, o: (jnp.maximum(t - 1, 0), 0, 0))] * n,
            out_specs=pl.BlockSpec((1, n * cap, width), lambda t, o: (t, 0, 0)),
        ),
        name="dispatch",
    )(order, mine, *source_first, *source_later)

    return (
        passed_all[None],
        scan_grad[None],
        gate_grad[None],
        expert_grad[None],
        weight_grad[None],
        total[:experts].T[None],
        total[experts][None],
    )


def solution(mesh):
    placed = (
        P("section", None, ("dp", "tensor"), None),
        P("section", None, ("dp", "tensor"), None),
        P("section", None, ("dp", "tensor"), None, None),
        P("section", None, ("dp", "tensor"), None),
        P("section", None, ("dp", "tensor"), None),
        P("section", None, "dp", "tensor"),
        P("section", None, "dp", "tensor"),
        P("section", "tensor", None),
        P("section", "dp", None),
        P("section", "dp"),
    )
    return jax.shard_map(
        on_device,
        mesh=mesh,
        in_specs=placed,
        out_specs=(
            P("section", None, ("dp", "tensor"), None),
            P("section", None, "dp", "tensor"),
            P("section", None, "dp", "tensor"),
            P("section", None, ("dp", "tensor"), None),
            P("section", "tensor", "dp"),
            P("section", "dp", None),
            P("section", "dp"),
        ),
        check_vma=False,
    )
```

time: 508 us -> 251 us (0.49)
  matrix products: 175 us -> 0 us
  waiting for transfers between devices: 167 us -> 90 us
  Pallas kernels: 0 us -> 66.4 us
  other arithmetic: 48.6 us -> 9.73 us
  blocking collectives: 40.4 us -> 5.43 us
  starting transfers between devices: 27.9 us -> 60 us
  between operations: 16.9 us -> 0.98 us
  local copies, waits for them, and re-layouts: 26.2 us -> 16.6 us
    dot_general x18 -> x0, matrix products: 175 us -> none  [the longest x3 105 us: on_device(): lax.dot_general(gated, shard_rows, (((0,), (0,)), ((), ())), preferred_el...]
    reduce_scatter x1 -> x0, waiting for transfers between devices: 102 us -> none  [on_device(): lax.psum_scatter(grad_acc.astype(jnp.bfloat16), 'dp', scatter_dimension=1...]
    ppermute x2 -> x24, waiting for transfers between devices: 6.57 us -> 88.6 us  [the longest x17 75.5 us: partner(): return lax.ppermute(shard, axis, [(i, i ^ mask) for i in range(length)])]
    pallas_call x0 -> x9, Pallas kernels: none -> 66.4 us  [the longest x1 21.2 us: on_device(): call(functools.partial(inner_kernel, n), out_shape=[jax.ShapeDtypeStruct(...]
    all_to_all x6 -> x2, waiting for transfers between devices: 59.2 us -> 1.38 us  [columns_over(): return lax.all_to_all(split, 'dp', split_axis=0, concat_axis=0, tiled=True)]
    ppermute x2 -> x24, starting transfers between devices: 2.58 us -> 52.8 us  [the longest x17 44.1 us: partner(): return lax.ppermute(shard, axis, [(i, i ^ mask) for i in range(length)])]
    broadcast_in_dim x6 -> x1, other arithmetic: 20.9 us -> 0.95 us  [on_device(): passed_all[None]]
    psum x1 -> x0, blocking collectives: 19.1 us -> none  [on_device(): lax.psum(router_acc.astype(jnp.bfloat16), 'tensor').astype(jnp.float32)]
  transfers between devices with their start and end apart: 13 -> 26, of which waited for: 7 -> 11; matrix products, arithmetic and copies ran while one was open for 47% -> 7% of each run, Pallas kernels for 0% -> 19%
where the time goes in v2:
time: 251 us; the launch traced here: 249 us
  waiting for transfers between devices  90 us (36%)
  Pallas kernels  66.4 us (26%)
  starting transfers between devices  60 us (24%)
  local copies, waits for them, and re-layouts  16.6 us (7%)
  other arithmetic  9.73 us (4%)
  blocking collectives  5.43 us (2%)
    ppermute x17, waiting for transfers between devices, partner(): return lax.ppermute(shard, axis, [(i, i ^ mask) for i in range(length)])  75.5 us
    ppermute x17, starting transfers between devices, partner(): return lax.ppermute(shard, axis, [(i, i ^ mask) for i in range(length)])  44.1 us
    pallas_call x1, Pallas kernels, on_device(): call(functools.partial(inner_kernel, n), out_shape=[jax.ShapeDtypeStruct(...  21.2 us
    pallas_call x1, Pallas kernels, on_device(): call(weight_kernel, out_shape=jax.ShapeDtypeStruct((inner, columns), F32)...  14.4 us
    ppermute x3, waiting for transfers between devices, second_stage(): ends = lax.ppermute(two, 'tensor', [(2, 3), (1, 0)])  13.1 us
    pallas_call x2, Pallas kernels, step_back(): call(functools.partial(step_kernel, experts, len(returned), kept, other i...  10.7 us
    pallas_call x2, Pallas kernels, columns_over(): call(functools.partial(columns_kernel, n), grid=(n_dp,), out_shape=jax.Sh...  7.45 us
    all_to_all x2, starting transfers between devices, columns_over(): return lax.all_to_all(split, 'dp', split_axis=0, concat_axis=0, tiled=True)  7.16 us
  transfers between devices with their start and end apart: 26, of which 11 were waited for; matrix products, arithmetic and copies ran while one was open for 7% of the time, Pallas kernels for 19%

profile of v2, /device:TPU:0, one launch (start us, length us, event | category | flops | bytes accessed | tf_op | source)
XLA Modules:
  0.0 249.1 jit_solution(1212546422403348892)
XLA Ops:
  0.7 3.3 %dynamic-slice_bitcast_fusion = (bf16[3,16,8192]{2,1,0:T(8,128)(2,1)S(1)}, bf16[3,16,8192]{2,1,0:T(8,128)(2,1)}, bf16[3,16,8192]{2,1,0:T(8,128)(2,1)}, bf16[3,16,8192]{2,1,0:T(8,128)(2,1)}) fusion(bf16[3,4,16,8192]{3,2,1,0:T(8,128)(2,1)} %bitcast.69, s32[]{:T(128)S(6)} %select_n.44, s32[]{:T(128)S(6)} %select_n.43, s32[]{:T(128)S(6)} %select_n.42, ...), kind=kLoop, calls=%fused_computation.1 | loop fusion | bytes 6291472 | tf_op jit(solution)/shard_map/jit(dynamic_index_in_dim)/squeeze | solution.py:307
  4.0 3.0 %collective-permute-start = (bf16[3,16,8192]{2,1,0:T(8,128)(2,1)}, bf16[3,16,8192]{2,1,0:T(8,128)(2,1)S(1)}, u32[]{:S(2)}, u32[]{:S(2)}) collective-permute-start(bf16[3,16,8192]{2,1,0:T(8,128)(2,1)} %get-tuple-element.71), channel_id=1, source_target_pairs={{0,1},{1,0},{2,3},{3,2},{4,5},{5,4},{6,7},{7,6},{8,9},{9,8},{10,11... | collective-permute-start | bytes 2359304 | tf_op jit(solution)/shard_map/ppermute | solution.py:18
  7.0 2.6 %collective-permute-start.1 = (bf16[3,16,8192]{2,1,0:T(8,128)(2,1)}, bf16[3,16,8192]{2,1,0:T(8,128)(2,1)S(1)}, u32[]{:S(2)}, u32[]{:S(2)}) collective-permute-start(bf16[3,16,8192]{2,1,0:T(8,128)(2,1)} %get-tuple-element.70), channel_id=1, source_target_pairs={{0,2},{1,3},{2,0},{3,1},{4,6},{5,7},{6,4},{7,5},{8,10},{9,11},{10,... | collective-permute-start | bytes 2359304 | tf_op jit(solution)/shard_map/ppermute | solution.py:18
  10.3 3.9 %reshape_squeeze.18.refs_2_.refs_3_ = bf16[3,16,16384]{2,1,0:T(8,128)(2,1)} reshape(bf16[1,3,16,2,8192]{4,3,2,1,0:T(2,128)(2,1)} %param.12) | data formatting | bytes 3145728 | tf_op jit(solution)/shard_map/reshape;squeeze | solution.py:328
  15.0 5.4 %all_gather.3 = bf16[5,8192]{1,0:T(8,128)(2,1)S(1)} all-gather(bf16[5,2048]{1,0:T(8,128)(2,1)S(1)} %pad_maximum_fusion.2), channel_id=1, replica_groups=mesh['section'=2,'dp'=4,'tensor'=4] {'dp'}, dimensions={1}, use_global_device_ids=true | all-gather | bytes 102400 | tf_op jit(solution)/shard_map/all_gather | solution.py:314
  21.1 2.5 %probs.1 = (f32[48,16]{1,0:T(8,128)}, f32[48,1]{1,0:T(8,128)}, f32[48,16]{1,0:T(8,128)}) custom-call(bf16[48,8192]{1,0:T(8,128)(2,1)} %bitcast.61, bf16[16,8192]{1,0:T(8,128)(2,1)} %pad.8.small_ref.refs_6_.refs_7_, s32[48,2]{1,0:T(8,128)} %bitcast.75), custom_call_target="tpu_custom_call" | custom-call | tf_op jit(solution)/shard_map/probs/pallas_call | solution.py:317
  25.0 15.8 %collective-permute-done.refs_8_.refs_9_ = bf16[3,16,8192]{2,1,0:T(8,128)(2,1)S(1)} collective-permute-done((bf16[3,16,8192]{2,1,0:T(8,128)(2,1)}, bf16[3,16,8192]{2,1,0:T(8,128)(2,1)S(1)}, u32[]{:S(2)}, u32[]{:S(2)}) %collective-permute-start) | collective-permute-done | bytes 786464 | tf_op jit(solution)/shard_map/ppermute | solution.py:18
  40.8 21.4 %collective-permute-done.1.refs_9_.refs_10_ = bf16[3,16,8192]{2,1,0:T(8,128)(2,1)S(1)} collective-permute-done((bf16[3,16,8192]{2,1,0:T(8,128)(2,1)}, bf16[3,16,8192]{2,1,0:T(8,128)(2,1)S(1)}, u32[]{:S(2)}, u32[]{:S(2)}) %collective-permute-start.1) | collective-permute-done | bytes 786464 | tf_op jit(solution)/shard_map/ppermute | solution.py:18
  63.4 5.0 %step.2 = (bf16[2,16,8192]{2,1,0:T(8,128)(2,1)}, f32[16,8192]{1,0:T(8,128)}) custom-call(s32[5]{0:T(128)} %concatenate.22.flag_ref, bf16[3,16,8192]{2,1,0:T(8,128)(2,1)} %bitcast.64, bf16[3,16,8192]{2,1,0:T(8,128)(2,1)} %bitcast.62, bf16[3,16,16384]{2,1,0:T(8,128)(2,1)} %reshape_squeeze.18.refs_2_.refs_3_, s32[3,16,2]{2,1,0:T(8,128)} %copy.34.refs_3_.refs_4_, ...), custom_call_target="tpu_custom_call" | custom-call | tf_op jit(solution)/shard_map/step/pallas_call | solution.py:349
  68.5 4.0 %gate.1 = bf16[3,4,16,2048]{3,2,1,0:T(8,128)(2,1)} custom-call(s32[4]{0:T(128)} %pad_add_fusion.order_ref, bf16[3,4,16,2048]{3,2,1,0:T(8,128)(2,1)} %bitcast.71, bf16[3,4,16,2048]{3,2,1,0:T(8,128)(2,1)} %bitcast.73), custom_call_target="tpu_custom_call" | custom-call | tf_op jit(solution)/shard_map/gate/pallas_call | solution.py:385
  72.4 1.5 collective-permute-start.10
  74.0 1.3 collective-permute-start.3
  75.3 1.0 slice.40.refs_0_
  76.2 15.8 %collective-permute-start.4 = (bf16[1,16,8192]{2,1,0:T(8,128)(2,1)S(1)}, bf16[1,16,8192]{2,1,0:T(8,128)(2,1)S(1)}, u32[]{:S(2)}, u32[]{:S(2)}) collective-permute-start(bf16[1,16,8192]{2,1,0:T(8,128)(2,1)S(1)} %slice.40.refs_0_), channel_id=1, source_target_pairs={{0,1},{1,0},{2,3},{3,2},{4,5},{5,4},{6,7},{7,6},{8,9},{9,8},{10,11... | collective-permute-start | bytes 786440 | tf_op jit(solution)/shard_map/ppermute | solution.py:18
  92.0 1.1 collective-permute-start.5
  93.1 1.4 collective-permute-start.6
  95.3 5.7 %step.3 = (bf16[2,16,8192]{2,1,0:T(8,128)(2,1)}, f32[16,8192]{1,0:T(8,128)}) custom-call(s32[5]{0:T(128)} %concatenate.22.flag_ref, bf16[3,16,8192]{2,1,0:T(8,128)(2,1)} %bitcast.65, bf16[2,16,8192]{2,1,0:T(8,128)(2,1)} %copy-done.12, bf16[3,16,8192]{2,1,0:T(8,128)(2,1)} %bitcast.63, bf16[3,16,16384]{2,1,0:T(8,128)(2,1)} %reshape_squeeze.18.refs_2_.refs_3_, ...), custom_call_target="tpu_custom_call" | custom-call | tf_op jit(solution)/shard_map/step/pallas_call | solution.py:349
  101.0 12.4 %collective-permute-done.5.refs_2_ = bf16[1,16,8192]{2,1,0:T(8,128)(2,1)S(1)} collective-permute-done((bf16[1,16,8192]{2,1,0:T(8,128)(2,1)S(1)}, bf16[1,16,8192]{2,1,0:T(8,128)(2,1)S(1)}, u32[]{:S(2)}, u32[]{:S(2)}) %collective-permute-start.5) | collective-permute-done | bytes 262176 | tf_op jit(solution)/shard_map/ppermute | solution.py:18
  113.4 3.4 %collective-permute-start.7 = (bf16[2,16,8192]{2,1,0:T(8,128)(2,1)}, bf16[2,16,8192]{2,1,0:T(8,128)(2,1)S(1)}, u32[]{:S(2)}, u32[]{:S(2)}) collective-permute-start(bf16[2,16,8192]{2,1,0:T(8,128)(2,1)} %get-tuple-element.53.refs_4_.refs_0_), channel_id=1, source_target_pairs={{0,1},{1,0},{2,3},{3,2},{4,5},{5,4},{6,7},{7,6},{8,9},{9,8},{10,11... | collective-permute-start | bytes 1572872 | tf_op jit(solution)/shard_map/ppermute | solution.py:18
  116.8 1.0 collective-permute-start.8
  118.5 18.8 %collective-permute-done.7.refs_5_.refs_1_ = bf16[2,16,8192]{2,1,0:T(8,128)(2,1)S(1)} collective-permute-done((bf16[2,16,8192]{2,1,0:T(8,128)(2,1)}, bf16[2,16,8192]{2,1,0:T(8,128)(2,1)S(1)}, u32[]{:S(2)}, u32[]{:S(2)}) %collective-permute-start.7) | collective-permute-done | bytes 524320 | tf_op jit(solution)/shard_map/ppermute | solution.py:18
  137.3 5.5 %collective-permute-start.16 = (bf16[1,16,8192]{2,1,0:T(8,128)(2,1)}, bf16[1,16,8192]{2,1,0:T(8,128)(2,1)}, u32[]{:S(2)}, u32[]{:S(2)}) collective-permute-start(bf16[1,16,8192]{2,1,0:T(8,128)(2,1)} %slice_bitcast_fusion.refs_0_), channel_id=1, source_target_pairs={{0,1},{1,0},{2,3},{3,2},{4,5},{5,4},{6,7},{7,6},{8,9},{9,8},{10,11... | collective-permute-start | bytes 786440 | tf_op jit(solution)/shard_map/ppermute | solution.py:18
  142.8 2.6 %collective-permute-start.17 = (bf16[1,16,8192]{2,1,0:T(8,128)(2,1)}, bf16[1,16,8192]{2,1,0:T(8,128)(2,1)}, u32[]{:S(2)}, u32[]{:S(2)}) collective-permute-start(bf16[1,16,8192]{2,1,0:T(8,128)(2,1)} %slice_bitcast_fusion.refs_0_), channel_id=1, source_target_pairs={{0,2},{1,3},{2,0},{3,1},{4,6},{5,7},{6,4},{7,5},{8,10},{9,11},{10,... | collective-permute-start | bytes 786440 | tf_op jit(solution)/shard_map/ppermute | solution.py:18
  145.4 3.4 %columns.2 = bf16[4,64,2048]{2,1,0:T(8,128)(2,1)} custom-call(bf16[1,16,8192]{2,1,0:T(8,128)(2,1)} %copy-done.4, bf16[1,16,8192]{2,1,0:T(8,128)(2,1)} %copy-done.13, bf16[1,16,8192]{2,1,0:T(8,128)(2,1)} %copy-done.14, bf16[1,16,8192]{2,1,0:T(8,128)(2,1)} %copy-done.15), custom_call_target="tpu_custom_call" | custom-call | tf_op jit(solution)/shard_map/columns/pallas_call | solution.py:368
  148.7 3.5 %all-to-all-start = ((bf16[4,64,2048]{2,1,0:T(8,128)(2,1)}), bf16[4,64,2048]{2,1,0:T(8,128)(2,1)S(1)}, u32[]{:S(2)}, u32[]{:S(2)}) async-start(bf16[4,64,2048]{2,1,0:T(8,128)(2,1)} %columns.2), calls=%async_computation | async-start | bytes 2097152 | tf_op jit(solution)/shard_map/all_to_all | solution.py:377
  152.2 0.9 collective-permute-done.17.refs_2_
  153.8 1.3 collective-permute-start.19
  155.2 1.5 collective-permute-start.12
  156.6 1.3 collective-permute-start.13
  157.9 1.9 bitcast_select_fusion.refs_4_
  160.6 4.7 %collective-permute-done.19 = bf16[1,16,8192]{2,1,0:T(8,128)(2,1)} collective-permute-done((bf16[1,16,8192]{2,1,0:T(8,128)(2,1)}, bf16[1,16,8192]{2,1,0:T(8,128)(2,1)}, u32[]{:S(2)}, u32[]{:S(2)}) %collective-permute-start.19) | collective-permute-done | bytes 262176 | tf_op jit(solution)/shard_map/ppermute | solution.py:44
  165.3 1.4 all-to-all-done.refs_4_
  166.7 8.4 %collective-permute-done.13 = bf16[2,16,8192]{2,1,0:T(8,128)(2,1)} collective-permute-done((bf16[2,16,8192]{2,1,0:T(8,128)(2,1)S(1)}, bf16[2,16,8192]{2,1,0:T(8,128)(2,1)}, u32[]{:S(2)}, u32[]{:S(2)}) %collective-permute-start.13) | collective-permute-done | bytes 524320 | tf_op jit(solution)/shard_map/ppermute | solution.py:44
  175.0 1.9 broadcast_select_fusion.1.refs_7_.refs_3_
  176.9 4.1 %columns.3 = bf16[4,144,2048]{2,1,0:T(8,128)(2,1)} custom-call(bf16[2,16,8192]{2,1,0:T(8,128)(2,1)} %get-tuple-element.53.refs_4_.refs_0_, bf16[2,16,8192]{2,1,0:T(8,128)(2,1)} %copy-done.10, bf16[2,16,8192]{2,1,0:T(8,128)(2,1)} %copy-done.11, bf16[2,16,8192]{2,1,0:T(8,128)(2,1)} %broadcast_select_fusion.1.refs_7_.refs_3_, ...), custom_call_target="tpu_custom_call" | custom-call | tf_op jit(solution)/shard_map/columns/pallas_call | solution.py:368
  181.0 3.6 %all-to-all-start.1 = ((bf16[4,144,2048]{2,1,0:T(8,128)(2,1)}), bf16[4,144,2048]{2,1,0:T(8,128)(2,1)S(1)}, u32[]{:S(2)}, u32[]{:S(2)}) async-start(bf16[4,144,2048]{2,1,0:T(8,128)(2,1)} %columns.3), calls=%async_computation.1 | async-start | bytes 4718592 | tf_op jit(solution)/shard_map/all_to_all | solution.py:377
  184.7 1.7 broadcast_select_fusion.2.refs_3_
  186.4 2.1 collective-permute-start.21
  189.2 21.2 %project.1 = (bf16[3,64,2048]{2,1,0:T(8,128)(2,1)}, bf16[3,64,2048]{2,1,0:T(8,128)(2,1)}) custom-call(s32[4]{0:T(128)} %pad_add_fusion.order_ref, bf16[1,16,8192]{2,1,0:T(8,128)(2,1)} %copy-done.4, bf16[1,16,8192]{2,1,0:T(8,128)(2,1)} %copy-done.13, bf16[1,16,8192]{2,1,0:T(8,128)(2,1)} %copy-done.14, bf16[1,16,8192]{2,1,0:T(8,128)(2,1)} %copy-done.15, ...), custom_call_target="tpu_custom_call" | custom-call | tf_op jit(solution)/shard_map/project/pallas_call | solution.py:418
  211.2 2.0 collective-permute-done.21.refs_6_
  213.2 1.4 collective-permute-start.22
  214.7 1.3 collective-permute-start.23
  216.1 3.5 %collective-permute-start.14 = (f32[6,2048]{1,0:T(8,128)S(1)}, f32[6,2048]{1,0:T(8,128)S(1)}, u32[]{:S(2)}, u32[]{:S(2)}) collective-permute-start(f32[6,2048]{1,0:T(8,128)S(1)} %pad_maximum_fusion), channel_id=1, source_target_pairs={{0,1},{1,0},{2,3},{3,2},{4,5},{5,4},{6,7},{7,6},{8,9},{9,8},{10,11... | collective-permute-start | bytes 147464 | tf_op jit(solution)/shard_map/ppermute | solution.py:18
  219.6 0.9 maximum_bitcast_fusion
  220.5 14.4 %weight_grad.1 = f32[2048,2048]{1,0:T(8,128)} custom-call(s32[4]{0:T(128)} %iota_xor_fusion.order_ref, bf16[192,2048]{1,0:T(8,128)(2,1)} %bitcast.68, bf16[192,2048]{1,0:T(8,128)(2,1)} %collective-permute-done.9.refs_1_, bf16[192,2048]{1,0:T(8,128)(2,1)} %collective-permute-done.10.refs_2_, bf16[192,2048]{1,0:T(8,128)(2,1)} %collective-permute-done.11.refs_3_, ...), custom_call_target="tpu_custom_call" | custom-call | tf_op jit(solution)/shard_map/weight_grad/pallas_call | solution.py:436
  235.7 1.9 broadcast_select_fusion.refs_7_
  237.6 3.3 %collective-permute-done.15 = f32[7,2048]{1,0:T(8,128)S(1)} collective-permute-done((f32[7,2048]{1,0:T(8,128)S(1)}, f32[7,2048]{1,0:T(8,128)S(1)}, u32[]{:S(2)}, u32[]{:S(2)}) %collective-permute-start.15) | collective-permute-done | bytes 57376 | tf_op jit(solution)/shard_map/ppermute | solution.py:18
  242.9 6.2 %dispatch.1 = bf16[3,64,8192]{2,1,0:T(8,128)(2,1)} custom-call(s32[4]{0:T(128)} %pad_add_fusion.order_ref, f32[3,4,16]{2,1,0:T(4,128)} %bitcast.80, bf16[1,16,8192]{2,1,0:T(8,128)(2,1)} %slice_bitcast_fusion.refs_0_, bf16[1,16,8192]{2,1,0:T(8,128)(2,1)} %collective-permute-done.16.refs_1_, bf16[1,16,8192]{2,1,0:T(8,128)(2,1)} %collective-permute-done.17.refs_2_, ...), custom_call_target="tpu_custom_call" | custom-call | tf_op jit(solution)/shard_map/dispatch/pallas_call | solution.py:468
  (90 shorter events, 11.9 us)
Async XLA Ops:
  0.7 8.9 %copy-start.19 = (s32[1,3,16,2]{2,3,1,0:T(2,128)S(1)}, s32[1,3,16,2]{2,3,1,0:T(2,128)}, u32[]{:S(2)}) copy-start(s32[1,3,16,2]{2,3,1,0:T(2,128)} %param.13) | copy-start | bytes 1156
  4.0 11.0 %copy-start.18 = (bf16[1,2048,4]{1,2,0:T(4,128)(2,1)S(1)}, bf16[1,2048,4]{1,2,0:T(4,128)(2,1)}, u32[]{:S(2)}) copy-start(bf16[1,2048,4]{1,2,0:T(4,128)(2,1)} %param.18) | copy-start | bytes 49156
  4.0 11.0 %copy-start.20 = (bf16[1,2048]{1,0:T(2,128)(2,1)S(1)}, bf16[1,2048]{1,0:T(2,128)(2,1)}, u32[]{:S(2)}) copy-start(bf16[1,2048]{1,0:T(2,128)(2,1)} %param.19) | copy-start | bytes 12292
  4.0 36.9 %collective-permute-start = (bf16[3,16,8192]{2,1,0:T(8,128)(2,1)}, bf16[3,16,8192]{2,1,0:T(8,128)(2,1)S(1)}, u32[]{:S(2)}, u32[]{:S(2)}) collective-permute-start(bf16[3,16,8192]{2,1,0:T(8,128)(2,1)} %get-tuple-element.71), channel_id=1, source_target_pairs={{0,1},{1,0},{2,3},{3,2},{4,5},{5,4},{6,7},{7,6},{8,9},{9,8},{10,11... | collective-permute-start | bytes 2359304 | tf_op jit(solution)/shard_map/ppermute | solution.py:18
  7.0 55.3 %collective-permute-start.1 = (bf16[3,16,8192]{2,1,0:T(8,128)(2,1)}, bf16[3,16,8192]{2,1,0:T(8,128)(2,1)S(1)}, u32[]{:S(2)}, u32[]{:S(2)}) collective-permute-start(bf16[3,16,8192]{2,1,0:T(8,128)(2,1)} %get-tuple-element.70), channel_id=1, source_target_pairs={{0,2},{1,3},{2,0},{3,1},{4,6},{5,7},{6,4},{7,5},{8,10},{9,11},{10,... | collective-permute-start | bytes 2359304 | tf_op jit(solution)/shard_map/ppermute | solution.py:18
  9.6 52.7 %collective-permute-start.2 = (bf16[3,16,8192]{2,1,0:T(8,128)(2,1)S(1)}, bf16[3,16,8192]{2,1,0:T(8,128)(2,1)S(1)}, u32[]{:S(2)}, u32[]{:S(2)}) collective-permute-start(bf16[3,16,8192]{2,1,0:T(8,128)(2,1)S(1)} %get-tuple-element.69), channel_id=1, source_target_pairs={{0,3},{1,2},{2,1},{3,0},{4,7},{5,6},{6,5},{7,4},{8,11},{9,10},{10,... | collective-permute-start | bytes 2359304 | tf_op jit(solution)/shard_map/ppermute | solution.py:18
  40.8 21.5 %copy-start.7 = (bf16[3,16,8192]{2,1,0:T(8,128)(2,1)}, bf16[3,16,8192]{2,1,0:T(8,128)(2,1)S(1)}, u32[]{:S(2)}) copy-start(bf16[3,16,8192]{2,1,0:T(8,128)(2,1)S(1)} %collective-permute-done.refs_8_.refs_9_) | copy-start | bytes 2359300
  62.3 0.9 copy-start.8
  62.3 1.1 copy-start.9
  72.4 45.3 %collective-permute-start.10 = (bf16[192,2048]{1,0:T(8,128)(2,1)}, bf16[192,2048]{1,0:T(8,128)(2,1)}, u32[]{:S(2)}, u32[]{:S(2)}) collective-permute-start(bf16[192,2048]{1,0:T(8,128)(2,1)} %bitcast.66), channel_id=1, source_target_pairs={{0,8},{4,12},{8,0},{12,4},{1,9},{5,13},{9,1},{13,5},{2,10},{6,14},... | collective-permute-start | bytes 2359304 | tf_op jit(solution)/shard_map/ppermute | solution.py:18
  74.0 20.6 %collective-permute-start.3 = (bf16[2,16,8192]{2,1,0:T(8,128)(2,1)}, bf16[2,16,8192]{2,1,0:T(8,128)(2,1)S(1)}, u32[]{:S(2)}, u32[]{:S(2)}) collective-permute-start(bf16[2,16,8192]{2,1,0:T(8,128)(2,1)} %get-tuple-element.40), channel_id=1, source_target_pairs={{16,0},{17,1},{18,2},{19,3},{20,4},{21,5},{22,6},{23,7},{24,8},{25... | collective-permute-start | bytes 1572872 | tf_op jit(solution)/shard_map/ppermute | solution.py:380
  76.2 24.8 %copy-start.4 = (bf16[1,16,8192]{2,1,0:T(8,128)(2,1)}, bf16[1,16,8192]{2,1,0:T(8,128)(2,1)S(1)}, u32[]{:S(2)}) copy-start(bf16[1,16,8192]{2,1,0:T(8,128)(2,1)S(1)} %slice.40.refs_0_) | copy-start | bytes 786436
  76.2 41.5 %copy-start.1 = (bf16[1,3,16,8192]{3,2,1,0:T(8,128)(2,1)S(1)}, bf16[1,3,16,8192]{3,2,1,0:T(8,128)(2,1)}, u32[]{:S(2)}) copy-start(bf16[1,3,16,8192]{3,2,1,0:T(8,128)(2,1)} %param.10) | copy-start | bytes 2359300
  76.2 24.8 %collective-permute-start.4 = (bf16[1,16,8192]{2,1,0:T(8,128)(2,1)S(1)}, bf16[1,16,8192]{2,1,0:T(8,128)(2,1)S(1)}, u32[]{:S(2)}, u32[]{:S(2)}) collective-permute-start(bf16[1,16,8192]{2,1,0:T(8,128)(2,1)S(1)} %slice.40.refs_0_), channel_id=1, source_target_pairs={{0,1},{1,0},{2,3},{3,2},{4,5},{5,4},{6,7},{7,6},{8,9},{9,8},{10,11... | collective-permute-start | bytes 786440 | tf_op jit(solution)/shard_map/ppermute | solution.py:18
  92.0 21.3 %collective-permute-start.5 = (bf16[1,16,8192]{2,1,0:T(8,128)(2,1)S(1)}, bf16[1,16,8192]{2,1,0:T(8,128)(2,1)S(1)}, u32[]{:S(2)}, u32[]{:S(2)}) collective-permute-start(bf16[1,16,8192]{2,1,0:T(8,128)(2,1)S(1)} %slice.40.refs_0_), channel_id=1, source_target_pairs={{0,2},{1,3},{2,0},{3,1},{4,6},{5,7},{6,4},{7,5},{8,10},{9,11},{10,... | collective-permute-start | bytes 786440 | tf_op jit(solution)/shard_map/ppermute | solution.py:18
  93.1 20.3 %collective-permute-start.6 = (bf16[1,16,8192]{2,1,0:T(8,128)(2,1)S(1)}, bf16[1,16,8192]{2,1,0:T(8,128)(2,1)S(1)}, u32[]{:S(2)}, u32[]{:S(2)}) collective-permute-start(bf16[1,16,8192]{2,1,0:T(8,128)(2,1)S(1)} %slice.40.refs_0_), channel_id=1, source_target_pairs={{0,3},{1,2},{2,1},{3,0},{4,7},{5,6},{6,5},{7,4},{8,11},{9,10},{10,... | collective-permute-start | bytes 786440 | tf_op jit(solution)/shard_map/ppermute | solution.py:18
  94.5 0.8 copy-start.12
  94.5 60.6 %collective-permute-start.9 = (bf16[192,2048]{1,0:T(8,128)(2,1)}, bf16[192,2048]{1,0:T(8,128)(2,1)}, u32[]{:S(2)}, u32[]{:S(2)}) collective-permute-start(bf16[192,2048]{1,0:T(8,128)(2,1)} %bitcast.67), channel_id=1, source_target_pairs={{0,4},{4,0},{8,12},{12,8},{1,5},{5,1},{9,13},{13,9},{2,6},{6,2},{1... | collective-permute-start | bytes 2359304 | tf_op jit(solution)/shard_map/ppermute | solution.py:18
  101.0 54.2 %copy-start.2 = (bf16[2,16,8192]{2,1,0:T(8,128)(2,1)S(1)}, bf16[2,16,8192]{2,1,0:T(8,128)(2,1)}, u32[]{:S(2)}) copy-start(bf16[2,16,8192]{2,1,0:T(8,128)(2,1)} %get-tuple-element.53.refs_4_.refs_0_) | copy-start | bytes 1572868
  101.0 44.3 %copy-start.13 = (bf16[1,16,8192]{2,1,0:T(8,128)(2,1)}, bf16[1,16,8192]{2,1,0:T(8,128)(2,1)S(1)}, u32[]{:S(2)}) copy-start(bf16[1,16,8192]{2,1,0:T(8,128)(2,1)S(1)} %collective-permute-done.4.refs_1_) | copy-start | bytes 786436
  113.4 32.0 %copy-start.14 = (bf16[1,16,8192]{2,1,0:T(8,128)(2,1)}, bf16[1,16,8192]{2,1,0:T(8,128)(2,1)S(1)}, u32[]{:S(2)}) copy-start(bf16[1,16,8192]{2,1,0:T(8,128)(2,1)S(1)} %collective-permute-done.5.refs_2_) | copy-start | bytes 786436
  113.4 32.0 %copy-start.15 = (bf16[1,16,8192]{2,1,0:T(8,128)(2,1)}, bf16[1,16,8192]{2,1,0:T(8,128)(2,1)S(1)}, u32[]{:S(2)}) copy-start(bf16[1,16,8192]{2,1,0:T(8,128)(2,1)S(1)} %collective-permute-done.6.refs_3_) | copy-start | bytes 786436
  113.4 23.9 %collective-permute-start.7 = (bf16[2,16,8192]{2,1,0:T(8,128)(2,1)}, bf16[2,16,8192]{2,1,0:T(8,128)(2,1)S(1)}, u32[]{:S(2)}, u32[]{:S(2)}) collective-permute-start(bf16[2,16,8192]{2,1,0:T(8,128)(2,1)} %get-tuple-element.53.refs_4_.refs_0_), channel_id=1, source_target_pairs={{0,1},{1,0},{2,3},{3,2},{4,5},{5,4},{6,7},{7,6},{8,9},{9,8},{10,11... | collective-permute-start | bytes 1572872 | tf_op jit(solution)/shard_map/ppermute | solution.py:18
  116.8 20.5 %collective-permute-start.8 = (bf16[2,16,8192]{2,1,0:T(8,128)(2,1)}, bf16[2,16,8192]{2,1,0:T(8,128)(2,1)S(1)}, u32[]{:S(2)}, u32[]{:S(2)}) collective-permute-start(bf16[2,16,8192]{2,1,0:T(8,128)(2,1)} %get-tuple-element.53.refs_4_.refs_0_), channel_id=1, source_target_pairs={{0,2},{1,3},{2,0},{3,1},{4,6},{5,7},{6,4},{7,5},{8,10},{9,11},{10,... | collective-permute-start | bytes 1572872 | tf_op jit(solution)/shard_map/ppermute | solution.py:18
  117.8 37.4 %collective-permute-start.11 = (bf16[192,2048]{1,0:T(8,128)(2,1)}, bf16[192,2048]{1,0:T(8,128)(2,1)}, u32[]{:S(2)}, u32[]{:S(2)}) collective-permute-start(bf16[192,2048]{1,0:T(8,128)(2,1)} %collective-permute-done.10.refs_2_), channel_id=1, source_target_pairs={{0,4},{4,0},{8,12},{12,8},{1,5},{5,1},{9,13},{13,9},{2,6},{6,2},{1... | collective-permute-start | bytes 2359304 | tf_op jit(solution)/shard_map/ppermute | solution.py:18
  137.3 39.6 %copy-start.10 = (bf16[2,16,8192]{2,1,0:T(8,128)(2,1)}, bf16[2,16,8192]{2,1,0:T(8,128)(2,1)S(1)}, u32[]{:S(2)}) copy-start(bf16[2,16,8192]{2,1,0:T(8,128)(2,1)S(1)} %collective-permute-done.7.refs_5_.refs_1_) | copy-start | bytes 1572868
  137.3 39.6 %copy-start.11 = (bf16[2,16,8192]{2,1,0:T(8,128)(2,1)}, bf16[2,16,8192]{2,1,0:T(8,128)(2,1)S(1)}, u32[]{:S(2)}) copy-start(bf16[2,16,8192]{2,1,0:T(8,128)(2,1)S(1)} %collective-permute-done.8.refs_6_.refs_2_) | copy-start | bytes 1572868
  137.3 14.9 %collective-permute-start.16 = (bf16[1,16,8192]{2,1,0:T(8,128)(2,1)}, bf16[1,16,8192]{2,1,0:T(8,128)(2,1)}, u32[]{:S(2)}, u32[]{:S(2)}) collective-permute-start(bf16[1,16,8192]{2,1,0:T(8,128)(2,1)} %slice_bitcast_fusion.refs_0_), channel_id=1, source_target_pairs={{0,1},{1,0},{2,3},{3,2},{4,5},{5,4},{6,7},{7,6},{8,9},{9,8},{10,11... | collective-permute-start | bytes 786440 | tf_op jit(solution)/shard_map/ppermute | solution.py:18
  142.8 10.4 %collective-permute-start.17 = (bf16[1,16,8192]{2,1,0:T(8,128)(2,1)}, bf16[1,16,8192]{2,1,0:T(8,128)(2,1)}, u32[]{:S(2)}, u32[]{:S(2)}) collective-permute-start(bf16[1,16,8192]{2,1,0:T(8,128)(2,1)} %slice_bitcast_fusion.refs_0_), channel_id=1, source_target_pairs={{0,2},{1,3},{2,0},{3,1},{4,6},{5,7},{6,4},{7,5},{8,10},{9,11},{10,... | collective-permute-start | bytes 786440 | tf_op jit(solution)/shard_map/ppermute | solution.py:18
  148.7 18.0 %all-to-all-start = ((bf16[4,64,2048]{2,1,0:T(8,128)(2,1)}), bf16[4,64,2048]{2,1,0:T(8,128)(2,1)S(1)}, u32[]{:S(2)}, u32[]{:S(2)}) async-start(bf16[4,64,2048]{2,1,0:T(8,128)(2,1)} %columns.2), calls=%async_computation | async-start | bytes 2097152 | tf_op jit(solution)/shard_map/all_to_all | solution.py:377
  153.2 6.7 %collective-permute-start.18 = (bf16[1,16,8192]{2,1,0:T(8,128)(2,1)}, bf16[1,16,8192]{2,1,0:T(8,128)(2,1)S(1)}, u32[]{:S(2)}, u32[]{:S(2)}) collective-permute-start(bf16[1,16,8192]{2,1,0:T(8,128)(2,1)} %slice_bitcast_fusion.refs_0_), channel_id=1, source_target_pairs={{1,2},{2,1},{5,6},{6,5},{9,10},{10,9},{13,14},{14,13},{17,18},{18,... | collective-permute-start | bytes 786440 | tf_op jit(solution)/shard_map/ppermute | solution.py:43
  153.8 11.4 %collective-permute-start.19 = (bf16[1,16,8192]{2,1,0:T(8,128)(2,1)}, bf16[1,16,8192]{2,1,0:T(8,128)(2,1)}, u32[]{:S(2)}, u32[]{:S(2)}) collective-permute-start(bf16[1,16,8192]{2,1,0:T(8,128)(2,1)} %collective-permute-done.17.refs_2_), channel_id=1, source_target_pairs={{2,3},{1,0},{6,7},{5,4},{10,11},{9,8},{14,15},{13,12},{18,19},{17,... | collective-permute-start | bytes 786440 | tf_op jit(solution)/shard_map/ppermute | solution.py:44
  155.2 11.5 %collective-permute-start.12 = (bf16[2,16,8192]{2,1,0:T(8,128)(2,1)S(1)}, bf16[2,16,8192]{2,1,0:T(8,128)(2,1)}, u32[]{:S(2)}, u32[]{:S(2)}) collective-permute-start(bf16[2,16,8192]{2,1,0:T(8,128)(2,1)S(1)} %copy-done.2), channel_id=1, source_target_pairs={{1,2},{2,1},{5,6},{6,5},{9,10},{10,9},{13,14},{14,13},{17,18},{18,... | collective-permute-start | bytes 1572872 | tf_op jit(solution)/shard_map/ppermute | solution.py:43
  156.6 18.4 %collective-permute-start.13 = (bf16[2,16,8192]{2,1,0:T(8,128)(2,1)S(1)}, bf16[2,16,8192]{2,1,0:T(8,128)(2,1)}, u32[]{:S(2)}, u32[]{:S(2)}) collective-permute-start(bf16[2,16,8192]{2,1,0:T(8,128)(2,1)S(1)} %collective-permute-done.8.refs_6_.refs_2_), channel_id=1, source_target_pairs={{2,3},{1,0},{6,7},{5,4},{10,11},{9,8},{14,15},{13,12},{18,19},{17,... | collective-permute-start | bytes 1572872 | tf_op jit(solution)/shard_map/ppermute | solution.py:44
  159.9 0.7 copy-start.16
  166.7 14.4 %copy-start.6 = (bf16[4,64,2048]{2,1,0:T(8,128)(2,1)}, bf16[4,64,2048]{2,1,0:T(8,128)(2,1)S(1)}, u32[]{:S(2)}) copy-start(bf16[4,64,2048]{2,1,0:T(8,128)(2,1)S(1)} %all-to-all-done.refs_4_) | copy-start | bytes 3145732
  181.0 7.5 %copy-start.17 = (f32[48,16]{1,0:T(8,128)S(1)}, f32[48,16]{1,0:T(8,128)}, u32[]{:S(2)}) copy-start(f32[48,16]{1,0:T(8,128)} %get-tuple-element.51) | copy-start | bytes 9220
  181.0 34.9 %all-to-all-start.1 = ((bf16[4,144,2048]{2,1,0:T(8,128)(2,1)}), bf16[4,144,2048]{2,1,0:T(8,128)(2,1)S(1)}, u32[]{:S(2)}, u32[]{:S(2)}) async-start(bf16[4,144,2048]{2,1,0:T(8,128)(2,1)} %columns.3), calls=%async_computation.1 | async-start | bytes 4718592 | tf_op jit(solution)/shard_map/all_to_all | solution.py:377
  186.4 24.8 %collective-permute-start.20 = (bf16[2,16,8192]{2,1,0:T(8,128)(2,1)}, bf16[2,16,8192]{2,1,0:T(8,128)(2,1)}, u32[]{:S(2)}, u32[]{:S(2)}) collective-permute-start(bf16[2,16,8192]{2,1,0:T(8,128)(2,1)} %bitcast_select_fusion.refs_4_), channel_id=1, source_target_pairs={{0,1},{1,0},{2,3},{3,2},{4,5},{5,4},{6,7},{7,6},{8,9},{9,8},{10,11... | collective-permute-start | bytes 1572872 | tf_op jit(solution)/shard_map/ppermute | solution.py:18
  186.4 26.8 %collective-permute-start.21 = (bf16[2,16,8192]{2,1,0:T(8,128)(2,1)}, bf16[2,16,8192]{2,1,0:T(8,128)(2,1)}, u32[]{:S(2)}, u32[]{:S(2)}) collective-permute-start(bf16[2,16,8192]{2,1,0:T(8,128)(2,1)} %bitcast_select_fusion.refs_4_), channel_id=1, source_target_pairs={{0,2},{1,3},{2,0},{3,1},{4,6},{5,7},{6,4},{7,5},{8,10},{9,11},{10,... | collective-permute-start | bytes 1572872 | tf_op jit(solution)/shard_map/ppermute | solution.py:18
  189.2 30.3 %copy-start.3 = (bf16[2,16,8192]{2,1,0:T(8,128)(2,1)S(1)}, bf16[2,16,8192]{2,1,0:T(8,128)(2,1)}, u32[]{:S(2)}) copy-start(bf16[2,16,8192]{2,1,0:T(8,128)(2,1)} %get-tuple-element.53.refs_4_.refs_0_) | copy-start | bytes 1572868
  189.2 30.3 %copy-start.5 = (bf16[1,16,8192]{2,1,0:T(8,128)(2,1)S(1)}, bf16[1,16,8192]{2,1,0:T(8,128)(2,1)}, u32[]{:S(2)}) copy-start(bf16[1,16,8192]{2,1,0:T(8,128)(2,1)} %copy-done.4) | copy-start | bytes 786436
  213.2 21.7 %collective-permute-start.22 = (bf16[2,16,8192]{2,1,0:T(8,128)(2,1)}, bf16[2,16,8192]{2,1,0:T(8,128)(2,1)}, u32[]{:S(2)}, u32[]{:S(2)}) collective-permute-start(bf16[2,16,8192]{2,1,0:T(8,128)(2,1)} %bitcast_select_fusion.refs_4_), channel_id=1, source_target_pairs={{1,2},{2,1},{5,6},{6,5},{9,10},{10,9},{13,14},{14,13},{17,18},{18,... | collective-permute-start | bytes 1572872 | tf_op jit(solution)/shard_map/ppermute | solution.py:43
  214.7 20.3 %collective-permute-start.23 = (bf16[2,16,8192]{2,1,0:T(8,128)(2,1)}, bf16[2,16,8192]{2,1,0:T(8,128)(2,1)}, u32[]{:S(2)}, u32[]{:S(2)}) collective-permute-start(bf16[2,16,8192]{2,1,0:T(8,128)(2,1)} %collective-permute-done.21.refs_6_), channel_id=1, source_target_pairs={{2,3},{1,0},{6,7},{5,4},{10,11},{9,8},{14,15},{13,12},{18,19},{17,... | collective-permute-start | bytes 1572872 | tf_op jit(solution)/shard_map/ppermute | solution.py:44
  216.0 4.5 %copy-start = (bf16[4,144,2048]{2,1,0:T(8,128)(2,1)}, bf16[4,144,2048]{2,1,0:T(8,128)(2,1)S(1)}, u32[]{:S(2)}) copy-start(bf16[4,144,2048]{2,1,0:T(8,128)(2,1)S(1)} %all-to-all-done.1.refs_5_) | copy-start | bytes 7077892
  216.1 18.9 %collective-permute-start.14 = (f32[6,2048]{1,0:T(8,128)S(1)}, f32[6,2048]{1,0:T(8,128)S(1)}, u32[]{:S(2)}, u32[]{:S(2)}) collective-permute-start(f32[6,2048]{1,0:T(8,128)S(1)} %pad_maximum_fusion), channel_id=1, source_target_pairs={{0,1},{1,0},{2,3},{3,2},{4,5},{5,4},{6,7},{7,6},{8,9},{9,8},{10,11... | collective-permute-start | bytes 147464 | tf_op jit(solution)/shard_map/ppermute | solution.py:18
  235.0 5.9 %collective-permute-start.15 = (f32[7,2048]{1,0:T(8,128)S(1)}, f32[7,2048]{1,0:T(8,128)S(1)}, u32[]{:S(2)}, u32[]{:S(2)}) collective-permute-start(f32[7,2048]{1,0:T(8,128)S(1)} %pad_maximum_fusion.1), channel_id=1, source_target_pairs={{0,2},{1,3},{2,0},{3,1},{4,6},{5,7},{6,4},{7,5},{8,10},{9,11},{10,... | collective-permute-start | bytes 172040 | tf_op jit(solution)/shard_map/ppermute | solution.py:18

commit v3 on v2

--- a/solution.py
+++ b/solution.py
@@ -362,6 +362,17 @@
             name="step",
         )(flag, *arrays)
 
+    four = (micro, n, rows, inner)
+    spec = pl.BlockSpec((1, n, rows, inner), lambda t, o: (t, 0, 0, 0))
+    gated = call(
+        gate_kernel,
+        out_shape=jax.ShapeDtypeStruct(four, BF16),
+        grid_spec=pltpu.PrefetchScalarGridSpec(
+            num_scalar_prefetch=1, grid=(micro,), in_specs=[spec] * 2, out_specs=spec
+        ),
+        name="gate",
+    )(order, tied(scan_out[0].reshape(four), probs), gate_in[0].reshape(four))
+
     def columns_over(blocks, terms=()):
         count = blocks[0].shape[0]
         high = count * group + (padded if terms else 0)
@@ -376,21 +387,11 @@
         )(*blocks, *terms)
         return lax.all_to_all(split, "dp", split_axis=0, concat_axis=0, tiled=True)
 
-    first, term_first = step_back(0, micro - 1, 1, incoming[0])
+    first, term_first = step_back(0, micro - 1, 1, tied(incoming[0], gated))
     received = lax.ppermute(first, "section", [(1, 0)])
     near_rows = exchange_rows(first[:1])
 
-    four = (micro, n, rows, inner)
-    spec = pl.BlockSpec((1, n, rows, inner), lambda t, o: (t, 0, 0, 0))
-    gated = call(
-        gate_kernel,
-        out_shape=jax.ShapeDtypeStruct(four, BF16),
-        grid_spec=pltpu.PrefetchScalarGridSpec(
-            num_scalar_prefetch=1, grid=(micro,), in_specs=[spec] * 2, out_specs=spec
-        ),
-        name="gate",
-    )(order, tied(scan_out[0].reshape(four), first), gate_in[0].reshape(four))
-    gated = gated.reshape(micro * group, inner)
+    gated = tied(gated.reshape(micro * group, inner), first)
     if n_dp == 4:
         across = partner(gated, "dp", 2)
         lefts = [gated, partner(gated, "dp", 1), across, partner(across, "dp", 1)]
@@ -451,17 +452,9 @@
     total = jnp.sum(tied(rights[1], scan_grad)[:, -padded:].astype(F32), axis=0)[: experts + 1]
     marks = marked[:, :experts].T.reshape(1, -1)
     marks = jnp.pad(marks, ((0, 0), (0, -marks.shape[1] % columns))).reshape(-1, columns)
-    if n == 4:
-        both = partner(jnp.concatenate([total, marks], axis=0), "tensor", 1)
-        total = total + both[: experts + 1]
-        marks = jnp.concatenate([marks, both[experts + 1 :]], axis=0)
-        both = partner(jnp.concatenate([total, marks], axis=0), "tensor", 2)
-        total = total + both[: experts + 1]
-        marks = jnp.concatenate([marks, both[experts + 1 :]], axis=0)
-    else:
-        shared = exchange_rows(jnp.concatenate([total, marks], axis=0))
-        total = sum(x[: experts + 1] for x in shared)
-        marks = jnp.concatenate([x[experts + 1 :] for x in shared], axis=0)
+    shared = exchange_rows(jnp.concatenate([total, marks], axis=0))
+    total = sum(x[: experts + 1] for x in shared)
+    marks = jnp.concatenate([x[experts + 1 :] for x in shared], axis=0)
     marks = marks.reshape(n, -1)[:, : experts * micro * rows].reshape(n, experts, micro, rows)
     mine = jnp.swapaxes(lax.dynamic_index_in_dim(marks, me, 1, False), 0, 1)
 

time: 251 us -> 244 us (0.972)
  waiting for transfers between devices: 90 us -> 84.3 us
    ppermute x17 -> x18, waiting for transfers between devices: 75.5 us -> 68.4 us  [partner(): return lax.ppermute(shard, axis, [(i, i ^ mask) for i in range(length)])]
    ppermute x17 -> x18, starting transfers between devices: 44.1 us -> 46 us  [partner(): return lax.ppermute(shard, axis, [(i, i ^ mask) for i in range(length)])]
  transfers between devices with their start and end apart: 26 -> 27, of which waited for: 11 -> 10; matrix products, arithmetic and copies ran while one was open for 7% -> 7% of each run, Pallas kernels for 19% -> 21%
where the time goes in v3:
time: 244 us; the launch traced here: 243 us
  waiting for transfers between devices  84.3 us (35%)
  Pallas kernels  66.4 us (27%)
  starting transfers between devices  60.3 us (25%)
  local copies, waits for them, and re-layouts  15.8 us (6%)
  other arithmetic  9.62 us (4%)
  blocking collectives  5.43 us (2%)
    ppermute x18, waiting for transfers between devices, partner(): return lax.ppermute(shard, axis, [(i, i ^ mask) for i in range(length)])  68.4 us
    ppermute x18, starting transfers between devices, partner(): return lax.ppermute(shard, axis, [(i, i ^ mask) for i in range(length)])  46 us
    pallas_call x1, Pallas kernels, on_device(): call(functools.partial(inner_kernel, n), out_shape=[jax.ShapeDtypeStruct(...  21.2 us
    pallas_call x1, Pallas kernels, on_device(): call(weight_kernel, out_shape=jax.ShapeDtypeStruct((inner, columns), F32)...  14.4 us
    ppermute x3, waiting for transfers between devices, second_stage(): ends = lax.ppermute(two, 'tensor', [(2, 3), (1, 0)])  14.3 us
    pallas_call x2, Pallas kernels, step_back(): call(functools.partial(step_kernel, experts, len(returned), kept, other i...  10.7 us
    pallas_call x2, Pallas kernels, columns_over(): call(functools.partial(columns_kernel, n), grid=(n_dp,), out_shape=jax.Sh...  7.44 us
    all_to_all x2, starting transfers between devices, columns_over(): return lax.all_to_all(split, 'dp', split_axis=0, concat_axis=0, tiled=True)  7.16 us
  transfers between devices with their start and end apart: 27, of which 10 were waited for; matrix products, arithmetic and copies ran while one was open for 7% of the time, Pallas kernels for 21%

profile of v3, /device:TPU:0, one launch (start us, length us, event | category | flops | bytes accessed | tf_op | source)
XLA Modules:
  0.0 242.8 jit_solution(15464098744300112026)
XLA Ops:
  0.7 3.3 %dynamic-slice_bitcast_fusion = (bf16[3,16,8192]{2,1,0:T(8,128)(2,1)S(1)}, bf16[3,16,8192]{2,1,0:T(8,128)(2,1)}, bf16[3,16,8192]{2,1,0:T(8,128)(2,1)}, bf16[3,16,8192]{2,1,0:T(8,128)(2,1)}) fusion(bf16[3,4,16,8192]{3,2,1,0:T(8,128)(2,1)} %bitcast.69, s32[]{:T(128)S(6)} %select_n.44, s32[]{:T(128)S(6)} %select_n.43, s32[]{:T(128)S(6)} %select_n.42, ...), kind=kLoop, calls=%fused_computation.1 | loop fusion | bytes 6291472 | tf_op jit(solution)/shard_map/jit(dynamic_index_in_dim)/squeeze | solution.py:307
  4.0 3.0 %collective-permute-start = (bf16[3,16,8192]{2,1,0:T(8,128)(2,1)}, bf16[3,16,8192]{2,1,0:T(8,128)(2,1)S(1)}, u32[]{:S(2)}, u32[]{:S(2)}) collective-permute-start(bf16[3,16,8192]{2,1,0:T(8,128)(2,1)} %get-tuple-element.75), channel_id=1, source_target_pairs={{0,1},{1,0},{2,3},{3,2},{4,5},{5,4},{6,7},{7,6},{8,9},{9,8},{10,11... | collective-permute-start | bytes 2359304 | tf_op jit(solution)/shard_map/ppermute | solution.py:18
  7.0 2.6 %collective-permute-start.1 = (bf16[3,16,8192]{2,1,0:T(8,128)(2,1)}, bf16[3,16,8192]{2,1,0:T(8,128)(2,1)S(1)}, u32[]{:S(2)}, u32[]{:S(2)}) collective-permute-start(bf16[3,16,8192]{2,1,0:T(8,128)(2,1)} %get-tuple-element.74), channel_id=1, source_target_pairs={{0,2},{1,3},{2,0},{3,1},{4,6},{5,7},{6,4},{7,5},{8,10},{9,11},{10,... | collective-permute-start | bytes 2359304 | tf_op jit(solution)/shard_map/ppermute | solution.py:18
  10.4 5.4 %all_gather.3 = bf16[5,8192]{1,0:T(8,128)(2,1)S(1)} all-gather(bf16[5,2048]{1,0:T(8,128)(2,1)S(1)} %pad_maximum_fusion.1), channel_id=1, replica_groups=mesh['section'=2,'dp'=4,'tensor'=4] {'dp'}, dimensions={1}, use_global_device_ids=true | all-gather | bytes 102400 | tf_op jit(solution)/shard_map/all_gather | solution.py:314
  16.5 2.5 %probs.1 = (f32[48,16]{1,0:T(8,128)}, f32[48,1]{1,0:T(8,128)}, f32[48,16]{1,0:T(8,128)}) custom-call(bf16[48,8192]{1,0:T(8,128)(2,1)} %bitcast.61, bf16[16,8192]{1,0:T(8,128)(2,1)} %pad.8.small_ref.refs_6_.refs_7_, s32[48,2]{1,0:T(8,128)} %bitcast.75), custom_call_target="tpu_custom_call" | custom-call | tf_op jit(solution)/shard_map/probs/pallas_call | solution.py:317
  19.7 4.0 %gate.1 = bf16[3,4,16,2048]{3,2,1,0:T(8,128)(2,1)} custom-call(s32[4]{0:T(128)} %pad_add_fusion.order_ref, bf16[3,4,16,2048]{3,2,1,0:T(8,128)(2,1)} %bitcast.71, bf16[3,4,16,2048]{3,2,1,0:T(8,128)(2,1)} %bitcast.73), custom_call_target="tpu_custom_call" | custom-call | tf_op jit(solution)/shard_map/gate/pallas_call | solution.py:367
  24.3 3.9 %reshape_squeeze.22.refs_2_.refs_3_ = bf16[3,16,16384]{2,1,0:T(8,128)(2,1)} reshape(bf16[1,3,16,2,8192]{4,3,2,1,0:T(2,128)(2,1)} %param.12) | data formatting | bytes 3145728 | tf_op jit(solution)/shard_map/reshape;squeeze | solution.py:328
  28.9 12.0 %collective-permute-done.refs_8_.refs_9_ = bf16[3,16,8192]{2,1,0:T(8,128)(2,1)S(1)} collective-permute-done((bf16[3,16,8192]{2,1,0:T(8,128)(2,1)}, bf16[3,16,8192]{2,1,0:T(8,128)(2,1)S(1)}, u32[]{:S(2)}, u32[]{:S(2)}) %collective-permute-start) | collective-permute-done | bytes 786464 | tf_op jit(solution)/shard_map/ppermute | solution.py:18
  40.9 21.4 %collective-permute-done.1.refs_9_.refs_10_ = bf16[3,16,8192]{2,1,0:T(8,128)(2,1)S(1)} collective-permute-done((bf16[3,16,8192]{2,1,0:T(8,128)(2,1)}, bf16[3,16,8192]{2,1,0:T(8,128)(2,1)S(1)}, u32[]{:S(2)}, u32[]{:S(2)}) %collective-permute-start.1) | collective-permute-done | bytes 786464 | tf_op jit(solution)/shard_map/ppermute | solution.py:18
  62.3 0.9 copy-done.9
  63.4 5.1 %step.2 = (bf16[2,16,8192]{2,1,0:T(8,128)(2,1)}, f32[16,8192]{1,0:T(8,128)}) custom-call(s32[5]{0:T(128)} %concatenate.16.flag_ref, bf16[3,16,8192]{2,1,0:T(8,128)(2,1)} %bitcast.64, bf16[3,16,8192]{2,1,0:T(8,128)(2,1)} %bitcast.62, bf16[3,16,16384]{2,1,0:T(8,128)(2,1)} %reshape_squeeze.22.refs_2_.refs_3_, s32[3,16,2]{2,1,0:T(8,128)} %copy.34.refs_3_.refs_4_, ...), custom_call_target="tpu_custom_call" | custom-call | tf_op jit(solution)/shard_map/step/pallas_call | solution.py:349
  68.5 1.6 collective-permute-start.10
  70.1 1.3 collective-permute-start.3
  71.4 1.0 slice.46.refs_0_
  72.4 15.8 %collective-permute-start.4 = (bf16[1,16,8192]{2,1,0:T(8,128)(2,1)S(1)}, bf16[1,16,8192]{2,1,0:T(8,128)(2,1)S(1)}, u32[]{:S(2)}, u32[]{:S(2)}) collective-permute-start(bf16[1,16,8192]{2,1,0:T(8,128)(2,1)S(1)} %slice.46.refs_0_), channel_id=1, source_target_pairs={{0,1},{1,0},{2,3},{3,2},{4,5},{5,4},{6,7},{7,6},{8,9},{9,8},{10,11... | collective-permute-start | bytes 786440 | tf_op jit(solution)/shard_map/ppermute | solution.py:18
  88.2 1.1 collective-permute-start.5
  89.3 1.4 collective-permute-start.6
  90.7 0.8 copy-done.12
  91.5 5.6 %step.3 = (bf16[2,16,8192]{2,1,0:T(8,128)(2,1)}, f32[16,8192]{1,0:T(8,128)}) custom-call(s32[5]{0:T(128)} %concatenate.16.flag_ref, bf16[3,16,8192]{2,1,0:T(8,128)(2,1)} %bitcast.65, bf16[2,16,8192]{2,1,0:T(8,128)(2,1)} %copy-done.12, bf16[3,16,8192]{2,1,0:T(8,128)(2,1)} %bitcast.63, bf16[3,16,16384]{2,1,0:T(8,128)(2,1)} %reshape_squeeze.22.refs_2_.refs_3_, ...), custom_call_target="tpu_custom_call" | custom-call | tf_op jit(solution)/shard_map/step/pallas_call | solution.py:349
  97.1 12.4 %collective-permute-done.5.refs_2_ = bf16[1,16,8192]{2,1,0:T(8,128)(2,1)S(1)} collective-permute-done((bf16[1,16,8192]{2,1,0:T(8,128)(2,1)S(1)}, bf16[1,16,8192]{2,1,0:T(8,128)(2,1)S(1)}, u32[]{:S(2)}, u32[]{:S(2)}) %collective-permute-start.5) | collective-permute-done | bytes 262176 | tf_op jit(solution)/shard_map/ppermute | solution.py:18
  109.5 3.4 %collective-permute-start.7 = (bf16[2,16,8192]{2,1,0:T(8,128)(2,1)}, bf16[2,16,8192]{2,1,0:T(8,128)(2,1)S(1)}, u32[]{:S(2)}, u32[]{:S(2)}) collective-permute-start(bf16[2,16,8192]{2,1,0:T(8,128)(2,1)} %get-tuple-element.57.refs_4_.refs_0_), channel_id=1, source_target_pairs={{0,1},{1,0},{2,3},{3,2},{4,5},{5,4},{6,7},{7,6},{8,9},{9,8},{10,11... | collective-permute-start | bytes 1572872 | tf_op jit(solution)/shard_map/ppermute | solution.py:18
  112.9 1.0 collective-permute-start.8
  114.7 18.7 %collective-permute-done.7.refs_5_.refs_1_ = bf16[2,16,8192]{2,1,0:T(8,128)(2,1)S(1)} collective-permute-done((bf16[2,16,8192]{2,1,0:T(8,128)(2,1)}, bf16[2,16,8192]{2,1,0:T(8,128)(2,1)S(1)}, u32[]{:S(2)}, u32[]{:S(2)}) %collective-permute-start.7) | collective-permute-done | bytes 524320 | tf_op jit(solution)/shard_map/ppermute | solution.py:18
  133.4 5.6 %collective-permute-start.17 = (bf16[1,16,8192]{2,1,0:T(8,128)(2,1)}, bf16[1,16,8192]{2,1,0:T(8,128)(2,1)}, u32[]{:S(2)}, u32[]{:S(2)}) collective-permute-start(bf16[1,16,8192]{2,1,0:T(8,128)(2,1)} %slice_bitcast_fusion.refs_0_), channel_id=1, source_target_pairs={{0,1},{1,0},{2,3},{3,2},{4,5},{5,4},{6,7},{7,6},{8,9},{9,8},{10,11... | collective-permute-start | bytes 786440 | tf_op jit(solution)/shard_map/ppermute | solution.py:18
  139.0 2.5 %collective-permute-start.18 = (bf16[1,16,8192]{2,1,0:T(8,128)(2,1)}, bf16[1,16,8192]{2,1,0:T(8,128)(2,1)}, u32[]{:S(2)}, u32[]{:S(2)}) collective-permute-start(bf16[1,16,8192]{2,1,0:T(8,128)(2,1)} %slice_bitcast_fusion.refs_0_), channel_id=1, source_target_pairs={{0,2},{1,3},{2,0},{3,1},{4,6},{5,7},{6,4},{7,5},{8,10},{9,11},{10,... | collective-permute-start | bytes 786440 | tf_op jit(solution)/shard_map/ppermute | solution.py:18
  141.5 3.4 %columns.2 = bf16[4,64,2048]{2,1,0:T(8,128)(2,1)} custom-call(bf16[1,16,8192]{2,1,0:T(8,128)(2,1)} %copy-done.4, bf16[1,16,8192]{2,1,0:T(8,128)(2,1)} %copy-done.14, bf16[1,16,8192]{2,1,0:T(8,128)(2,1)} %copy-done.15, bf16[1,16,8192]{2,1,0:T(8,128)(2,1)} %copy-done.16), custom_call_target="tpu_custom_call" | custom-call | tf_op jit(solution)/shard_map/columns/pallas_call | solution.py:379
  144.9 3.5 %all-to-all-start = ((bf16[4,64,2048]{2,1,0:T(8,128)(2,1)}), bf16[4,64,2048]{2,1,0:T(8,128)(2,1)S(1)}, u32[]{:S(2)}, u32[]{:S(2)}) async-start(bf16[4,64,2048]{2,1,0:T(8,128)(2,1)} %columns.2), calls=%async_computation | async-start | bytes 2097152 | tf_op jit(solution)/shard_map/all_to_all | solution.py:388
  148.4 1.0 collective-permute-done.18.refs_2_
  150.0 1.3 collective-permute-start.20
  152.1 1.3 collective-permute-start.13
  153.4 1.9 bitcast_select_fusion.refs_4_
  155.3 6.0 %collective-permute-done.20 = bf16[1,16,8192]{2,1,0:T(8,128)(2,1)} collective-permute-done((bf16[1,16,8192]{2,1,0:T(8,128)(2,1)}, bf16[1,16,8192]{2,1,0:T(8,128)(2,1)}, u32[]{:S(2)}, u32[]{:S(2)}) %collective-permute-start.20) | collective-permute-done | bytes 262176 | tf_op jit(solution)/shard_map/ppermute | solution.py:44
  161.3 1.6 all-to-all-done.refs_4_
  162.8 8.4 %collective-permute-done.13 = bf16[2,16,8192]{2,1,0:T(8,128)(2,1)} collective-permute-done((bf16[2,16,8192]{2,1,0:T(8,128)(2,1)}, bf16[2,16,8192]{2,1,0:T(8,128)(2,1)}, u32[]{:S(2)}, u32[]{:S(2)}) %collective-permute-start.13) | collective-permute-done | bytes 524320 | tf_op jit(solution)/shard_map/ppermute | solution.py:44
  171.2 1.9 broadcast_select_fusion.1.refs_7_.refs_3_
  173.1 4.1 %columns.3 = bf16[4,144,2048]{2,1,0:T(8,128)(2,1)} custom-call(bf16[2,16,8192]{2,1,0:T(8,128)(2,1)} %get-tuple-element.57.refs_4_.refs_0_, bf16[2,16,8192]{2,1,0:T(8,128)(2,1)} %copy-done.11, bf16[2,16,8192]{2,1,0:T(8,128)(2,1)} %collective-permute-done.8.refs_6_.refs_2_, bf16[2,16,8192]{2,1,0:T(8,128)(2,1)} %broadcast_select_fusion.1.refs_7_.refs_3_, ...), custom_call_target="tpu_custom_call" | custom-call | tf_op jit(solution)/shard_map/columns/pallas_call | solution.py:379
  177.2 3.6 %all-to-all-start.1 = ((bf16[4,144,2048]{2,1,0:T(8,128)(2,1)}), bf16[4,144,2048]{2,1,0:T(8,128)(2,1)S(1)}, u32[]{:S(2)}, u32[]{:S(2)}) async-start(bf16[4,144,2048]{2,1,0:T(8,128)(2,1)} %columns.3), calls=%async_computation.1 | async-start | bytes 4718592 | tf_op jit(solution)/shard_map/all_to_all | solution.py:388
  180.8 1.7 broadcast_select_fusion.2.refs_3_
  182.5 2.1 collective-permute-start.22
  185.3 21.2 %project.1 = (bf16[3,64,2048]{2,1,0:T(8,128)(2,1)}, bf16[3,64,2048]{2,1,0:T(8,128)(2,1)}) custom-call(s32[4]{0:T(128)} %pad_add_fusion.order_ref, bf16[1,16,8192]{2,1,0:T(8,128)(2,1)} %copy-done.4, bf16[1,16,8192]{2,1,0:T(8,128)(2,1)} %copy-done.14, bf16[1,16,8192]{2,1,0:T(8,128)(2,1)} %copy-done.15, bf16[1,16,8192]{2,1,0:T(8,128)(2,1)} %copy-done.16, ...), custom_call_target="tpu_custom_call" | custom-call | tf_op jit(solution)/shard_map/project/pallas_call | solution.py:419
  207.2 2.1 collective-permute-done.22.refs_6_
  210.0 1.3 collective-permute-start.24
  211.3 0.9 maximum_bitcast_fusion
  212.4 3.5 %collective-permute-start.14 = (f32[6,2048]{1,0:T(8,128)S(1)}, f32[6,2048]{1,0:T(8,128)S(1)}, u32[]{:S(2)}, u32[]{:S(2)}) collective-permute-start(f32[6,2048]{1,0:T(8,128)S(1)} %pad_maximum_fusion), channel_id=1, source_target_pairs={{0,1},{1,0},{2,3},{3,2},{4,5},{5,4},{6,7},{7,6},{8,9},{9,8},{10,11... | collective-permute-start | bytes 147464 | tf_op jit(solution)/shard_map/ppermute | solution.py:18
  216.0 2.3 collective-permute-start.16
  218.3 14.4 %weight_grad.1 = f32[2048,2048]{1,0:T(8,128)} custom-call(s32[4]{0:T(128)} %iota_xor_fusion.order_ref, bf16[192,2048]{1,0:T(8,128)(2,1)} %bitcast.66, bf16[192,2048]{1,0:T(8,128)(2,1)} %collective-permute-done.9.refs_1_, bf16[192,2048]{1,0:T(8,128)(2,1)} %collective-permute-done.10.refs_2_, bf16[192,2048]{1,0:T(8,128)(2,1)} %collective-permute-done.11.refs_3_, ...), custom_call_target="tpu_custom_call" | custom-call | tf_op jit(solution)/shard_map/weight_grad/pallas_call | solution.py:437
  232.7 1.9 broadcast_select_fusion.refs_7_
  236.7 6.2 %dispatch.1 = bf16[3,64,8192]{2,1,0:T(8,128)(2,1)} custom-call(s32[4]{0:T(128)} %pad_add_fusion.order_ref, f32[3,4,16]{2,1,0:T(4,128)} %bitcast.80, bf16[1,16,8192]{2,1,0:T(8,128)(2,1)} %slice_bitcast_fusion.refs_0_, bf16[1,16,8192]{2,1,0:T(8,128)(2,1)} %collective-permute-done.17.refs_1_, bf16[1,16,8192]{2,1,0:T(8,128)(2,1)} %collective-permute-done.18.refs_2_, ...), custom_call_target="tpu_custom_call" | custom-call | tf_op jit(solution)/shard_map/dispatch/pallas_call | solution.py:461
  (93 shorter events, 10.2 us)
Async XLA Ops:
  0.7 9.0 %copy-start.20 = (s32[1,3,16,2]{2,3,1,0:T(2,128)S(1)}, s32[1,3,16,2]{2,3,1,0:T(2,128)}, u32[]{:S(2)}) copy-start(s32[1,3,16,2]{2,3,1,0:T(2,128)} %param.13) | copy-start | bytes 1156
  0.7 9.7 %copy-start.19 = (bf16[1,2048,4]{1,2,0:T(4,128)(2,1)S(1)}, bf16[1,2048,4]{1,2,0:T(4,128)(2,1)}, u32[]{:S(2)}) copy-start(bf16[1,2048,4]{1,2,0:T(4,128)(2,1)} %param.18) | copy-start | bytes 49156
  0.7 9.6 %copy-start.21 = (bf16[1,2048]{1,0:T(2,128)(2,1)S(1)}, bf16[1,2048]{1,0:T(2,128)(2,1)}, u32[]{:S(2)}) copy-start(bf16[1,2048]{1,0:T(2,128)(2,1)} %param.19) | copy-start | bytes 12292
  4.0 36.9 %collective-permute-start = (bf16[3,16,8192]{2,1,0:T(8,128)(2,1)}, bf16[3,16,8192]{2,1,0:T(8,128)(2,1)S(1)}, u32[]{:S(2)}, u32[]{:S(2)}) collective-permute-start(bf16[3,16,8192]{2,1,0:T(8,128)(2,1)} %get-tuple-element.75), channel_id=1, source_target_pairs={{0,1},{1,0},{2,3},{3,2},{4,5},{5,4},{6,7},{7,6},{8,9},{9,8},{10,11... | collective-permute-start | bytes 2359304 | tf_op jit(solution)/shard_map/ppermute | solution.py:18
  7.0 55.3 %collective-permute-start.1 = (bf16[3,16,8192]{2,1,0:T(8,128)(2,1)}, bf16[3,16,8192]{2,1,0:T(8,128)(2,1)S(1)}, u32[]{:S(2)}, u32[]{:S(2)}) collective-permute-start(bf16[3,16,8192]{2,1,0:T(8,128)(2,1)} %get-tuple-element.74), channel_id=1, source_target_pairs={{0,2},{1,3},{2,0},{3,1},{4,6},{5,7},{6,4},{7,5},{8,10},{9,11},{10,... | collective-permute-start | bytes 2359304 | tf_op jit(solution)/shard_map/ppermute | solution.py:18
  9.6 52.7 %collective-permute-start.2 = (bf16[3,16,8192]{2,1,0:T(8,128)(2,1)S(1)}, bf16[3,16,8192]{2,1,0:T(8,128)(2,1)S(1)}, u32[]{:S(2)}, u32[]{:S(2)}) collective-permute-start(bf16[3,16,8192]{2,1,0:T(8,128)(2,1)S(1)} %get-tuple-element.73), channel_id=1, source_target_pairs={{0,3},{1,2},{2,1},{3,0},{4,7},{5,6},{6,5},{7,4},{8,11},{9,10},{10,... | collective-permute-start | bytes 2359304 | tf_op jit(solution)/shard_map/ppermute | solution.py:18
  40.9 21.5 %copy-start.8 = (bf16[3,16,8192]{2,1,0:T(8,128)(2,1)}, bf16[3,16,8192]{2,1,0:T(8,128)(2,1)S(1)}, u32[]{:S(2)}) copy-start(bf16[3,16,8192]{2,1,0:T(8,128)(2,1)S(1)} %collective-permute-done.refs_8_.refs_9_) | copy-start | bytes 2359300
  62.3 0.9 copy-start.9
  62.3 1.1 copy-start.10
  63.4 5.1 %copy-start.7 = (bf16[3,4,16,2048]{3,2,1,0:T(8,128)(2,1)S(1)}, bf16[3,4,16,2048]{3,2,1,0:T(8,128)(2,1)}, u32[]{:S(2)}) copy-start(bf16[3,4,16,2048]{3,2,1,0:T(8,128)(2,1)} %gate.1) | copy-start | bytes 2359300
  68.5 45.4 %collective-permute-start.10 = (bf16[192,2048]{1,0:T(8,128)(2,1)S(1)}, bf16[192,2048]{1,0:T(8,128)(2,1)}, u32[]{:S(2)}, u32[]{:S(2)}) collective-permute-start(bf16[192,2048]{1,0:T(8,128)(2,1)S(1)} %bitcast.67), channel_id=1, source_target_pairs={{0,8},{4,12},{8,0},{12,4},{1,9},{5,13},{9,1},{13,5},{2,10},{6,14},... | collective-permute-start | bytes 2359304 | tf_op jit(solution)/shard_map/ppermute | solution.py:18
  70.1 20.6 %collective-permute-start.3 = (bf16[2,16,8192]{2,1,0:T(8,128)(2,1)}, bf16[2,16,8192]{2,1,0:T(8,128)(2,1)S(1)}, u32[]{:S(2)}, u32[]{:S(2)}) collective-permute-start(bf16[2,16,8192]{2,1,0:T(8,128)(2,1)} %get-tuple-element.44), channel_id=1, source_target_pairs={{16,0},{17,1},{18,2},{19,3},{20,4},{21,5},{22,6},{23,7},{24,8},{25... | collective-permute-start | bytes 1572872 | tf_op jit(solution)/shard_map/ppermute | solution.py:391
  72.4 24.7 %copy-start.4 = (bf16[1,16,8192]{2,1,0:T(8,128)(2,1)}, bf16[1,16,8192]{2,1,0:T(8,128)(2,1)S(1)}, u32[]{:S(2)}) copy-start(bf16[1,16,8192]{2,1,0:T(8,128)(2,1)S(1)} %slice.46.refs_0_) | copy-start | bytes 786436
  72.4 41.5 %copy-start.1 = (bf16[1,3,16,8192]{3,2,1,0:T(8,128)(2,1)S(1)}, bf16[1,3,16,8192]{3,2,1,0:T(8,128)(2,1)}, u32[]{:S(2)}) copy-start(bf16[1,3,16,8192]{3,2,1,0:T(8,128)(2,1)} %param.10) | copy-start | bytes 2359300
  72.4 24.7 %collective-permute-start.4 = (bf16[1,16,8192]{2,1,0:T(8,128)(2,1)S(1)}, bf16[1,16,8192]{2,1,0:T(8,128)(2,1)S(1)}, u32[]{:S(2)}, u32[]{:S(2)}) collective-permute-start(bf16[1,16,8192]{2,1,0:T(8,128)(2,1)S(1)} %slice.46.refs_0_), channel_id=1, source_target_pairs={{0,1},{1,0},{2,3},{3,2},{4,5},{5,4},{6,7},{7,6},{8,9},{9,8},{10,11... | collective-permute-start | bytes 786440 | tf_op jit(solution)/shard_map/ppermute | solution.py:18
  88.2 21.3 %collective-permute-start.5 = (bf16[1,16,8192]{2,1,0:T(8,128)(2,1)S(1)}, bf16[1,16,8192]{2,1,0:T(8,128)(2,1)S(1)}, u32[]{:S(2)}, u32[]{:S(2)}) collective-permute-start(bf16[1,16,8192]{2,1,0:T(8,128)(2,1)S(1)} %slice.46.refs_0_), channel_id=1, source_target_pairs={{0,2},{1,3},{2,0},{3,1},{4,6},{5,7},{6,4},{7,5},{8,10},{9,11},{10,... | collective-permute-start | bytes 786440 | tf_op jit(solution)/shard_map/ppermute | solution.py:18
  89.3 20.2 %collective-permute-start.6 = (bf16[1,16,8192]{2,1,0:T(8,128)(2,1)S(1)}, bf16[1,16,8192]{2,1,0:T(8,128)(2,1)S(1)}, u32[]{:S(2)}, u32[]{:S(2)}) collective-permute-start(bf16[1,16,8192]{2,1,0:T(8,128)(2,1)S(1)} %slice.46.refs_0_), channel_id=1, source_target_pairs={{0,3},{1,2},{2,1},{3,0},{4,7},{5,6},{6,5},{7,4},{8,11},{9,10},{10,... | collective-permute-start | bytes 786440 | tf_op jit(solution)/shard_map/ppermute | solution.py:18
  90.7 60.7 %collective-permute-start.9 = (bf16[192,2048]{1,0:T(8,128)(2,1)S(1)}, bf16[192,2048]{1,0:T(8,128)(2,1)}, u32[]{:S(2)}, u32[]{:S(2)}) collective-permute-start(bf16[192,2048]{1,0:T(8,128)(2,1)S(1)} %bitcast.68), channel_id=1, source_target_pairs={{0,4},{4,0},{8,12},{12,8},{1,5},{5,1},{9,13},{13,9},{2,6},{6,2},{1... | collective-permute-start | bytes 2359304 | tf_op jit(solution)/shard_map/ppermute | solution.py:18
  97.1 54.3 %copy-start.2 = (bf16[2,16,8192]{2,1,0:T(8,128)(2,1)S(1)}, bf16[2,16,8192]{2,1,0:T(8,128)(2,1)}, u32[]{:S(2)}) copy-start(bf16[2,16,8192]{2,1,0:T(8,128)(2,1)} %get-tuple-element.57.refs_4_.refs_0_) | copy-start | bytes 1572868
  97.1 44.4 %copy-start.14 = (bf16[1,16,8192]{2,1,0:T(8,128)(2,1)}, bf16[1,16,8192]{2,1,0:T(8,128)(2,1)S(1)}, u32[]{:S(2)}) copy-start(bf16[1,16,8192]{2,1,0:T(8,128)(2,1)S(1)} %collective-permute-done.4.refs_1_) | copy-start | bytes 786436
  109.5 32.0 %copy-start.15 = (bf16[1,16,8192]{2,1,0:T(8,128)(2,1)}, bf16[1,16,8192]{2,1,0:T(8,128)(2,1)S(1)}, u32[]{:S(2)}) copy-start(bf16[1,16,8192]{2,1,0:T(8,128)(2,1)S(1)} %collective-permute-done.5.refs_2_) | copy-start | bytes 786436
  109.5 32.0 %copy-start.16 = (bf16[1,16,8192]{2,1,0:T(8,128)(2,1)}, bf16[1,16,8192]{2,1,0:T(8,128)(2,1)S(1)}, u32[]{:S(2)}) copy-start(bf16[1,16,8192]{2,1,0:T(8,128)(2,1)S(1)} %collective-permute-done.6.refs_3_) | copy-start | bytes 786436
  109.5 23.9 %collective-permute-start.7 = (bf16[2,16,8192]{2,1,0:T(8,128)(2,1)}, bf16[2,16,8192]{2,1,0:T(8,128)(2,1)S(1)}, u32[]{:S(2)}, u32[]{:S(2)}) collective-permute-start(bf16[2,16,8192]{2,1,0:T(8,128)(2,1)} %get-tuple-element.57.refs_4_.refs_0_), channel_id=1, source_target_pairs={{0,1},{1,0},{2,3},{3,2},{4,5},{5,4},{6,7},{7,6},{8,9},{9,8},{10,11... | collective-permute-start | bytes 1572872 | tf_op jit(solution)/shard_map/ppermute | solution.py:18
  112.9 20.5 %collective-permute-start.8 = (bf16[2,16,8192]{2,1,0:T(8,128)(2,1)}, bf16[2,16,8192]{2,1,0:T(8,128)(2,1)}, u32[]{:S(2)}, u32[]{:S(2)}) collective-permute-start(bf16[2,16,8192]{2,1,0:T(8,128)(2,1)} %get-tuple-element.57.refs_4_.refs_0_), channel_id=1, source_target_pairs={{0,2},{1,3},{2,0},{3,1},{4,6},{5,7},{6,4},{7,5},{8,10},{9,11},{10,... | collective-permute-start | bytes 1572872 | tf_op jit(solution)/shard_map/ppermute | solution.py:18
  113.9 37.4 %collective-permute-start.11 = (bf16[192,2048]{1,0:T(8,128)(2,1)}, bf16[192,2048]{1,0:T(8,128)(2,1)}, u32[]{:S(2)}, u32[]{:S(2)}) collective-permute-start(bf16[192,2048]{1,0:T(8,128)(2,1)} %collective-permute-done.10.refs_2_), channel_id=1, source_target_pairs={{0,4},{4,0},{8,12},{12,8},{1,5},{5,1},{9,13},{13,9},{2,6},{6,2},{1... | collective-permute-start | bytes 2359304 | tf_op jit(solution)/shard_map/ppermute | solution.py:18
  133.4 11.4 %copy-start.11 = (bf16[2,16,8192]{2,1,0:T(8,128)(2,1)}, bf16[2,16,8192]{2,1,0:T(8,128)(2,1)S(1)}, u32[]{:S(2)}) copy-start(bf16[2,16,8192]{2,1,0:T(8,128)(2,1)S(1)} %collective-permute-done.7.refs_5_.refs_1_) | copy-start | bytes 1572868
  133.4 15.0 %collective-permute-start.17 = (bf16[1,16,8192]{2,1,0:T(8,128)(2,1)}, bf16[1,16,8192]{2,1,0:T(8,128)(2,1)}, u32[]{:S(2)}, u32[]{:S(2)}) collective-permute-start(bf16[1,16,8192]{2,1,0:T(8,128)(2,1)} %slice_bitcast_fusion.refs_0_), channel_id=1, source_target_pairs={{0,1},{1,0},{2,3},{3,2},{4,5},{5,4},{6,7},{7,6},{8,9},{9,8},{10,11... | collective-permute-start | bytes 786440 | tf_op jit(solution)/shard_map/ppermute | solution.py:18
  139.0 10.4 %collective-permute-start.18 = (bf16[1,16,8192]{2,1,0:T(8,128)(2,1)}, bf16[1,16,8192]{2,1,0:T(8,128)(2,1)}, u32[]{:S(2)}, u32[]{:S(2)}) collective-permute-start(bf16[1,16,8192]{2,1,0:T(8,128)(2,1)} %slice_bitcast_fusion.refs_0_), channel_id=1, source_target_pairs={{0,2},{1,3},{2,0},{3,1},{4,6},{5,7},{6,4},{7,5},{8,10},{9,11},{10,... | collective-permute-start | bytes 786440 | tf_op jit(solution)/shard_map/ppermute | solution.py:18
  144.9 18.0 %all-to-all-start = ((bf16[4,64,2048]{2,1,0:T(8,128)(2,1)}), bf16[4,64,2048]{2,1,0:T(8,128)(2,1)S(1)}, u32[]{:S(2)}, u32[]{:S(2)}) async-start(bf16[4,64,2048]{2,1,0:T(8,128)(2,1)} %columns.2), calls=%async_computation | async-start | bytes 2097152 | tf_op jit(solution)/shard_map/all_to_all | solution.py:388
  149.4 5.9 %collective-permute-start.19 = (bf16[1,16,8192]{2,1,0:T(8,128)(2,1)}, bf16[1,16,8192]{2,1,0:T(8,128)(2,1)S(1)}, u32[]{:S(2)}, u32[]{:S(2)}) collective-permute-start(bf16[1,16,8192]{2,1,0:T(8,128)(2,1)} %slice_bitcast_fusion.refs_0_), channel_id=1, source_target_pairs={{1,2},{2,1},{5,6},{6,5},{9,10},{10,9},{13,14},{14,13},{17,18},{18,... | collective-permute-start | bytes 786440 | tf_op jit(solution)/shard_map/ppermute | solution.py:43
  150.0 11.2 %collective-permute-start.20 = (bf16[1,16,8192]{2,1,0:T(8,128)(2,1)}, bf16[1,16,8192]{2,1,0:T(8,128)(2,1)}, u32[]{:S(2)}, u32[]{:S(2)}) collective-permute-start(bf16[1,16,8192]{2,1,0:T(8,128)(2,1)} %collective-permute-done.18.refs_2_), channel_id=1, source_target_pairs={{2,3},{1,0},{6,7},{5,4},{10,11},{9,8},{14,15},{13,12},{18,19},{17,... | collective-permute-start | bytes 786440 | tf_op jit(solution)/shard_map/ppermute | solution.py:44
  151.4 11.4 %collective-permute-start.12 = (bf16[2,16,8192]{2,1,0:T(8,128)(2,1)S(1)}, bf16[2,16,8192]{2,1,0:T(8,128)(2,1)S(1)}, u32[]{:S(2)}, u32[]{:S(2)}) collective-permute-start(bf16[2,16,8192]{2,1,0:T(8,128)(2,1)S(1)} %copy-done.2), channel_id=1, source_target_pairs={{1,2},{2,1},{5,6},{6,5},{9,10},{10,9},{13,14},{14,13},{17,18},{18,... | collective-permute-start | bytes 1572872 | tf_op jit(solution)/shard_map/ppermute | solution.py:43
  152.1 19.1 %collective-permute-start.13 = (bf16[2,16,8192]{2,1,0:T(8,128)(2,1)}, bf16[2,16,8192]{2,1,0:T(8,128)(2,1)}, u32[]{:S(2)}, u32[]{:S(2)}) collective-permute-start(bf16[2,16,8192]{2,1,0:T(8,128)(2,1)} %collective-permute-done.8.refs_6_.refs_2_), channel_id=1, source_target_pairs={{2,3},{1,0},{6,7},{5,4},{10,11},{9,8},{14,15},{13,12},{18,19},{17,... | collective-permute-start | bytes 1572872 | tf_op jit(solution)/shard_map/ppermute | solution.py:44
  162.8 14.4 %copy-start.6 = (bf16[4,64,2048]{2,1,0:T(8,128)(2,1)}, bf16[4,64,2048]{2,1,0:T(8,128)(2,1)S(1)}, u32[]{:S(2)}) copy-start(bf16[4,64,2048]{2,1,0:T(8,128)(2,1)S(1)} %all-to-all-done.refs_4_) | copy-start | bytes 3145732
  177.2 7.4 %copy-start.18 = (f32[48,16]{1,0:T(8,128)S(1)}, f32[48,16]{1,0:T(8,128)}, u32[]{:S(2)}) copy-start(f32[48,16]{1,0:T(8,128)} %get-tuple-element.55) | copy-start | bytes 9220
  177.2 35.1 %all-to-all-start.1 = ((bf16[4,144,2048]{2,1,0:T(8,128)(2,1)}), bf16[4,144,2048]{2,1,0:T(8,128)(2,1)S(1)}, u32[]{:S(2)}, u32[]{:S(2)}) async-start(bf16[4,144,2048]{2,1,0:T(8,128)(2,1)} %columns.3), calls=%async_computation.1 | async-start | bytes 4718592 | tf_op jit(solution)/shard_map/all_to_all | solution.py:388
  182.5 24.7 %collective-permute-start.21 = (bf16[2,16,8192]{2,1,0:T(8,128)(2,1)}, bf16[2,16,8192]{2,1,0:T(8,128)(2,1)S(1)}, u32[]{:S(2)}, u32[]{:S(2)}) collective-permute-start(bf16[2,16,8192]{2,1,0:T(8,128)(2,1)} %bitcast_select_fusion.refs_4_), channel_id=1, source_target_pairs={{0,1},{1,0},{2,3},{3,2},{4,5},{5,4},{6,7},{7,6},{8,9},{9,8},{10,11... | collective-permute-start | bytes 1572872 | tf_op jit(solution)/shard_map/ppermute | solution.py:18
  182.5 26.8 %collective-permute-start.22 = (bf16[2,16,8192]{2,1,0:T(8,128)(2,1)}, bf16[2,16,8192]{2,1,0:T(8,128)(2,1)}, u32[]{:S(2)}, u32[]{:S(2)}) collective-permute-start(bf16[2,16,8192]{2,1,0:T(8,128)(2,1)} %bitcast_select_fusion.refs_4_), channel_id=1, source_target_pairs={{0,2},{1,3},{2,0},{3,1},{4,6},{5,7},{6,4},{7,5},{8,10},{9,11},{10,... | collective-permute-start | bytes 1572872 | tf_op jit(solution)/shard_map/ppermute | solution.py:18
  185.3 24.0 %copy-start.13 = (bf16[2,16,8192]{2,1,0:T(8,128)(2,1)S(1)}, bf16[2,16,8192]{2,1,0:T(8,128)(2,1)}, u32[]{:S(2)}) copy-start(bf16[2,16,8192]{2,1,0:T(8,128)(2,1)} %bitcast_select_fusion.refs_4_) | copy-start | bytes 1572868
  185.3 26.0 %copy-start.3 = (bf16[2,16,8192]{2,1,0:T(8,128)(2,1)S(1)}, bf16[2,16,8192]{2,1,0:T(8,128)(2,1)}, u32[]{:S(2)}) copy-start(bf16[2,16,8192]{2,1,0:T(8,128)(2,1)} %get-tuple-element.57.refs_4_.refs_0_) | copy-start | bytes 1572868
  185.3 26.0 %copy-start.5 = (bf16[1,16,8192]{2,1,0:T(8,128)(2,1)S(1)}, bf16[1,16,8192]{2,1,0:T(8,128)(2,1)}, u32[]{:S(2)}) copy-start(bf16[1,16,8192]{2,1,0:T(8,128)(2,1)} %copy-done.4) | copy-start | bytes 786436
  207.2 2.1 copy-start.17
  209.3 23.4 %collective-permute-start.23 = (bf16[2,16,8192]{2,1,0:T(8,128)(2,1)S(1)}, bf16[2,16,8192]{2,1,0:T(8,128)(2,1)S(1)}, u32[]{:S(2)}, u32[]{:S(2)}) collective-permute-start(bf16[2,16,8192]{2,1,0:T(8,128)(2,1)S(1)} %copy-done.13), channel_id=1, source_target_pairs={{1,2},{2,1},{5,6},{6,5},{9,10},{10,9},{13,14},{14,13},{17,18},{18,... | collective-permute-start | bytes 1572872 | tf_op jit(solution)/shard_map/ppermute | solution.py:43
  210.0 22.7 %collective-permute-start.24 = (bf16[2,16,8192]{2,1,0:T(8,128)(2,1)}, bf16[2,16,8192]{2,1,0:T(8,128)(2,1)}, u32[]{:S(2)}, u32[]{:S(2)}) collective-permute-start(bf16[2,16,8192]{2,1,0:T(8,128)(2,1)} %collective-permute-done.22.refs_6_), channel_id=1, source_target_pairs={{2,3},{1,0},{6,7},{5,4},{10,11},{9,8},{14,15},{13,12},{18,19},{17,... | collective-permute-start | bytes 1572872 | tf_op jit(solution)/shard_map/ppermute | solution.py:44
  212.3 6.0 %copy-start = (bf16[4,144,2048]{2,1,0:T(8,128)(2,1)}, bf16[4,144,2048]{2,1,0:T(8,128)(2,1)S(1)}, u32[]{:S(2)}) copy-start(bf16[4,144,2048]{2,1,0:T(8,128)(2,1)S(1)} %all-to-all-done.1.refs_5_) | copy-start | bytes 7077892
  212.4 22.3 %collective-permute-start.14 = (f32[6,2048]{1,0:T(8,128)S(1)}, f32[6,2048]{1,0:T(8,128)S(1)}, u32[]{:S(2)}, u32[]{:S(2)}) collective-permute-start(f32[6,2048]{1,0:T(8,128)S(1)} %pad_maximum_fusion), channel_id=1, source_target_pairs={{0,1},{1,0},{2,3},{3,2},{4,5},{5,4},{6,7},{7,6},{8,9},{9,8},{10,11... | collective-permute-start | bytes 147464 | tf_op jit(solution)/shard_map/ppermute | solution.py:18
  215.8 18.8 %collective-permute-start.15 = (f32[6,2048]{1,0:T(8,128)S(1)}, f32[6,2048]{1,0:T(8,128)S(1)}, u32[]{:S(2)}, u32[]{:S(2)}) collective-permute-start(f32[6,2048]{1,0:T(8,128)S(1)} %pad_maximum_fusion), channel_id=1, source_target_pairs={{0,2},{1,3},{2,0},{3,1},{4,6},{5,7},{6,4},{7,5},{8,10},{9,11},{10,... | collective-permute-start | bytes 147464 | tf_op jit(solution)/shard_map/ppermute | solution.py:18
  216.0 18.6 %collective-permute-start.16 = (f32[6,2048]{1,0:T(8,128)S(1)}, f32[6,2048]{1,0:T(8,128)S(1)}, u32[]{:S(2)}, u32[]{:S(2)}) collective-permute-start(f32[6,2048]{1,0:T(8,128)S(1)} %pad_maximum_fusion), channel_id=1, source_target_pairs={{0,3},{1,2},{2,1},{3,0},{4,7},{5,6},{6,5},{7,4},{8,11},{9,10},{10,... | collective-permute-start | bytes 147464 | tf_op jit(solution)/shard_map/ppermute | solution.py:18
  (1 other events, 0.8 us)

commit v4 on v3

--- a/solution.py
+++ b/solution.py
@@ -434,6 +434,7 @@
     source_later = second_stage(source_half, scan_grad)
     depth = lefts[0].shape[0]
     order_dp = me_dp ^ jnp.arange(n_dp, dtype=jnp.int32)
+    tile = min(inner, 512)
     weight_grad = call(
         weight_kernel,
         out_shape=jax.ShapeDtypeStruct((inner, columns), F32),

time: 244 us -> 243 us (level)
  no operation moved by 1% of the time
where the time goes in v4:
time: 243 us; the launch traced here: 241 us
  waiting for transfers between devices  84.3 us (35%)
  Pallas kernels  64.9 us (27%)
  starting transfers between devices  60.3 us (25%)
  local copies, waits for them, and re-layouts  15.8 us (7%)
  other arithmetic  9.62 us (4%)
  blocking collectives  5.43 us (2%)
    ppermute x18, waiting for transfers between devices, partner(): return lax.ppermute(shard, axis, [(i, i ^ mask) for i in range(length)])  68.4 us
    ppermute x18, starting transfers between devices, partner(): return lax.ppermute(shard, axis, [(i, i ^ mask) for i in range(length)])  46 us
    pallas_call x1, Pallas kernels, on_device(): call(functools.partial(inner_kernel, n), out_shape=[jax.ShapeDtypeStruct(...  21.2 us
    ppermute x3, waiting for transfers between devices, second_stage(): ends = lax.ppermute(two, 'tensor', [(2, 3), (1, 0)])  14.3 us
    pallas_call x1, Pallas kernels, on_device(): call(weight_kernel, out_shape=jax.ShapeDtypeStruct((inner, columns), F32)...  12.9 us
    pallas_call x2, Pallas kernels, step_back(): call(functools.partial(step_kernel, experts, len(returned), kept, other i...  10.7 us
    pallas_call x2, Pallas kernels, columns_over(): call(functools.partial(columns_kernel, n), grid=(n_dp,), out_shape=jax.Sh...  7.44 us
    all_to_all x2, starting transfers between devices, columns_over(): return lax.all_to_all(split, 'dp', split_axis=0, concat_axis=0, tiled=True)  7.16 us
  transfers between devices with their start and end apart: 27, of which 10 were waited for; matrix products, arithmetic and copies ran while one was open for 7% of the time, Pallas kernels for 21%

profile of v4, /device:TPU:0, one launch (start us, length us, event | category | flops | bytes accessed | tf_op | source)
XLA Modules:
  0.0 241.3 jit_solution(164724948426475033)
XLA Ops:
  0.7 3.3 %dynamic-slice_bitcast_fusion = (bf16[3,16,8192]{2,1,0:T(8,128)(2,1)S(1)}, bf16[3,16,8192]{2,1,0:T(8,128)(2,1)}, bf16[3,16,8192]{2,1,0:T(8,128)(2,1)}, bf16[3,16,8192]{2,1,0:T(8,128)(2,1)}) fusion(bf16[3,4,16,8192]{3,2,1,0:T(8,128)(2,1)} %bitcast.69, s32[]{:T(128)S(6)} %select_n.44, s32[]{:T(128)S(6)} %select_n.43, s32[]{:T(128)S(6)} %select_n.42, ...), kind=kLoop, calls=%fused_computation.1 | loop fusion | bytes 6291472 | tf_op jit(solution)/shard_map/jit(dynamic_index_in_dim)/squeeze | solution.py:307
  4.0 3.0 %collective-permute-start = (bf16[3,16,8192]{2,1,0:T(8,128)(2,1)}, bf16[3,16,8192]{2,1,0:T(8,128)(2,1)S(1)}, u32[]{:S(2)}, u32[]{:S(2)}) collective-permute-start(bf16[3,16,8192]{2,1,0:T(8,128)(2,1)} %get-tuple-element.75), channel_id=1, source_target_pairs={{0,1},{1,0},{2,3},{3,2},{4,5},{5,4},{6,7},{7,6},{8,9},{9,8},{10,11... | collective-permute-start | bytes 2359304 | tf_op jit(solution)/shard_map/ppermute | solution.py:18
  7.0 2.6 %collective-permute-start.1 = (bf16[3,16,8192]{2,1,0:T(8,128)(2,1)}, bf16[3,16,8192]{2,1,0:T(8,128)(2,1)S(1)}, u32[]{:S(2)}, u32[]{:S(2)}) collective-permute-start(bf16[3,16,8192]{2,1,0:T(8,128)(2,1)} %get-tuple-element.74), channel_id=1, source_target_pairs={{0,2},{1,3},{2,0},{3,1},{4,6},{5,7},{6,4},{7,5},{8,10},{9,11},{10,... | collective-permute-start | bytes 2359304 | tf_op jit(solution)/shard_map/ppermute | solution.py:18
  10.4 5.4 %all_gather.3 = bf16[5,8192]{1,0:T(8,128)(2,1)S(1)} all-gather(bf16[5,2048]{1,0:T(8,128)(2,1)S(1)} %pad_maximum_fusion.1), channel_id=1, replica_groups=mesh['section'=2,'dp'=4,'tensor'=4] {'dp'}, dimensions={1}, use_global_device_ids=true | all-gather | bytes 102400 | tf_op jit(solution)/shard_map/all_gather | solution.py:314
  16.5 2.5 %probs.1 = (f32[48,16]{1,0:T(8,128)}, f32[48,1]{1,0:T(8,128)}, f32[48,16]{1,0:T(8,128)}) custom-call(bf16[48,8192]{1,0:T(8,128)(2,1)} %bitcast.61, bf16[16,8192]{1,0:T(8,128)(2,1)} %pad.8.small_ref.refs_6_.refs_7_, s32[48,2]{1,0:T(8,128)} %bitcast.75), custom_call_target="tpu_custom_call" | custom-call | tf_op jit(solution)/shard_map/probs/pallas_call | solution.py:317
  19.7 4.0 %gate.1 = bf16[3,4,16,2048]{3,2,1,0:T(8,128)(2,1)} custom-call(s32[4]{0:T(128)} %pad_add_fusion.order_ref, bf16[3,4,16,2048]{3,2,1,0:T(8,128)(2,1)} %bitcast.71, bf16[3,4,16,2048]{3,2,1,0:T(8,128)(2,1)} %bitcast.73), custom_call_target="tpu_custom_call" | custom-call | tf_op jit(solution)/shard_map/gate/pallas_call | solution.py:367
  24.3 3.9 %reshape_squeeze.22.refs_2_.refs_3_ = bf16[3,16,16384]{2,1,0:T(8,128)(2,1)} reshape(bf16[1,3,16,2,8192]{4,3,2,1,0:T(2,128)(2,1)} %param.12) | data formatting | bytes 3145728 | tf_op jit(solution)/shard_map/reshape;squeeze | solution.py:328
  28.9 12.0 %collective-permute-done.refs_8_.refs_9_ = bf16[3,16,8192]{2,1,0:T(8,128)(2,1)S(1)} collective-permute-done((bf16[3,16,8192]{2,1,0:T(8,128)(2,1)}, bf16[3,16,8192]{2,1,0:T(8,128)(2,1)S(1)}, u32[]{:S(2)}, u32[]{:S(2)}) %collective-permute-start) | collective-permute-done | bytes 786464 | tf_op jit(solution)/shard_map/ppermute | solution.py:18
  40.9 21.4 %collective-permute-done.1.refs_9_.refs_10_ = bf16[3,16,8192]{2,1,0:T(8,128)(2,1)S(1)} collective-permute-done((bf16[3,16,8192]{2,1,0:T(8,128)(2,1)}, bf16[3,16,8192]{2,1,0:T(8,128)(2,1)S(1)}, u32[]{:S(2)}, u32[]{:S(2)}) %collective-permute-start.1) | collective-permute-done | bytes 786464 | tf_op jit(solution)/shard_map/ppermute | solution.py:18
  62.3 0.9 copy-done.9
  63.4 5.1 %step.2 = (bf16[2,16,8192]{2,1,0:T(8,128)(2,1)}, f32[16,8192]{1,0:T(8,128)}) custom-call(s32[5]{0:T(128)} %concatenate.16.flag_ref, bf16[3,16,8192]{2,1,0:T(8,128)(2,1)} %bitcast.64, bf16[3,16,8192]{2,1,0:T(8,128)(2,1)} %bitcast.62, bf16[3,16,16384]{2,1,0:T(8,128)(2,1)} %reshape_squeeze.22.refs_2_.refs_3_, s32[3,16,2]{2,1,0:T(8,128)} %copy.34.refs_3_.refs_4_, ...), custom_call_target="tpu_custom_call" | custom-call | tf_op jit(solution)/shard_map/step/pallas_call | solution.py:349
  68.5 1.6 collective-permute-start.10
  70.1 1.3 collective-permute-start.3
  71.4 1.0 slice.46.refs_0_
  72.4 15.8 %collective-permute-start.4 = (bf16[1,16,8192]{2,1,0:T(8,128)(2,1)S(1)}, bf16[1,16,8192]{2,1,0:T(8,128)(2,1)S(1)}, u32[]{:S(2)}, u32[]{:S(2)}) collective-permute-start(bf16[1,16,8192]{2,1,0:T(8,128)(2,1)S(1)} %slice.46.refs_0_), channel_id=1, source_target_pairs={{0,1},{1,0},{2,3},{3,2},{4,5},{5,4},{6,7},{7,6},{8,9},{9,8},{10,11... | collective-permute-start | bytes 786440 | tf_op jit(solution)/shard_map/ppermute | solution.py:18
  88.2 1.1 collective-permute-start.5
  89.3 1.4 collective-permute-start.6
  90.7 0.8 copy-done.12
  91.5 5.6 %step.3 = (bf16[2,16,8192]{2,1,0:T(8,128)(2,1)}, f32[16,8192]{1,0:T(8,128)}) custom-call(s32[5]{0:T(128)} %concatenate.16.flag_ref, bf16[3,16,8192]{2,1,0:T(8,128)(2,1)} %bitcast.65, bf16[2,16,8192]{2,1,0:T(8,128)(2,1)} %copy-done.12, bf16[3,16,8192]{2,1,0:T(8,128)(2,1)} %bitcast.63, bf16[3,16,16384]{2,1,0:T(8,128)(2,1)} %reshape_squeeze.22.refs_2_.refs_3_, ...), custom_call_target="tpu_custom_call" | custom-call | tf_op jit(solution)/shard_map/step/pallas_call | solution.py:349
  97.1 12.4 %collective-permute-done.5.refs_2_ = bf16[1,16,8192]{2,1,0:T(8,128)(2,1)S(1)} collective-permute-done((bf16[1,16,8192]{2,1,0:T(8,128)(2,1)S(1)}, bf16[1,16,8192]{2,1,0:T(8,128)(2,1)S(1)}, u32[]{:S(2)}, u32[]{:S(2)}) %collective-permute-start.5) | collective-permute-done | bytes 262176 | tf_op jit(solution)/shard_map/ppermute | solution.py:18
  109.5 3.4 %collective-permute-start.7 = (bf16[2,16,8192]{2,1,0:T(8,128)(2,1)}, bf16[2,16,8192]{2,1,0:T(8,128)(2,1)S(1)}, u32[]{:S(2)}, u32[]{:S(2)}) collective-permute-start(bf16[2,16,8192]{2,1,0:T(8,128)(2,1)} %get-tuple-element.57.refs_4_.refs_0_), channel_id=1, source_target_pairs={{0,1},{1,0},{2,3},{3,2},{4,5},{5,4},{6,7},{7,6},{8,9},{9,8},{10,11... | collective-permute-start | bytes 1572872 | tf_op jit(solution)/shard_map/ppermute | solution.py:18
  112.9 1.0 collective-permute-start.8
  114.7 18.7 %collective-permute-done.7.refs_5_.refs_1_ = bf16[2,16,8192]{2,1,0:T(8,128)(2,1)S(1)} collective-permute-done((bf16[2,16,8192]{2,1,0:T(8,128)(2,1)}, bf16[2,16,8192]{2,1,0:T(8,128)(2,1)S(1)}, u32[]{:S(2)}, u32[]{:S(2)}) %collective-permute-start.7) | collective-permute-done | bytes 524320 | tf_op jit(solution)/shard_map/ppermute | solution.py:18
  133.4 5.6 %collective-permute-start.17 = (bf16[1,16,8192]{2,1,0:T(8,128)(2,1)}, bf16[1,16,8192]{2,1,0:T(8,128)(2,1)}, u32[]{:S(2)}, u32[]{:S(2)}) collective-permute-start(bf16[1,16,8192]{2,1,0:T(8,128)(2,1)} %slice_bitcast_fusion.refs_0_), channel_id=1, source_target_pairs={{0,1},{1,0},{2,3},{3,2},{4,5},{5,4},{6,7},{7,6},{8,9},{9,8},{10,11... | collective-permute-start | bytes 786440 | tf_op jit(solution)/shard_map/ppermute | solution.py:18
  139.0 2.5 %collective-permute-start.18 = (bf16[1,16,8192]{2,1,0:T(8,128)(2,1)}, bf16[1,16,8192]{2,1,0:T(8,128)(2,1)}, u32[]{:S(2)}, u32[]{:S(2)}) collective-permute-start(bf16[1,16,8192]{2,1,0:T(8,128)(2,1)} %slice_bitcast_fusion.refs_0_), channel_id=1, source_target_pairs={{0,2},{1,3},{2,0},{3,1},{4,6},{5,7},{6,4},{7,5},{8,10},{9,11},{10,... | collective-permute-start | bytes 786440 | tf_op jit(solution)/shard_map/ppermute | solution.py:18
  141.5 3.4 %columns.2 = bf16[4,64,2048]{2,1,0:T(8,128)(2,1)} custom-call(bf16[1,16,8192]{2,1,0:T(8,128)(2,1)} %copy-done.4, bf16[1,16,8192]{2,1,0:T(8,128)(2,1)} %copy-done.14, bf16[1,16,8192]{2,1,0:T(8,128)(2,1)} %copy-done.15, bf16[1,16,8192]{2,1,0:T(8,128)(2,1)} %copy-done.16), custom_call_target="tpu_custom_call" | custom-call | tf_op jit(solution)/shard_map/columns/pallas_call | solution.py:379
  144.9 3.5 %all-to-all-start = ((bf16[4,64,2048]{2,1,0:T(8,128)(2,1)}), bf16[4,64,2048]{2,1,0:T(8,128)(2,1)S(1)}, u32[]{:S(2)}, u32[]{:S(2)}) async-start(bf16[4,64,2048]{2,1,0:T(8,128)(2,1)} %columns.2), calls=%async_computation | async-start | bytes 2097152 | tf_op jit(solution)/shard_map/all_to_all | solution.py:388
  148.4 1.0 collective-permute-done.18.refs_2_
  150.0 1.3 collective-permute-start.20
  152.1 1.3 collective-permute-start.13
  153.4 1.9 bitcast_select_fusion.refs_4_
  155.3 6.0 %collective-permute-done.20 = bf16[1,16,8192]{2,1,0:T(8,128)(2,1)} collective-permute-done((bf16[1,16,8192]{2,1,0:T(8,128)(2,1)}, bf16[1,16,8192]{2,1,0:T(8,128)(2,1)}, u32[]{:S(2)}, u32[]{:S(2)}) %collective-permute-start.20) | collective-permute-done | bytes 262176 | tf_op jit(solution)/shard_map/ppermute | solution.py:44
  161.3 1.6 all-to-all-done.refs_4_
  162.8 8.4 %collective-permute-done.13 = bf16[2,16,8192]{2,1,0:T(8,128)(2,1)} collective-permute-done((bf16[2,16,8192]{2,1,0:T(8,128)(2,1)}, bf16[2,16,8192]{2,1,0:T(8,128)(2,1)}, u32[]{:S(2)}, u32[]{:S(2)}) %collective-permute-start.13) | collective-permute-done | bytes 524320 | tf_op jit(solution)/shard_map/ppermute | solution.py:44
  171.2 1.9 broadcast_select_fusion.1.refs_7_.refs_3_
  173.1 4.1 %columns.3 = bf16[4,144,2048]{2,1,0:T(8,128)(2,1)} custom-call(bf16[2,16,8192]{2,1,0:T(8,128)(2,1)} %get-tuple-element.57.refs_4_.refs_0_, bf16[2,16,8192]{2,1,0:T(8,128)(2,1)} %copy-done.11, bf16[2,16,8192]{2,1,0:T(8,128)(2,1)} %collective-permute-done.8.refs_6_.refs_2_, bf16[2,16,8192]{2,1,0:T(8,128)(2,1)} %broadcast_select_fusion.1.refs_7_.refs_3_, ...), custom_call_target="tpu_custom_call" | custom-call | tf_op jit(solution)/shard_map/columns/pallas_call | solution.py:379
  177.2 3.6 %all-to-all-start.1 = ((bf16[4,144,2048]{2,1,0:T(8,128)(2,1)}), bf16[4,144,2048]{2,1,0:T(8,128)(2,1)S(1)}, u32[]{:S(2)}, u32[]{:S(2)}) async-start(bf16[4,144,2048]{2,1,0:T(8,128)(2,1)} %columns.3), calls=%async_computation.1 | async-start | bytes 4718592 | tf_op jit(solution)/shard_map/all_to_all | solution.py:388
  180.8 1.7 broadcast_select_fusion.2.refs_3_
  182.5 2.1 collective-permute-start.22
  185.3 21.2 %project.1 = (bf16[3,64,2048]{2,1,0:T(8,128)(2,1)}, bf16[3,64,2048]{2,1,0:T(8,128)(2,1)}) custom-call(s32[4]{0:T(128)} %pad_add_fusion.order_ref, bf16[1,16,8192]{2,1,0:T(8,128)(2,1)} %copy-done.4, bf16[1,16,8192]{2,1,0:T(8,128)(2,1)} %copy-done.14, bf16[1,16,8192]{2,1,0:T(8,128)(2,1)} %copy-done.15, bf16[1,16,8192]{2,1,0:T(8,128)(2,1)} %copy-done.16, ...), custom_call_target="tpu_custom_call" | custom-call | tf_op jit(solution)/shard_map/project/pallas_call | solution.py:419
  207.2 2.1 collective-permute-done.22.refs_6_
  210.0 1.3 collective-permute-start.24
  211.3 0.9 maximum_bitcast_fusion
  212.4 3.5 %collective-permute-start.14 = (f32[6,2048]{1,0:T(8,128)S(1)}, f32[6,2048]{1,0:T(8,128)S(1)}, u32[]{:S(2)}, u32[]{:S(2)}) collective-permute-start(f32[6,2048]{1,0:T(8,128)S(1)} %pad_maximum_fusion), channel_id=1, source_target_pairs={{0,1},{1,0},{2,3},{3,2},{4,5},{5,4},{6,7},{7,6},{8,9},{9,8},{10,11... | collective-permute-start | bytes 147464 | tf_op jit(solution)/shard_map/ppermute | solution.py:18
  216.0 2.3 collective-permute-start.16
  218.3 12.9 %weight_grad.1 = f32[2048,2048]{1,0:T(8,128)} custom-call(s32[4]{0:T(128)} %iota_xor_fusion.order_ref, bf16[192,2048]{1,0:T(8,128)(2,1)} %bitcast.66, bf16[192,2048]{1,0:T(8,128)(2,1)} %collective-permute-done.9.refs_1_, bf16[192,2048]{1,0:T(8,128)(2,1)} %collective-permute-done.10.refs_2_, bf16[192,2048]{1,0:T(8,128)(2,1)} %collective-permute-done.11.refs_3_, ...), custom_call_target="tpu_custom_call" | custom-call | tf_op jit(solution)/shard_map/weight_grad/pallas_call | solution.py:438
  231.2 1.9 broadcast_select_fusion.refs_7_
  235.1 6.2 %dispatch.1 = bf16[3,64,8192]{2,1,0:T(8,128)(2,1)} custom-call(s32[4]{0:T(128)} %pad_add_fusion.order_ref, f32[3,4,16]{2,1,0:T(4,128)} %bitcast.80, bf16[1,16,8192]{2,1,0:T(8,128)(2,1)} %slice_bitcast_fusion.refs_0_, bf16[1,16,8192]{2,1,0:T(8,128)(2,1)} %collective-permute-done.17.refs_1_, bf16[1,16,8192]{2,1,0:T(8,128)(2,1)} %collective-permute-done.18.refs_2_, ...), custom_call_target="tpu_custom_call" | custom-call | tf_op jit(solution)/shard_map/dispatch/pallas_call | solution.py:462
  (93 shorter events, 10.2 us)
Async XLA Ops:
  0.7 9.0 %copy-start.20 = (s32[1,3,16,2]{2,3,1,0:T(2,128)S(1)}, s32[1,3,16,2]{2,3,1,0:T(2,128)}, u32[]{:S(2)}) copy-start(s32[1,3,16,2]{2,3,1,0:T(2,128)} %param.13) | copy-start | bytes 1156
  0.7 9.7 %copy-start.19 = (bf16[1,2048,4]{1,2,0:T(4,128)(2,1)S(1)}, bf16[1,2048,4]{1,2,0:T(4,128)(2,1)}, u32[]{:S(2)}) copy-start(bf16[1,2048,4]{1,2,0:T(4,128)(2,1)} %param.18) | copy-start | bytes 49156
  0.7 9.6 %copy-start.21 = (bf16[1,2048]{1,0:T(2,128)(2,1)S(1)}, bf16[1,2048]{1,0:T(2,128)(2,1)}, u32[]{:S(2)}) copy-start(bf16[1,2048]{1,0:T(2,128)(2,1)} %param.19) | copy-start | bytes 12292
  4.0 36.9 %collective-permute-start = (bf16[3,16,8192]{2,1,0:T(8,128)(2,1)}, bf16[3,16,8192]{2,1,0:T(8,128)(2,1)S(1)}, u32[]{:S(2)}, u32[]{:S(2)}) collective-permute-start(bf16[3,16,8192]{2,1,0:T(8,128)(2,1)} %get-tuple-element.75), channel_id=1, source_target_pairs={{0,1},{1,0},{2,3},{3,2},{4,5},{5,4},{6,7},{7,6},{8,9},{9,8},{10,11... | collective-permute-start | bytes 2359304 | tf_op jit(solution)/shard_map/ppermute | solution.py:18
  7.0 55.3 %collective-permute-start.1 = (bf16[3,16,8192]{2,1,0:T(8,128)(2,1)}, bf16[3,16,8192]{2,1,0:T(8,128)(2,1)S(1)}, u32[]{:S(2)}, u32[]{:S(2)}) collective-permute-start(bf16[3,16,8192]{2,1,0:T(8,128)(2,1)} %get-tuple-element.74), channel_id=1, source_target_pairs={{0,2},{1,3},{2,0},{3,1},{4,6},{5,7},{6,4},{7,5},{8,10},{9,11},{10,... | collective-permute-start | bytes 2359304 | tf_op jit(solution)/shard_map/ppermute | solution.py:18
  9.6 52.7 %collective-permute-start.2 = (bf16[3,16,8192]{2,1,0:T(8,128)(2,1)S(1)}, bf16[3,16,8192]{2,1,0:T(8,128)(2,1)S(1)}, u32[]{:S(2)}, u32[]{:S(2)}) collective-permute-start(bf16[3,16,8192]{2,1,0:T(8,128)(2,1)S(1)} %get-tuple-element.73), channel_id=1, source_target_pairs={{0,3},{1,2},{2,1},{3,0},{4,7},{5,6},{6,5},{7,4},{8,11},{9,10},{10,... | collective-permute-start | bytes 2359304 | tf_op jit(solution)/shard_map/ppermute | solution.py:18
  40.9 21.5 %copy-start.8 = (bf16[3,16,8192]{2,1,0:T(8,128)(2,1)}, bf16[3,16,8192]{2,1,0:T(8,128)(2,1)S(1)}, u32[]{:S(2)}) copy-start(bf16[3,16,8192]{2,1,0:T(8,128)(2,1)S(1)} %collective-permute-done.refs_8_.refs_9_) | copy-start | bytes 2359300
  62.3 0.9 copy-start.9
  62.3 1.1 copy-start.10
  63.4 5.1 %copy-start.7 = (bf16[3,4,16,2048]{3,2,1,0:T(8,128)(2,1)S(1)}, bf16[3,4,16,2048]{3,2,1,0:T(8,128)(2,1)}, u32[]{:S(2)}) copy-start(bf16[3,4,16,2048]{3,2,1,0:T(8,128)(2,1)} %gate.1) | copy-start | bytes 2359300
  68.5 45.4 %collective-permute-start.10 = (bf16[192,2048]{1,0:T(8,128)(2,1)S(1)}, bf16[192,2048]{1,0:T(8,128)(2,1)}, u32[]{:S(2)}, u32[]{:S(2)}) collective-permute-start(bf16[192,2048]{1,0:T(8,128)(2,1)S(1)} %bitcast.67), channel_id=1, source_target_pairs={{0,8},{4,12},{8,0},{12,4},{1,9},{5,13},{9,1},{13,5},{2,10},{6,14},... | collective-permute-start | bytes 2359304 | tf_op jit(solution)/shard_map/ppermute | solution.py:18
  70.1 20.6 %collective-permute-start.3 = (bf16[2,16,8192]{2,1,0:T(8,128)(2,1)}, bf16[2,16,8192]{2,1,0:T(8,128)(2,1)S(1)}, u32[]{:S(2)}, u32[]{:S(2)}) collective-permute-start(bf16[2,16,8192]{2,1,0:T(8,128)(2,1)} %get-tuple-element.44), channel_id=1, source_target_pairs={{16,0},{17,1},{18,2},{19,3},{20,4},{21,5},{22,6},{23,7},{24,8},{25... | collective-permute-start | bytes 1572872 | tf_op jit(solution)/shard_map/ppermute | solution.py:391
  72.4 24.7 %copy-start.4 = (bf16[1,16,8192]{2,1,0:T(8,128)(2,1)}, bf16[1,16,8192]{2,1,0:T(8,128)(2,1)S(1)}, u32[]{:S(2)}) copy-start(bf16[1,16,8192]{2,1,0:T(8,128)(2,1)S(1)} %slice.46.refs_0_) | copy-start | bytes 786436
  72.4 41.5 %copy-start.1 = (bf16[1,3,16,8192]{3,2,1,0:T(8,128)(2,1)S(1)}, bf16[1,3,16,8192]{3,2,1,0:T(8,128)(2,1)}, u32[]{:S(2)}) copy-start(bf16[1,3,16,8192]{3,2,1,0:T(8,128)(2,1)} %param.10) | copy-start | bytes 2359300
  72.4 24.7 %collective-permute-start.4 = (bf16[1,16,8192]{2,1,0:T(8,128)(2,1)S(1)}, bf16[1,16,8192]{2,1,0:T(8,128)(2,1)S(1)}, u32[]{:S(2)}, u32[]{:S(2)}) collective-permute-start(bf16[1,16,8192]{2,1,0:T(8,128)(2,1)S(1)} %slice.46.refs_0_), channel_id=1, source_target_pairs={{0,1},{1,0},{2,3},{3,2},{4,5},{5,4},{6,7},{7,6},{8,9},{9,8},{10,11... | collective-permute-start | bytes 786440 | tf_op jit(solution)/shard_map/ppermute | solution.py:18
  88.2 21.3 %collective-permute-start.5 = (bf16[1,16,8192]{2,1,0:T(8,128)(2,1)S(1)}, bf16[1,16,8192]{2,1,0:T(8,128)(2,1)S(1)}, u32[]{:S(2)}, u32[]{:S(2)}) collective-permute-start(bf16[1,16,8192]{2,1,0:T(8,128)(2,1)S(1)} %slice.46.refs_0_), channel_id=1, source_target_pairs={{0,2},{1,3},{2,0},{3,1},{4,6},{5,7},{6,4},{7,5},{8,10},{9,11},{10,... | collective-permute-start | bytes 786440 | tf_op jit(solution)/shard_map/ppermute | solution.py:18
  89.3 20.2 %collective-permute-start.6 = (bf16[1,16,8192]{2,1,0:T(8,128)(2,1)S(1)}, bf16[1,16,8192]{2,1,0:T(8,128)(2,1)S(1)}, u32[]{:S(2)}, u32[]{:S(2)}) collective-permute-start(bf16[1,16,8192]{2,1,0:T(8,128)(2,1)S(1)} %slice.46.refs_0_), channel_id=1, source_target_pairs={{0,3},{1,2},{2,1},{3,0},{4,7},{5,6},{6,5},{7,4},{8,11},{9,10},{10,... | collective-permute-start | bytes 786440 | tf_op jit(solution)/shard_map/ppermute | solution.py:18
  90.7 60.7 %collective-permute-start.9 = (bf16[192,2048]{1,0:T(8,128)(2,1)S(1)}, bf16[192,2048]{1,0:T(8,128)(2,1)}, u32[]{:S(2)}, u32[]{:S(2)}) collective-permute-start(bf16[192,2048]{1,0:T(8,128)(2,1)S(1)} %bitcast.68), channel_id=1, source_target_pairs={{0,4},{4,0},{8,12},{12,8},{1,5},{5,1},{9,13},{13,9},{2,6},{6,2},{1... | collective-permute-start | bytes 2359304 | tf_op jit(solution)/shard_map/ppermute | solution.py:18
  97.1 54.3 %copy-start.2 = (bf16[2,16,8192]{2,1,0:T(8,128)(2,1)S(1)}, bf16[2,16,8192]{2,1,0:T(8,128)(2,1)}, u32[]{:S(2)}) copy-start(bf16[2,16,8192]{2,1,0:T(8,128)(2,1)} %get-tuple-element.57.refs_4_.refs_0_) | copy-start | bytes 1572868
  97.1 44.4 %copy-start.14 = (bf16[1,16,8192]{2,1,0:T(8,128)(2,1)}, bf16[1,16,8192]{2,1,0:T(8,128)(2,1)S(1)}, u32[]{:S(2)}) copy-start(bf16[1,16,8192]{2,1,0:T(8,128)(2,1)S(1)} %collective-permute-done.4.refs_1_) | copy-start | bytes 786436
  109.5 32.0 %copy-start.15 = (bf16[1,16,8192]{2,1,0:T(8,128)(2,1)}, bf16[1,16,8192]{2,1,0:T(8,128)(2,1)S(1)}, u32[]{:S(2)}) copy-start(bf16[1,16,8192]{2,1,0:T(8,128)(2,1)S(1)} %collective-permute-done.5.refs_2_) | copy-start | bytes 786436
  109.5 32.0 %copy-start.16 = (bf16[1,16,8192]{2,1,0:T(8,128)(2,1)}, bf16[1,16,8192]{2,1,0:T(8,128)(2,1)S(1)}, u32[]{:S(2)}) copy-start(bf16[1,16,8192]{2,1,0:T(8,128)(2,1)S(1)} %collective-permute-done.6.refs_3_) | copy-start | bytes 786436
  109.5 23.9 %collective-permute-start.7 = (bf16[2,16,8192]{2,1,0:T(8,128)(2,1)}, bf16[2,16,8192]{2,1,0:T(8,128)(2,1)S(1)}, u32[]{:S(2)}, u32[]{:S(2)}) collective-permute-start(bf16[2,16,8192]{2,1,0:T(8,128)(2,1)} %get-tuple-element.57.refs_4_.refs_0_), channel_id=1, source_target_pairs={{0,1},{1,0},{2,3},{3,2},{4,5},{5,4},{6,7},{7,6},{8,9},{9,8},{10,11... | collective-permute-start | bytes 1572872 | tf_op jit(solution)/shard_map/ppermute | solution.py:18
  112.9 20.5 %collective-permute-start.8 = (bf16[2,16,8192]{2,1,0:T(8,128)(2,1)}, bf16[2,16,8192]{2,1,0:T(8,128)(2,1)}, u32[]{:S(2)}, u32[]{:S(2)}) collective-permute-start(bf16[2,16,8192]{2,1,0:T(8,128)(2,1)} %get-tuple-element.57.refs_4_.refs_0_), channel_id=1, source_target_pairs={{0,2},{1,3},{2,0},{3,1},{4,6},{5,7},{6,4},{7,5},{8,10},{9,11},{10,... | collective-permute-start | bytes 1572872 | tf_op jit(solution)/shard_map/ppermute | solution.py:18
  113.9 37.4 %collective-permute-start.11 = (bf16[192,2048]{1,0:T(8,128)(2,1)}, bf16[192,2048]{1,0:T(8,128)(2,1)}, u32[]{:S(2)}, u32[]{:S(2)}) collective-permute-start(bf16[192,2048]{1,0:T(8,128)(2,1)} %collective-permute-done.10.refs_2_), channel_id=1, source_target_pairs={{0,4},{4,0},{8,12},{12,8},{1,5},{5,1},{9,13},{13,9},{2,6},{6,2},{1... | collective-permute-start | bytes 2359304 | tf_op jit(solution)/shard_map/ppermute | solution.py:18
  133.4 11.4 %copy-start.11 = (bf16[2,16,8192]{2,1,0:T(8,128)(2,1)}, bf16[2,16,8192]{2,1,0:T(8,128)(2,1)S(1)}, u32[]{:S(2)}) copy-start(bf16[2,16,8192]{2,1,0:T(8,128)(2,1)S(1)} %collective-permute-done.7.refs_5_.refs_1_) | copy-start | bytes 1572868
  133.4 15.0 %collective-permute-start.17 = (bf16[1,16,8192]{2,1,0:T(8,128)(2,1)}, bf16[1,16,8192]{2,1,0:T(8,128)(2,1)}, u32[]{:S(2)}, u32[]{:S(2)}) collective-permute-start(bf16[1,16,8192]{2,1,0:T(8,128)(2,1)} %slice_bitcast_fusion.refs_0_), channel_id=1, source_target_pairs={{0,1},{1,0},{2,3},{3,2},{4,5},{5,4},{6,7},{7,6},{8,9},{9,8},{10,11... | collective-permute-start | bytes 786440 | tf_op jit(solution)/shard_map/ppermute | solution.py:18
  139.0 10.4 %collective-permute-start.18 = (bf16[1,16,8192]{2,1,0:T(8,128)(2,1)}, bf16[1,16,8192]{2,1,0:T(8,128)(2,1)}, u32[]{:S(2)}, u32[]{:S(2)}) collective-permute-start(bf16[1,16,8192]{2,1,0:T(8,128)(2,1)} %slice_bitcast_fusion.refs_0_), channel_id=1, source_target_pairs={{0,2},{1,3},{2,0},{3,1},{4,6},{5,7},{6,4},{7,5},{8,10},{9,11},{10,... | collective-permute-start | bytes 786440 | tf_op jit(solution)/shard_map/ppermute | solution.py:18
  144.9 18.0 %all-to-all-start = ((bf16[4,64,2048]{2,1,0:T(8,128)(2,1)}), bf16[4,64,2048]{2,1,0:T(8,128)(2,1)S(1)}, u32[]{:S(2)}, u32[]{:S(2)}) async-start(bf16[4,64,2048]{2,1,0:T(8,128)(2,1)} %columns.2), calls=%async_computation | async-start | bytes 2097152 | tf_op jit(solution)/shard_map/all_to_all | solution.py:388
  149.4 5.9 %collective-permute-start.19 = (bf16[1,16,8192]{2,1,0:T(8,128)(2,1)}, bf16[1,16,8192]{2,1,0:T(8,128)(2,1)S(1)}, u32[]{:S(2)}, u32[]{:S(2)}) collective-permute-start(bf16[1,16,8192]{2,1,0:T(8,128)(2,1)} %slice_bitcast_fusion.refs_0_), channel_id=1, source_target_pairs={{1,2},{2,1},{5,6},{6,5},{9,10},{10,9},{13,14},{14,13},{17,18},{18,... | collective-permute-start | bytes 786440 | tf_op jit(solution)/shard_map/ppermute | solution.py:43
  150.0 11.2 %collective-permute-start.20 = (bf16[1,16,8192]{2,1,0:T(8,128)(2,1)}, bf16[1,16,8192]{2,1,0:T(8,128)(2,1)}, u32[]{:S(2)}, u32[]{:S(2)}) collective-permute-start(bf16[1,16,8192]{2,1,0:T(8,128)(2,1)} %collective-permute-done.18.refs_2_), channel_id=1, source_target_pairs={{2,3},{1,0},{6,7},{5,4},{10,11},{9,8},{14,15},{13,12},{18,19},{17,... | collective-permute-start | bytes 786440 | tf_op jit(solution)/shard_map/ppermute | solution.py:44
  151.4 11.4 %collective-permute-start.12 = (bf16[2,16,8192]{2,1,0:T(8,128)(2,1)S(1)}, bf16[2,16,8192]{2,1,0:T(8,128)(2,1)S(1)}, u32[]{:S(2)}, u32[]{:S(2)}) collective-permute-start(bf16[2,16,8192]{2,1,0:T(8,128)(2,1)S(1)} %copy-done.2), channel_id=1, source_target_pairs={{1,2},{2,1},{5,6},{6,5},{9,10},{10,9},{13,14},{14,13},{17,18},{18,... | collective-permute-start | bytes 1572872 | tf_op jit(solution)/shard_map/ppermute | solution.py:43
  152.1 19.1 %collective-permute-start.13 = (bf16[2,16,8192]{2,1,0:T(8,128)(2,1)}, bf16[2,16,8192]{2,1,0:T(8,128)(2,1)}, u32[]{:S(2)}, u32[]{:S(2)}) collective-permute-start(bf16[2,16,8192]{2,1,0:T(8,128)(2,1)} %collective-permute-done.8.refs_6_.refs_2_), channel_id=1, source_target_pairs={{2,3},{1,0},{6,7},{5,4},{10,11},{9,8},{14,15},{13,12},{18,19},{17,... | collective-permute-start | bytes 1572872 | tf_op jit(solution)/shard_map/ppermute | solution.py:44
  162.8 14.4 %copy-start.6 = (bf16[4,64,2048]{2,1,0:T(8,128)(2,1)}, bf16[4,64,2048]{2,1,0:T(8,128)(2,1)S(1)}, u32[]{:S(2)}) copy-start(bf16[4,64,2048]{2,1,0:T(8,128)(2,1)S(1)} %all-to-all-done.refs_4_) | copy-start | bytes 3145732
  177.2 7.4 %copy-start.18 = (f32[48,16]{1,0:T(8,128)S(1)}, f32[48,16]{1,0:T(8,128)}, u32[]{:S(2)}) copy-start(f32[48,16]{1,0:T(8,128)} %get-tuple-element.55) | copy-start | bytes 9220
  177.2 35.1 %all-to-all-start.1 = ((bf16[4,144,2048]{2,1,0:T(8,128)(2,1)}), bf16[4,144,2048]{2,1,0:T(8,128)(2,1)S(1)}, u32[]{:S(2)}, u32[]{:S(2)}) async-start(bf16[4,144,2048]{2,1,0:T(8,128)(2,1)} %columns.3), calls=%async_computation.1 | async-start | bytes 4718592 | tf_op jit(solution)/shard_map/all_to_all | solution.py:388
  182.5 24.7 %collective-permute-start.21 = (bf16[2,16,8192]{2,1,0:T(8,128)(2,1)}, bf16[2,16,8192]{2,1,0:T(8,128)(2,1)S(1)}, u32[]{:S(2)}, u32[]{:S(2)}) collective-permute-start(bf16[2,16,8192]{2,1,0:T(8,128)(2,1)} %bitcast_select_fusion.refs_4_), channel_id=1, source_target_pairs={{0,1},{1,0},{2,3},{3,2},{4,5},{5,4},{6,7},{7,6},{8,9},{9,8},{10,11... | collective-permute-start | bytes 1572872 | tf_op jit(solution)/shard_map/ppermute | solution.py:18
  182.5 26.8 %collective-permute-start.22 = (bf16[2,16,8192]{2,1,0:T(8,128)(2,1)}, bf16[2,16,8192]{2,1,0:T(8,128)(2,1)}, u32[]{:S(2)}, u32[]{:S(2)}) collective-permute-start(bf16[2,16,8192]{2,1,0:T(8,128)(2,1)} %bitcast_select_fusion.refs_4_), channel_id=1, source_target_pairs={{0,2},{1,3},{2,0},{3,1},{4,6},{5,7},{6,4},{7,5},{8,10},{9,11},{10,... | collective-permute-start | bytes 1572872 | tf_op jit(solution)/shard_map/ppermute | solution.py:18
  185.3 24.0 %copy-start.13 = (bf16[2,16,8192]{2,1,0:T(8,128)(2,1)S(1)}, bf16[2,16,8192]{2,1,0:T(8,128)(2,1)}, u32[]{:S(2)}) copy-start(bf16[2,16,8192]{2,1,0:T(8,128)(2,1)} %bitcast_select_fusion.refs_4_) | copy-start | bytes 1572868
  185.3 26.0 %copy-start.3 = (bf16[2,16,8192]{2,1,0:T(8,128)(2,1)S(1)}, bf16[2,16,8192]{2,1,0:T(8,128)(2,1)}, u32[]{:S(2)}) copy-start(bf16[2,16,8192]{2,1,0:T(8,128)(2,1)} %get-tuple-element.57.refs_4_.refs_0_) | copy-start | bytes 1572868
  185.3 26.0 %copy-start.5 = (bf16[1,16,8192]{2,1,0:T(8,128)(2,1)S(1)}, bf16[1,16,8192]{2,1,0:T(8,128)(2,1)}, u32[]{:S(2)}) copy-start(bf16[1,16,8192]{2,1,0:T(8,128)(2,1)} %copy-done.4) | copy-start | bytes 786436
  207.2 2.1 copy-start.17
  209.3 21.9 %collective-permute-start.23 = (bf16[2,16,8192]{2,1,0:T(8,128)(2,1)S(1)}, bf16[2,16,8192]{2,1,0:T(8,128)(2,1)S(1)}, u32[]{:S(2)}, u32[]{:S(2)}) collective-permute-start(bf16[2,16,8192]{2,1,0:T(8,128)(2,1)S(1)} %copy-done.13), channel_id=1, source_target_pairs={{1,2},{2,1},{5,6},{6,5},{9,10},{10,9},{13,14},{14,13},{17,18},{18,... | collective-permute-start | bytes 1572872 | tf_op jit(solution)/shard_map/ppermute | solution.py:43
  210.0 21.2 %collective-permute-start.24 = (bf16[2,16,8192]{2,1,0:T(8,128)(2,1)}, bf16[2,16,8192]{2,1,0:T(8,128)(2,1)}, u32[]{:S(2)}, u32[]{:S(2)}) collective-permute-start(bf16[2,16,8192]{2,1,0:T(8,128)(2,1)} %collective-permute-done.22.refs_6_), channel_id=1, source_target_pairs={{2,3},{1,0},{6,7},{5,4},{10,11},{9,8},{14,15},{13,12},{18,19},{17,... | collective-permute-start | bytes 1572872 | tf_op jit(solution)/shard_map/ppermute | solution.py:44
  212.3 6.0 %copy-start = (bf16[4,144,2048]{2,1,0:T(8,128)(2,1)}, bf16[4,144,2048]{2,1,0:T(8,128)(2,1)S(1)}, u32[]{:S(2)}) copy-start(bf16[4,144,2048]{2,1,0:T(8,128)(2,1)S(1)} %all-to-all-done.1.refs_5_) | copy-start | bytes 7077892
  212.4 20.7 %collective-permute-start.14 = (f32[6,2048]{1,0:T(8,128)S(1)}, f32[6,2048]{1,0:T(8,128)S(1)}, u32[]{:S(2)}, u32[]{:S(2)}) collective-permute-start(f32[6,2048]{1,0:T(8,128)S(1)} %pad_maximum_fusion), channel_id=1, source_target_pairs={{0,1},{1,0},{2,3},{3,2},{4,5},{5,4},{6,7},{7,6},{8,9},{9,8},{10,11... | collective-permute-start | bytes 147464 | tf_op jit(solution)/shard_map/ppermute | solution.py:18
  215.8 17.3 %collective-permute-start.15 = (f32[6,2048]{1,0:T(8,128)S(1)}, f32[6,2048]{1,0:T(8,128)S(1)}, u32[]{:S(2)}, u32[]{:S(2)}) collective-permute-start(f32[6,2048]{1,0:T(8,128)S(1)} %pad_maximum_fusion), channel_id=1, source_target_pairs={{0,2},{1,3},{2,0},{3,1},{4,6},{5,7},{6,4},{7,5},{8,10},{9,11},{10,... | collective-permute-start | bytes 147464 | tf_op jit(solution)/shard_map/ppermute | solution.py:18
  216.0 17.1 %collective-permute-start.16 = (f32[6,2048]{1,0:T(8,128)S(1)}, f32[6,2048]{1,0:T(8,128)S(1)}, u32[]{:S(2)}, u32[]{:S(2)}) collective-permute-start(f32[6,2048]{1,0:T(8,128)S(1)} %pad_maximum_fusion), channel_id=1, source_target_pairs={{0,3},{1,2},{2,1},{3,0},{4,7},{5,6},{6,5},{7,4},{8,11},{9,10},{10,... | collective-permute-start | bytes 147464 | tf_op jit(solution)/shard_map/ppermute | solution.py:18
  (1 other events, 0.8 us)
